TPU v7x, 256 devices: a whole 4x4x8 slice. The times are simulated.
256 devices in a mesh: row: 8 (over y, core), col: 32 (over z, x).
Axes of the slice: x: 4, y: 4, z: 8, core: 2. Of those that a mesh axis runs over, the one named last changes fastest.
Arguments:
- act_values: bfloat16 [1024, 12288], P('row', 'col'), may hold values from -6 to 6
- act_scales: float32 [1024, 96], P('row', 'col'), may hold values from 0.25 to 4
- weight_values: bfloat16 [12288, 12288], P('row', 'col'), may hold values from -0.0546875 to 0.0546875
- weight_scales: float32 [96, 96], P('row', 'col'), may hold values from 0.5 to 2
- cotangent: bfloat16 [1024, 12288], P('row', 'col'), may hold values from -6 to 6
Outputs:
- output: bfloat16 [1024, 12288], P('row', 'col')
- activation_grad: bfloat16 [1024, 12288], P('row', 'col')
- weight_grad: float32 [12288, 12288], P('row', 'col')
All inputs are finite; a program needn't handle non-finite values.
Results may differ from a plain program's by a relative error of at most 0.0057.
Values may be sent and summed in bfloat16 or wider, within the bound.
No kernel may reach another device: no remote copies, remote signals or barrier semaphores. Data moves between devices by JAX's collectives and lax.ppermute only.
A program may use at most 128 MiB of HBM per device.

v0:
```python
import jax
import jax.numpy as jnp
from jax import lax
from jax.sharding import PartitionSpec as P


def dequantize_rows(values, scales):
    blocks = (
        values.astype(jnp.float32).reshape(values.shape[0], scales.shape[1], -1)
        * scales[:, :, None]
    )
    return blocks.reshape(values.shape).astype(jnp.bfloat16)


def dequantize_tile(values, scales):
    blocks = values.astype(jnp.float32).reshape(
        scales.shape[0], -1, scales.shape[1], values.shape[1] // scales.shape[1]
    )
    blocks = blocks * scales[:, None, :, None]
    return blocks.reshape(values.shape).astype(jnp.bfloat16)


def per_device(act_values, act_scales, weight_values, weight_scales, cotangent):
    activations = dequantize_rows(act_values, act_scales)
    weight = dequantize_tile(weight_values, weight_scales)
    act_wide = lax.all_gather(activations, "col", axis=1, tiled=True)
    act_deep = lax.all_to_all(act_wide, "row", split_axis=1, concat_axis=0, tiled=True)
    cot_tall = lax.all_gather(cotangent, "row", axis=0, tiled=True)
    weight_grad = lax.dot_general(
        act_deep, cot_tall, (((0,), (0,)), ((), ())), preferred_element_type=jnp.float32
    )
    weight_grad = weight_grad * float(cot_tall.shape[0]) ** (-0.5)
    output = jnp.dot(
        act_wide,
        lax.all_gather(weight, "row", axis=0, tiled=True),
        preferred_element_type=jnp.float32,
    ).astype(jnp.bfloat16)
    partials = lax.dot_general(
        cotangent,
        lax.all_gather(weight, "row", axis=0, tiled=True),
        (((1,), (1,)), ((), ())),
        preferred_element_type=jnp.float32,
    )
    activation_grad = lax.psum_scatter(partials, "col", scatter_dimension=1, tiled=True).astype(
        jnp.bfloat16
    )
    return (output, activation_grad, weight_grad)


def solution(mesh):
    in_specs = (P("row", "col"), P("row", "col"), P("row", "col"), P("row", "col"), P("row", "col"))
    out_specs = (P("row", "col"), P("row", "col"), P("row", "col"))
    return jax.shard_map(
        per_device, mesh=mesh, in_specs=in_specs, out_specs=out_specs, check_vma=False
    )
```

profile of v0, /device:TPU:2, one launch (start us, length us, event | category | flops | bytes accessed | tf_op | source)
XLA Modules:
  0.0 387.4 jit_solution(6814302109589810344)
XLA Ops:
  7.2 0.0 all-gather.5.cloned.1.call-start
  7.2 1.6 copy.12
  8.8 1.0 mul.31
  9.7 0.0 copy-start.2
  9.8 0.0 copy-start.3
  9.8 0.0 copy-start.1
  9.8 1.9 fusion
  11.7 0.0 all-gather.5.cloned.1.call-update
  11.7 0.0 all-gather.3.cloned.1.call-start
  11.7 0.0 copy-done.2
  11.8 0.1 copy.11
  11.9 0.0 copy-done.3
  11.9 0.7 fusion.1
  12.5 0.0 all-gather.3.cloned.1.call-update
  12.6 0.0 reduce-scatter.2.cloned.1.call-start
  12.6 58.8 %all-gather.5.cloned.1.call-done = bf16[12288,384]{0,1:T(8,128)(2,1)} async-done(((bf16[1536,384]{0,1:T(8,128)(2,1)}), bf16[12288,384]{0,1:T(8,128)(2,1)}) %all-gather.5.cloned.1.call-update) | async-done | bytes 9437200 | tf_op jit(solution)/shard_map/all_gather | solution.py:35
  71.5 0.0 copy-done.1
  71.5 9.0 %convolution_bitcast_fusion = f32[128,12288]{0,1:T(8,128)} fusion(bf16[12288,384]{0,1:T(8,128)(2,1)} %all-gather.5.cloned.1.call-done, bf16[128,384]{1,0:T(8,128)(2,1)S(1)} %copy-done.1), kind=kOutput, calls=%fused_computation | convolution fusion | flops 1207959552 | bytes 15826944 | tf_op jit(solution)/shard_map/dot_general | solution.py:38
  80.5 0.0 reduce-scatter.2.cloned.1.call-update
  80.5 73.1 %all-gather.3.cloned.1.call-done = bf16[128,12288]{0,1:T(8,128)(2,1)} async-done(((bf16[128,384]{0,1:T(8,128)(2,1)}), bf16[128,12288]{0,1:T(8,128)(2,1)}) %all-gather.3.cloned.1.call-update) | async-done | bytes 3145744 | tf_op jit(solution)/shard_map/all_gather | solution.py:26
  153.6 4.7 %copy.13 = bf16[128,8,1536]{2,0,1:T(8,128)(2,1)} copy(bf16[128,8,1536]{0,2,1:T(8,128)(2,1)} %bitcast.24) | data formatting | bytes 6291456 | tf_op jit(solution)/shard_map/all_to_all | solution.py:27
  158.3 4.3 %all-to-all-start = ((bf16[128,8,1536]{2,0,1:T(8,128)(2,1)}), bf16[128,8,1536]{2,0,1:T(8,128)(2,1)S(1)}, u32[]{:S(2)}, u32[]{:S(2)}) async-start(bf16[128,8,1536]{2,0,1:T(8,128)(2,1)} %copy.13), calls=%async_computation.1 | async-start | bytes 6291456 | tf_op jit(solution)/shard_map/all_to_all | solution.py:27
  162.5 47.7 %all_gather.12 = bf16[1024,384]{1,0:T(8,128)(2,1)} all-gather(bf16[128,384]{1,0:T(8,128)(2,1)S(1)} %copy-done.1), channel_id=1, replica_groups=mesh['row'=8,'col'=32] {'row'}, dimensions={0}, use_global_device_ids=true | all-gather | bytes 884736 | tf_op jit(solution)/shard_map/all_gather | solution.py:28
  210.3 0.0 all-to-all-done
  210.3 0.0 copy-start
  210.3 4.5 %convolution_multiply_fusion = f32[1536,384]{1,0:T(8,128)} fusion(bf16[1024,1536]{1,0:T(8,128)(2,1)S(1)} %bitcast.26, bf16[1024,384]{1,0:T(8,128)(2,1)} %all_gather.12), kind=kOutput, calls=%fused_computation.1 | convolution fusion | flops 1208549376 | bytes 6291456 | tf_op jit(solution)/shard_map/dot_general | solution.py:29
  214.8 0.0 copy-done
  214.8 7.4 %convolution_convert_fusion = bf16[128,384]{1,0:T(8,128)(2,1)} fusion(bf16[128,12288]{0,1:T(8,128)(2,1)S(1)} %copy-done, bf16[12288,384]{0,1:T(8,128)(2,1)} %all-gather.5.cloned.1.call-done), kind=kOutput, calls=%fused_computation.4 | convolution fusion | flops 1208008704 | bytes 12681216 | tf_op jit(solution)/shard_map/dot_general | solution.py:33
  222.2 156.9 %reduce-scatter.2.cloned.1.call-done = f32[128,384]{0,1:T(8,128)} async-done(((f32[128,12288]{0,1:T(8,128)}), f32[128,384]{0,1:T(8,128)}) %reduce-scatter.2.cloned.1.call-update) | async-done | bytes 196624 | tf_op jit(solution)/shard_map/reduce_scatter | solution.py:44
  379.2 0.9 convert_element_type.23
  380.1 0.8 copy.14
Async XLA Ops:
  7.2 64.3 %all-gather.5.cloned.1.call-start = ((), (), s32[]{:S(2)}) async-start(), calls=%async_computation.3 | async-start | bytes 10616832 | tf_op jit(solution)/shard_map/all_gather | solution.py:35
  9.7 2.0 copy-start.2
  9.8 2.1 copy-start.3
  9.8 61.7 %copy-start.1 = (bf16[128,384]{1,0:T(8,128)(2,1)S(1)}, bf16[128,384]{1,0:T(8,128)(2,1)}, u32[]{:S(2)}) copy-start(bf16[128,384]{1,0:T(8,128)(2,1)} %param.9) | copy-start | bytes 294916
  11.7 141.9 %all-gather.3.cloned.1.call-start = ((), (), s32[]{:S(2)}) async-start(), calls=%async_computation.2 | async-start | bytes 3244032 | tf_op jit(solution)/shard_map/all_gather | solution.py:26
  12.6 366.6 %reduce-scatter.2.cloned.1.call-start = ((), (), s32[]{:S(2)}) async-start(), calls=%async_computation.4 | async-start | bytes 6488064 | tf_op jit(solution)/shard_map/reduce_scatter | solution.py:44
  158.3 52.0 %all-to-all-start = ((bf16[128,8,1536]{2,0,1:T(8,128)(2,1)}), bf16[128,8,1536]{2,0,1:T(8,128)(2,1)S(1)}, u32[]{:S(2)}, u32[]{:S(2)}) async-start(bf16[128,8,1536]{2,0,1:T(8,128)(2,1)} %copy.13), calls=%async_computation.1 | async-start | bytes 6291456 | tf_op jit(solution)/shard_map/all_to_all | solution.py:27
  210.3 4.5 %copy-start = (bf16[128,12288]{0,1:T(8,128)(2,1)S(1)}, bf16[128,12288]{0,1:T(8,128)(2,1)}, u32[]{:S(2)}) copy-start(bf16[128,12288]{0,1:T(8,128)(2,1)} %all-gather.3.cloned.1.call-done) | copy-start | bytes 9437188
Sparse Core Ops, SparseCore 0:
  11.8 59.5 all-gather.4
  74.6 78.9 all-gather.2
  157.6 221.5 reduce-scatter.1
where the time goes:
time: 389 us; the launch traced here: 387 us
  waiting for transfers between devices  289 us (74%)
  blocking collectives  47.7 us (12%)
  matrix products  21 us (5%)
  between operations  13.8 us (4%)
  local copies, waits for them, and re-layouts  8.07 us (2%)
  starting transfers between devices  4.41 us (1%)
    reduce_scatter x1, waiting for transfers between devices, per_device(): lax.psum_scatter(partials, 'col', scatter_dimension=1, tiled=True)  157 us
    all_gather x1, waiting for transfers between devices, per_device(): act_wide = lax.all_gather(activations, 'col', axis=1, tiled=True)  73.1 us
    all_gather x1, waiting for transfers between devices, per_device(): lax.all_gather(weight, 'row', axis=0, tiled=True)  58.8 us
    all_gather x1, blocking collectives, per_device(): cot_tall = lax.all_gather(cotangent, 'row', axis=0, tiled=True)  47.7 us
    dot_general x1, matrix products, per_device(): lax.dot_general(cotangent, lax.all_gather(weight, 'row', axis=0, tiled=Tr...  9.02 us
  transfers between devices with their start and end apart: 4, of which 3 were waited for; matrix products, arithmetic and copies ran while one was open for 7% of the time, Pallas kernels for 0%

commit v1 on v0

v1 whole, which is shorter than its diff:
```python
import jax
import jax.numpy as jnp
from jax import lax
from jax.sharding import PartitionSpec as P

NY, NC, NZ, NX = 4, 2, 8, 4
NR = NY * NC
SKEW = (0, 4, 1, 5, 2, 6, 3, 7)
UNSKEW = tuple(SKEW.index(i) for i in range(NZ))
BF, F32 = jnp.bfloat16, jnp.float32


def dequantize_rows(values, scales):
    blocks = (
        values.astype(F32).reshape(values.shape[0], scales.shape[1], -1)
        * scales[:, :, None]
    )
    return blocks.reshape(values.shape).astype(BF)


def dequantize_tile(values, scales):
    blocks = values.astype(F32).reshape(
        scales.shape[0], -1, scales.shape[1], values.shape[1] // scales.shape[1]
    )
    blocks = blocks * scales[:, None, :, None]
    return blocks.reshape(values.shape).astype(BF)


def move(value, where):
    pairs = []
    for r in range(NR):
        for z in range(NZ):
            for x in range(NX):
                r2, z2, x2 = where(r, z, x)
                pairs.append(
                    (
                        (r * NZ + z) * NX + x,
                        ((r2 % NR) * NZ + z2 % NZ) * NX + x2 % NX,
                    )
                )
    return lax.ppermute(value, ("row", "col"), pairs)


def along_x(value, k):
    return move(value, lambda r, z, x: (r, z, x + k))


def along_z(value, k):
    return move(value, lambda r, z, x: (r, z + k, x))


def along_y(value, k):
    return move(value, lambda r, z, x: (r + NC * k, z, x))


def other_core(value):
    return move(value, lambda r, z, x: (r ^ 1, z, x))


def mm(a, b):
    return jnp.dot(a, b, preferred_element_type=F32)


def mm_t(a, b):
    return lax.dot_general(a, b, (((1,), (1,)), ((), ())), preferred_element_type=F32)


def per_device(act_values, act_scales, weight_values, weight_scales, cotangent):
    r = lax.axis_index("row")
    col = lax.axis_index("col")
    z, x = col // NX, col % NX
    t, n = cotangent.shape

    act = dequantize_rows(act_values, act_scales)
    here = move(act, lambda r, z, x: (z, z + SKEW[r], x))
    cots = [cotangent, along_y(cotangent, 1), along_y(cotangent, -1), along_y(cotangent, 2)]
    wide = jnp.zeros((t, NX, n), BF)
    parts = [here, along_x(here, 1), along_x(here, -1), along_x(here, 2)]
    for part, off in zip(parts, (0, 3, 1, 2)):
        wide = lax.dynamic_update_slice(wide, part[:, None, :], (0, (x + off) % NX, 0))
    block = wide.reshape(t, NX * n)

    near = jnp.stack(cots)
    cot_rows = jnp.concatenate([near, other_core(near)])
    steps = jnp.arange(NZ)
    rows = jnp.array(UNSKEW)[(z + steps - r) % NZ]
    apart = (rows // NC - r // NC) % NY
    slot = jnp.array((0, 2, 3, 1))[apart] + jnp.where(rows % NC == r % NC, 0, NY)
    cot = jnp.take(cot_rows, slot, axis=0).reshape(NZ * t, n)

    weight = dequantize_tile(weight_values, weight_scales)
    by_x = weight.reshape(NX, n, n)

    def rows_of(off):
        return lax.dynamic_index_in_dim(by_x, (x + off) % NX, keepdims=False)

    half = NZ * t // 2
    lo, hi = cot[:half], cot[half:]
    w_far, w_right, w_left = rows_of(2), rows_of(1), rows_of(3)
    far_lo = along_x(mm_t(lo, w_far).astype(BF), 1)
    far_hi = along_x(mm_t(hi, w_far).astype(BF), -1)
    right_hi = along_x(mm_t(hi, w_right).astype(BF), 1)
    left_lo = along_x(mm_t(lo, w_left).astype(BF), -1)
    right_lo = along_x((mm_t(lo, w_right) + far_lo.astype(F32)).astype(BF), 1)
    left_hi = along_x((mm_t(hi, w_left) + far_hi.astype(F32)).astype(BF), -1)
    w_here = rows_of(0)
    sum_lo = mm_t(lo, w_here) + right_lo.astype(F32) + left_lo.astype(F32)
    sum_hi = mm_t(hi, w_here) + right_hi.astype(F32) + left_hi.astype(F32)

    def grad(s):
        of, at = (sum_lo, s) if s < NZ // 2 else (sum_hi, s - NZ // 2)
        return of[at * t : (at + 1) * t]

    up = along_z(grad(4).astype(BF), 1)
    down = along_z(grad(5).astype(BF), -1)
    for s in (3, 2, 1):
        up = along_z((grad(s) + up.astype(F32)).astype(BF), 1)
        if s > 1:
            down = along_z((grad(9 - s) + down.astype(F32)).astype(BF), -1)
    total = grad(0) + up.astype(F32) + down.astype(F32)
    activation_grad = move(
        total.astype(BF), lambda r, z, x: (UNSKEW[(z - r) % NZ], r, x)
    )

    blocks = [None] * NZ
    blocks[0] = block
    for s in range(1, NZ // 2 + 1):
        blocks[s] = along_z(blocks[s - 1], -1)
        if s < NZ // 2:
            blocks[NZ - s] = along_z(blocks[(NZ - s + 1) % NZ], 1)
    output = 0
    for s in range(NZ):
        share = mm(blocks[s], weight).astype(BF)
        share = move(share, lambda r, z, x: (UNSKEW[(z + s - r) % NZ], z, x))
        output = output + share.astype(F32)
    output = output.astype(BF)

    weight_grad = lax.dot_general(
        jnp.concatenate(blocks),
        cot,
        (((0,), (0,)), ((), ())),
        preferred_element_type=F32,
    )
    weight_grad = weight_grad * float(NR * t) ** (-0.5)
    return output, activation_grad, weight_grad


def solution(mesh):
    spec = P("row", "col")
    return jax.shard_map(
        per_device,
        mesh=mesh,
        in_specs=(spec,) * 5,
        out_specs=(spec,) * 3,
        check_vma=False,
    )
```

time: 389 us -> 155 us (0.40)
  waiting for transfers between devices: 289 us -> 42.4 us
  starting transfers between devices: 4.41 us -> 69.5 us
  blocking collectives: 47.7 us -> 0 us
  between operations: 13.8 us -> 1.32 us
  local copies, waits for them, and re-layouts: 8.07 us -> 19.1 us
  matrix products: 21 us -> 13.2 us
    reduce_scatter x1 -> x0, waiting for transfers between devices: 157 us -> none  [per_device(): lax.psum_scatter(partials, 'col', scatter_dimension=1, tiled=True)]
    all_gather x2 -> x0, waiting for transfers between devices: 132 us -> none  [the longest x1 73.1 us: per_device(): act_wide = lax.all_gather(activations, 'col', axis=1, tiled=True)]
    ppermute x0 -> x37, starting transfers between devices: none -> 69.5 us  [move(): return lax.ppermute(value, ('row', 'col'), pairs)]
    all_gather x1 -> x0, blocking collectives: 47.7 us -> none  [per_device(): cot_tall = lax.all_gather(cotangent, 'row', axis=0, tiled=True)]
    ppermute x0 -> x37, waiting for transfers between devices: none -> 42.4 us  [move(): return lax.ppermute(value, ('row', 'col'), pairs)]
    unnamed x11 -> x24, local copies, waits for them, and re-layouts: 2.47 us -> 11.1 us
    dot_general x3 -> x17, matrix products: 21 us -> 13.2 us  [the longest x8 6.74 us: mm(): return jnp.dot(a, b, preferred_element_type=F32)]
    all_to_all x1 -> x0, local copies, waits for them, and re-layouts: 4.66 us -> none  [per_device(): lax.all_to_all(act_wide, 'row', split_axis=1, concat_axis=0, tiled=True)]
  transfers between devices with their start and end apart: 4 -> 37, of which waited for: 3 -> 11; matrix products, arithmetic and copies ran while one was open for 7% -> 24% of each run, Pallas kernels for 0% -> 0%
where the time goes in v1:
time: 155 us; the launch traced here: 152 us
  starting transfers between devices  69.5 us (45%)
  waiting for transfers between devices  42.4 us (27%)
  local copies, waits for them, and re-layouts  19.1 us (12%)
  matrix products  13.2 us (9%)
  other arithmetic  6.09 us (4%)
    ppermute x37, starting transfers between devices, move(): return lax.ppermute(value, ('row', 'col'), pairs)  69.5 us
    ppermute x37, waiting for transfers between devices, move(): return lax.ppermute(value, ('row', 'col'), pairs)  42.4 us
    unnamed x24, local copies, waits for them, and re-layouts  11.1 us
    dot_general x8, matrix products, mm(): return jnp.dot(a, b, preferred_element_type=F32)  6.74 us
    dot_general x8, matrix products, mm_t(): lax.dot_general(a, b, (((1,), (1,)), ((), ())), preferred_element_type=F32)  3.29 us
    dot_general x1, matrix products, per_device(): lax.dot_general(jnp.concatenate(blocks), cot, (((0,), (0,)), ((), ())), p...  3.21 us
  transfers between devices with their start and end apart: 37, of which 11 were waited for; matrix products, arithmetic and copies ran while one was open for 24% of the time, Pallas kernels for 0%

profile of v1, /device:TPU:2, one launch (start us, length us, event | category | flops | bytes accessed | tf_op | source)
XLA Modules:
  0.0 151.6 jit_solution(14558074015371614394)
XLA Ops:
  0.7 1.7 %collective-permute-start.19 = (bf16[128,384]{1,0:T(8,128)(2,1)}, bf16[128,384]{1,0:T(8,128)(2,1)}, u32[]{:S(2)}, u32[]{:S(2)}) collective-permute-start(bf16[128,384]{1,0:T(8,128)(2,1)} %param.11), channel_id=1, source_target_pairs={{0,64},{1,65},{2,66},{3,67},{4,68},{5,69},{6,70},{7,71},{8,72},{9,... | collective-permute-start | bytes 294920 | tf_op jit(solution)/shard_map/ppermute | solution.py:41
  2.3 1.7 %collective-permute-start.20 = (bf16[128,384]{1,0:T(8,128)(2,1)}, bf16[128,384]{1,0:T(8,128)(2,1)}, u32[]{:S(2)}, u32[]{:S(2)}) collective-permute-start(bf16[128,384]{1,0:T(8,128)(2,1)} %param.11), channel_id=1, source_target_pairs={{0,192},{1,193},{2,194},{3,195},{4,196},{5,197},{6,198},{7,199},{8... | collective-permute-start | bytes 294920 | tf_op jit(solution)/shard_map/ppermute | solution.py:41
  4.0 2.0 %collective-permute-start.21 = (bf16[128,384]{1,0:T(8,128)(2,1)}, bf16[128,384]{1,0:T(8,128)(2,1)}, u32[]{:S(2)}, u32[]{:S(2)}) collective-permute-start(bf16[128,384]{1,0:T(8,128)(2,1)} %param.11), channel_id=1, source_target_pairs={{0,128},{1,129},{2,130},{3,131},{4,132},{5,133},{6,134},{7,135},{8... | collective-permute-start | bytes 294920 | tf_op jit(solution)/shard_map/ppermute | solution.py:41
  7.0 1.4 fusion.32
  8.3 2.1 %collective-permute-start = (bf16[128,384]{0,1:T(8,128)(2,1)}, bf16[128,384]{0,1:T(8,128)(2,1)}, u32[]{:S(2)}, u32[]{:S(2)}) collective-permute-start(bf16[128,384]{0,1:T(8,128)(2,1)} %fusion.32), channel_id=1, source_target_pairs={{0,0},{1,1},{2,2},{3,3},{4,36},{5,37},{6,38},{7,39},{8,72},{9,73},... | collective-permute-start | bytes 294920 | tf_op jit(solution)/shard_map/ppermute | solution.py:41
  10.4 1.5 %constant_dynamic-update-slice_fusion.4 = bf16[8,128,384]{2,1,0:T(8,128)(2,1)} fusion(bf16[128,384]{1,0:T(8,128)(2,1)} %param.11), kind=kLoop, calls=%fused_computation.69 | loop fusion | bytes 196608
  12.0 1.3 gather_fusion
  15.0 1.2 fusion
  18.2 7.3 %collective-permute-start.22 = (bf16[4,128,384]{2,1,0:T(8,128)(2,1)S(1)}, bf16[4,128,384]{2,1,0:T(8,128)(2,1)S(1)}, u32[]{:S(2)}, u32[]{:S(2)}) collective-permute-start(bf16[4,128,384]{2,1,0:T(8,128)(2,1)S(1)} %pad_maximum_fusion), channel_id=1, source_target_pairs={{0,32},{1,33},{2,34},{3,35},{4,36},{5,37},{6,38},{7,39},{8,40},{9,... | collective-permute-start | bytes 1179656 | tf_op jit(solution)/shard_map/ppermute | solution.py:41
  25.5 1.5 collective-permute-start.1
  27.5 2.1 %collective-permute-start.3 = (bf16[128,384]{0,1:T(8,128)(2,1)}, bf16[128,384]{0,1:T(8,128)(2,1)S(1)}, u32[]{:S(2)}, u32[]{:S(2)}) collective-permute-start(bf16[128,384]{0,1:T(8,128)(2,1)} %collective-permute-done), channel_id=1, source_target_pairs={{0,2},{1,3},{2,0},{3,1},{4,6},{5,7},{6,4},{7,5},{8,10},{9,11},{10,... | collective-permute-start | bytes 294920 | tf_op jit(solution)/shard_map/ppermute | solution.py:41
  29.6 1.5 %constant_dynamic-update-slice_fusion.3 = bf16[8,128,384]{2,1,0:T(8,128)(2,1)} fusion(bf16[8,128,384]{2,1,0:T(8,128)(2,1)} %constant_dynamic-update-slice_fusion.4, bf16[128,384]{1,0:T(8,128)(2,1)} %collective-permute-done.19), kind=kLoop, calls=%fused_computation.68 | loop fusion | bytes 196608
  31.2 1.5 %constant_dynamic-update-slice_fusion.2 = bf16[8,128,384]{2,1,0:T(8,128)(2,1)} fusion(bf16[8,128,384]{2,1,0:T(8,128)(2,1)} %constant_dynamic-update-slice_fusion.3, bf16[128,384]{1,0:T(8,128)(2,1)} %collective-permute-done.20), kind=kLoop, calls=%fused_computation.67 | loop fusion | bytes 196608
  32.7 1.5 %constant_dynamic-update-slice_fusion.1 = bf16[8,128,384]{2,1,0:T(8,128)(2,1)} fusion(bf16[8,128,384]{2,1,0:T(8,128)(2,1)} %constant_dynamic-update-slice_fusion.2, bf16[128,384]{1,0:T(8,128)(2,1)} %collective-permute-done.21), kind=kLoop, calls=%fused_computation.66 | loop fusion | bytes 196608
  35.4 3.2 %collective-permute-start.5 = (bf16[128,1536]{0,1:T(8,128)(2,1)S(1)}, bf16[128,1536]{0,1:T(8,128)(2,1)}, u32[]{:S(2)}, u32[]{:S(2)}) collective-permute-start(bf16[128,1536]{0,1:T(8,128)(2,1)S(1)} %bitcast.131), channel_id=1, source_target_pairs={{0,28},{1,29},{2,30},{3,31},{4,0},{5,1},{6,2},{7,3},{8,4},{9,5},{1... | collective-permute-start | bytes 1179656 | tf_op jit(solution)/shard_map/ppermute | solution.py:41
  38.6 1.1 convolution_convert_fusion.11
  39.8 2.1 %collective-permute-start.4 = (bf16[128,384]{1,0:T(8,128)(2,1)}, bf16[128,384]{1,0:T(8,128)(2,1)}, u32[]{:S(2)}, u32[]{:S(2)}) collective-permute-start(bf16[128,384]{1,0:T(8,128)(2,1)} %convolution_convert_fusion.11), channel_id=1, source_target_pairs={{0,0},{1,1},{2,2},{3,3},{4,68},{5,69},{6,70},{7,71},{8,136},{9,137... | collective-permute-start | bytes 294920 | tf_op jit(solution)/shard_map/ppermute | solution.py:41
  43.5 1.8 %gather_fusion.2 = bf16[8,128,384]{2,1,0:T(8,128)(2,1)S(1)} fusion(bf16[8,128,384]{2,1,0:T(8,128)(2,1)} %constant_dynamic-update-slice_fusion, s32[1024]{0:T(1024)S(1)} %pad_clamp_fusion), kind=kCustom, calls=%fused_computation.2 | custom fusion | bytes 1572896 | tf_op jit(solution)/shard_map/jit(_take)/gather | solution.py:89
  46.9 1.5 collective-permute-start.25
  50.5 1.5 collective-permute-start.27
  52.0 1.6 %convolution_convert_fusion.4 = bf16[128,384]{1,0:T(8,128)(2,1)S(1)} fusion(bf16[128,1536]{0,1:T(8,128)(2,1)} %collective-permute-done.13, bf16[1536,384]{0,1:T(8,128)(2,1)S(1)} %fusion), kind=kOutput, calls=%fused_computation.10 | convolution fusion | flops 151044096 | bytes 1671168 | tf_op jit(solution)/shard_map/dot_general | solution.py:61
  54.4 1.5 convolution_convert_fusion.10
  57.0 3.5 %collective-permute-done.23 = bf16[512,384]{1,0:T(8,128)(2,1)S(1)} collective-permute-done((bf16[512,384]{1,0:T(8,128)(2,1)S(1)}, bf16[512,384]{1,0:T(8,128)(2,1)S(1)}, u32[]{:S(2)}, u32[]{:S(2)}) %collective-permute-start.23) | collective-permute-done | bytes 393248 | tf_op jit(solution)/shard_map/ppermute | solution.py:41
  60.9 5.1 %collective-permute-done.27 = bf16[512,384]{1,0:T(8,128)(2,1)S(1)} collective-permute-done((bf16[512,384]{1,0:T(8,128)(2,1)S(1)}, bf16[512,384]{1,0:T(8,128)(2,1)S(1)}, u32[]{:S(2)}, u32[]{:S(2)}) %collective-permute-start.27) | collective-permute-done | bytes 393248 | tf_op jit(solution)/shard_map/ppermute | solution.py:41
  66.4 2.1 %collective-permute-done.7 = bf16[128,1536]{0,1:T(8,128)(2,1)S(1)} collective-permute-done((bf16[128,1536]{0,1:T(8,128)(2,1)}, bf16[128,1536]{0,1:T(8,128)(2,1)S(1)}, u32[]{:S(2)}, u32[]{:S(2)}) %collective-permute-start.7) | collective-permute-done | bytes 393248 | tf_op jit(solution)/shard_map/ppermute | solution.py:41
  68.5 2.4 %collective-permute-start.28 = (bf16[512,384]{1,0:T(8,128)(2,1)S(1)}, bf16[512,384]{1,0:T(8,128)(2,1)S(1)}, u32[]{:S(2)}, u32[]{:S(2)}) collective-permute-start(bf16[512,384]{1,0:T(8,128)(2,1)S(1)} %add_convert_fusion), channel_id=1, source_target_pairs={{0,3},{1,0},{2,1},{3,2},{4,7},{5,4},{6,5},{7,6},{8,11},{9,8},{10,9... | collective-permute-start | bytes 1179656 | tf_op jit(solution)/shard_map/ppermute | solution.py:41
  71.5 5.5 %collective-permute-done.14 = bf16[128,1536]{0,1:T(8,128)(2,1)S(1)} collective-permute-done((bf16[128,1536]{0,1:T(8,128)(2,1)}, bf16[128,1536]{0,1:T(8,128)(2,1)S(1)}, u32[]{:S(2)}, u32[]{:S(2)}) %collective-permute-start.14) | collective-permute-done | bytes 393248 | tf_op jit(solution)/shard_map/ppermute | solution.py:41
  77.0 6.4 %collective-permute-start.18 = (bf16[128,384]{1,0:T(8,128)(2,1)S(1)}, bf16[128,384]{1,0:T(8,128)(2,1)S(1)}, u32[]{:S(2)}, u32[]{:S(2)}) collective-permute-start(bf16[128,384]{1,0:T(8,128)(2,1)S(1)} %convolution_convert_fusion.4), channel_id=1, source_target_pairs={{0,224},{1,225},{2,226},{3,227},{4,4},{5,5},{6,6},{7,7},{8,72},{9,... | collective-permute-start | bytes 294920 | tf_op jit(solution)/shard_map/ppermute | solution.py:41
  83.9 1.2 collective-permute-start.24
  85.2 3.3 %collective-permute-start.9 = (bf16[128,1536]{0,1:T(8,128)(2,1)S(1)}, bf16[128,1536]{0,1:T(8,128)(2,1)S(1)}, u32[]{:S(2)}, u32[]{:S(2)}) collective-permute-start(bf16[128,1536]{0,1:T(8,128)(2,1)S(1)} %collective-permute-done.7), channel_id=1, source_target_pairs={{0,28},{1,29},{2,30},{3,31},{4,0},{5,1},{6,2},{7,3},{8,4},{9,5},{1... | collective-permute-start | bytes 1179656 | tf_op jit(solution)/shard_map/ppermute | solution.py:41
  88.5 5.3 %collective-permute-done.24 = bf16[512,384]{1,0:T(8,128)(2,1)S(1)} collective-permute-done((bf16[512,384]{1,0:T(8,128)(2,1)S(1)}, bf16[512,384]{1,0:T(8,128)(2,1)S(1)}, u32[]{:S(2)}, u32[]{:S(2)}) %collective-permute-start.24) | collective-permute-done | bytes 393248 | tf_op jit(solution)/shard_map/ppermute | solution.py:41
  94.0 4.5 %collective-permute-done.33 = bf16[128,384]{1,0:T(8,128)(2,1)S(1)} collective-permute-done((bf16[128,384]{1,0:T(8,128)(2,1)S(1)}, bf16[128,384]{1,0:T(8,128)(2,1)S(1)}, u32[]{:S(2)}, u32[]{:S(2)}) %collective-permute-start.33) | collective-permute-done | bytes 98336 | tf_op jit(solution)/shard_map/ppermute | solution.py:41
  98.5 5.8 %collective-permute-done.29 = bf16[128,384]{1,0:T(8,128)(2,1)S(1)} collective-permute-done((bf16[128,384]{1,0:T(8,128)(2,1)S(1)}, bf16[128,384]{1,0:T(8,128)(2,1)S(1)}, u32[]{:S(2)}, u32[]{:S(2)}) %collective-permute-start.29) | collective-permute-done | bytes 98336 | tf_op jit(solution)/shard_map/ppermute | solution.py:41
  104.3 2.5 %collective-permute-start.34 = (bf16[128,384]{1,0:T(8,128)(2,1)S(1)}, bf16[128,384]{1,0:T(8,128)(2,1)S(1)}, u32[]{:S(2)}, u32[]{:S(2)}) collective-permute-start(bf16[128,384]{1,0:T(8,128)(2,1)S(1)} %fusion.25), channel_id=1, source_target_pairs={{0,28},{1,29},{2,30},{3,31},{4,0},{5,1},{6,2},{7,3},{8,4},{9,5},{1... | collective-permute-start | bytes 294920 | tf_op jit(solution)/shard_map/ppermute | solution.py:41
  107.5 3.3 %collective-permute-start.11 = (bf16[128,1536]{0,1:T(8,128)(2,1)S(1)}, bf16[128,1536]{0,1:T(8,128)(2,1)S(1)}, u32[]{:S(2)}, u32[]{:S(2)}) collective-permute-start(bf16[128,1536]{0,1:T(8,128)(2,1)S(1)} %collective-permute-done.9), channel_id=1, source_target_pairs={{0,28},{1,29},{2,30},{3,31},{4,0},{5,1},{6,2},{7,3},{8,4},{9,5},{1... | collective-permute-start | bytes 1179656 | tf_op jit(solution)/shard_map/ppermute | solution.py:41
  111.3 1.5 collective-permute-done.30
  113.0 3.3 %collective-permute-start.35 = (bf16[128,384]{1,0:T(8,128)(2,1)S(1)}, bf16[128,384]{1,0:T(8,128)(2,1)S(1)}, u32[]{:S(2)}, u32[]{:S(2)}) collective-permute-start(bf16[128,384]{1,0:T(8,128)(2,1)S(1)} %fusion.26), channel_id=1, source_target_pairs={{0,28},{1,29},{2,30},{3,31},{4,0},{5,1},{6,2},{7,3},{8,4},{9,5},{1... | collective-permute-start | bytes 294920 | tf_op jit(solution)/shard_map/ppermute | solution.py:41
  116.2 2.5 %collective-permute-done.31 = bf16[128,384]{1,0:T(8,128)(2,1)S(1)} collective-permute-done((bf16[128,384]{1,0:T(8,128)(2,1)S(1)}, bf16[128,384]{1,0:T(8,128)(2,1)S(1)}, u32[]{:S(2)}, u32[]{:S(2)}) %collective-permute-start.31) | collective-permute-done | bytes 98336 | tf_op jit(solution)/shard_map/ppermute | solution.py:41
  119.0 1.9 %collective-permute-start.6 = (bf16[128,384]{1,0:T(8,128)(2,1)S(1)}, bf16[128,384]{1,0:T(8,128)(2,1)S(1)}, u32[]{:S(2)}, u32[]{:S(2)}) collective-permute-start(bf16[128,384]{1,0:T(8,128)(2,1)S(1)} %convolution_convert_fusion.10), channel_id=1, source_target_pairs={{0,64},{1,65},{2,66},{3,67},{4,132},{5,133},{6,134},{7,135},{8,200... | collective-permute-start | bytes 294920 | tf_op jit(solution)/shard_map/ppermute | solution.py:41
  120.9 3.7 %collective-permute-done.32 = bf16[128,384]{1,0:T(8,128)(2,1)S(1)} collective-permute-done((bf16[128,384]{1,0:T(8,128)(2,1)S(1)}, bf16[128,384]{1,0:T(8,128)(2,1)S(1)}, u32[]{:S(2)}, u32[]{:S(2)}) %collective-permute-start.32) | collective-permute-done | bytes 98336 | tf_op jit(solution)/shard_map/ppermute | solution.py:41
  124.7 1.9 %collective-permute-start.17 = (bf16[128,384]{1,0:T(8,128)(2,1)S(1)}, bf16[128,384]{1,0:T(8,128)(2,1)S(1)}, u32[]{:S(2)}, u32[]{:S(2)}) collective-permute-start(bf16[128,384]{1,0:T(8,128)(2,1)S(1)} %convolution_convert_fusion.5), channel_id=1, source_target_pairs={{0,160},{1,161},{2,162},{3,163},{4,228},{5,229},{6,230},{7,231},{8... | collective-permute-start | bytes 294920 | tf_op jit(solution)/shard_map/ppermute | solution.py:41
  129.4 6.1 %collective-permute-start.8 = (bf16[128,384]{1,0:T(8,128)(2,1)S(1)}, bf16[128,384]{1,0:T(8,128)(2,1)S(1)}, u32[]{:S(2)}, u32[]{:S(2)}) collective-permute-start(bf16[128,384]{1,0:T(8,128)(2,1)S(1)} %convolution_convert_fusion.9), channel_id=1, source_target_pairs={{0,128},{1,129},{2,130},{3,131},{4,196},{5,197},{6,198},{7,199},{8... | collective-permute-start | bytes 294920 | tf_op jit(solution)/shard_map/ppermute | solution.py:41
  135.5 3.9 %collective-permute-start.16 = (bf16[128,384]{1,0:T(8,128)(2,1)S(1)}, bf16[128,384]{1,0:T(8,128)(2,1)S(1)}, u32[]{:S(2)}, u32[]{:S(2)}) collective-permute-start(bf16[128,384]{1,0:T(8,128)(2,1)S(1)} %convolution_convert_fusion.6), channel_id=1, source_target_pairs={{0,96},{1,97},{2,98},{3,99},{4,164},{5,165},{6,166},{7,167},{8,232... | collective-permute-start | bytes 294920 | tf_op jit(solution)/shard_map/ppermute | solution.py:41
  139.4 1.9 %collective-permute-start.10 = (bf16[128,384]{1,0:T(8,128)(2,1)S(1)}, bf16[128,384]{1,0:T(8,128)(2,1)S(1)}, u32[]{:S(2)}, u32[]{:S(2)}) collective-permute-start(bf16[128,384]{1,0:T(8,128)(2,1)S(1)} %convolution_convert_fusion.8), channel_id=1, source_target_pairs={{0,192},{1,193},{2,194},{3,195},{4,36},{5,37},{6,38},{7,39},{8,104... | collective-permute-start | bytes 294920 | tf_op jit(solution)/shard_map/ppermute | solution.py:41
  141.3 1.9 %collective-permute-start.12 = (bf16[128,384]{1,0:T(8,128)(2,1)S(1)}, bf16[128,384]{1,0:T(8,128)(2,1)S(1)}, u32[]{:S(2)}, u32[]{:S(2)}) collective-permute-start(bf16[128,384]{1,0:T(8,128)(2,1)S(1)} %convolution_convert_fusion.7), channel_id=1, source_target_pairs={{0,32},{1,33},{2,34},{3,35},{4,100},{5,101},{6,102},{7,103},{8,168... | collective-permute-start | bytes 294920 | tf_op jit(solution)/shard_map/ppermute | solution.py:41
  143.3 3.2 %convolution_multiply_fusion = f32[1536,384]{1,0:T(8,128)} fusion(bf16[1024,1536]{0,1:T(8,128)(2,1)S(1)} %constant_dynamic-update-slice_fusion.5, bf16[1024,384]{1,0:T(8,128)(2,1)S(1)} %bitcast_select_fusion), kind=kOutput, calls=%fused_computation.3 | convolution fusion | flops 1208549376 | bytes 6291456 | tf_op jit(solution)/shard_map/dot_general | solution.py:138
  146.5 2.9 %collective-permute-done.12 = bf16[128,384]{1,0:T(8,128)(2,1)S(1)} collective-permute-done((bf16[128,384]{1,0:T(8,128)(2,1)S(1)}, bf16[128,384]{1,0:T(8,128)(2,1)S(1)}, u32[]{:S(2)}, u32[]{:S(2)}) %collective-permute-start.12) | collective-permute-done | bytes 98336 | tf_op jit(solution)/shard_map/ppermute | solution.py:41
  149.3 1.6 %add_convert_fusion.2 = bf16[128,384]{1,0:T(8,128)(2,1)} fusion(bf16[128,384]{1,0:T(8,128)(2,1)S(1)} %collective-permute-done.18, bf16[128,384]{1,0:T(8,128)(2,1)S(1)} %collective-permute-done.17, bf16[128,384]{1,0:T(8,128)(2,1)S(1)} %collective-permute-done.16, bf16[128,384]{1,0:T(8,128)(2,1)S(1)} %collective-permute-done.12, ...), kind=kLoop, calls=%fused_computation.60 | loop fusion | flops 786432 | bytes 884736 | tf_op jit(solution)/shard_map/convert_element_type | solution.py:136
  (103 shorter events, 20.3 us)
Async XLA Ops:
  0.6 12.7 %copy-start = (s32[4]{0:T(128)S(1)}, s32[4]{0:T(128)}, u32[]{:S(2)}) copy-start(s32[4]{0:T(128)} %constant.148.clone) | copy-start | bytes 52
  0.6 13.4 %copy-start.1 = (bf16[1536,384]{1,0:T(8,128)(2,1)S(1)}, bf16[1536,384]{1,0:T(8,128)(2,1)}, u32[]{:S(2)}) copy-start(bf16[1536,384]{1,0:T(8,128)(2,1)} %param.9) | copy-start | bytes 3538948
  0.7 16.4 %collective-permute-start.19 = (bf16[128,384]{1,0:T(8,128)(2,1)}, bf16[128,384]{1,0:T(8,128)(2,1)}, u32[]{:S(2)}, u32[]{:S(2)}) collective-permute-start(bf16[128,384]{1,0:T(8,128)(2,1)} %param.11), channel_id=1, source_target_pairs={{0,64},{1,65},{2,66},{3,67},{4,68},{5,69},{6,70},{7,71},{8,72},{9,... | collective-permute-start | bytes 294920 | tf_op jit(solution)/shard_map/ppermute | solution.py:41
  2.3 14.8 %collective-permute-start.20 = (bf16[128,384]{1,0:T(8,128)(2,1)}, bf16[128,384]{1,0:T(8,128)(2,1)}, u32[]{:S(2)}, u32[]{:S(2)}) collective-permute-start(bf16[128,384]{1,0:T(8,128)(2,1)} %param.11), channel_id=1, source_target_pairs={{0,192},{1,193},{2,194},{3,195},{4,196},{5,197},{6,198},{7,199},{8... | collective-permute-start | bytes 294920 | tf_op jit(solution)/shard_map/ppermute | solution.py:41
  4.0 13.1 %collective-permute-start.21 = (bf16[128,384]{1,0:T(8,128)(2,1)}, bf16[128,384]{1,0:T(8,128)(2,1)}, u32[]{:S(2)}, u32[]{:S(2)}) collective-permute-start(bf16[128,384]{1,0:T(8,128)(2,1)} %param.11), channel_id=1, source_target_pairs={{0,128},{1,129},{2,130},{3,131},{4,132},{5,133},{6,134},{7,135},{8... | collective-permute-start | bytes 294920 | tf_op jit(solution)/shard_map/ppermute | solution.py:41
  8.3 17.1 %collective-permute-start = (bf16[128,384]{0,1:T(8,128)(2,1)}, bf16[128,384]{0,1:T(8,128)(2,1)}, u32[]{:S(2)}, u32[]{:S(2)}) collective-permute-start(bf16[128,384]{0,1:T(8,128)(2,1)} %fusion.32), channel_id=1, source_target_pairs={{0,0},{1,1},{2,2},{3,3},{4,36},{5,37},{6,38},{7,39},{8,72},{9,73},... | collective-permute-start | bytes 294920 | tf_op jit(solution)/shard_map/ppermute | solution.py:41
  14.1 0.7 copy-start.4
  16.3 0.9 copy-start.2
  18.2 24.6 %collective-permute-start.22 = (bf16[4,128,384]{2,1,0:T(8,128)(2,1)S(1)}, bf16[4,128,384]{2,1,0:T(8,128)(2,1)S(1)}, u32[]{:S(2)}, u32[]{:S(2)}) collective-permute-start(bf16[4,128,384]{2,1,0:T(8,128)(2,1)S(1)} %pad_maximum_fusion), channel_id=1, source_target_pairs={{0,32},{1,33},{2,34},{3,35},{4,36},{5,37},{6,38},{7,39},{8,40},{9,... | collective-permute-start | bytes 1179656 | tf_op jit(solution)/shard_map/ppermute | solution.py:41
  25.5 9.8 %collective-permute-start.1 = (bf16[128,384]{0,1:T(8,128)(2,1)}, bf16[128,384]{0,1:T(8,128)(2,1)S(1)}, u32[]{:S(2)}, u32[]{:S(2)}) collective-permute-start(bf16[128,384]{0,1:T(8,128)(2,1)} %collective-permute-done), channel_id=1, source_target_pairs={{0,1},{1,2},{2,3},{3,0},{4,5},{5,6},{6,7},{7,4},{8,9},{9,10},{10,1... | collective-permute-start | bytes 294920 | tf_op jit(solution)/shard_map/ppermute | solution.py:41
  27.0 8.3 %collective-permute-start.2 = (bf16[128,384]{0,1:T(8,128)(2,1)}, bf16[128,384]{0,1:T(8,128)(2,1)S(1)}, u32[]{:S(2)}, u32[]{:S(2)}) collective-permute-start(bf16[128,384]{0,1:T(8,128)(2,1)} %collective-permute-done), channel_id=1, source_target_pairs={{0,3},{1,0},{2,1},{3,2},{4,7},{5,4},{6,5},{7,6},{8,11},{9,8},{10,9... | collective-permute-start | bytes 294920 | tf_op jit(solution)/shard_map/ppermute | solution.py:41
  27.5 7.8 %collective-permute-start.3 = (bf16[128,384]{0,1:T(8,128)(2,1)}, bf16[128,384]{0,1:T(8,128)(2,1)S(1)}, u32[]{:S(2)}, u32[]{:S(2)}) collective-permute-start(bf16[128,384]{0,1:T(8,128)(2,1)} %collective-permute-done), channel_id=1, source_target_pairs={{0,2},{1,3},{2,0},{3,1},{4,6},{5,7},{6,4},{7,5},{8,10},{9,11},{10,... | collective-permute-start | bytes 294920 | tf_op jit(solution)/shard_map/ppermute | solution.py:41
  35.3 15.2 %collective-permute-start.13 = (bf16[128,1536]{0,1:T(8,128)(2,1)S(1)}, bf16[128,1536]{0,1:T(8,128)(2,1)}, u32[]{:S(2)}, u32[]{:S(2)}) collective-permute-start(bf16[128,1536]{0,1:T(8,128)(2,1)S(1)} %bitcast.130), channel_id=1, source_target_pairs={{0,4},{1,5},{2,6},{3,7},{4,8},{5,9},{6,10},{7,11},{8,12},{9,13},{1... | collective-permute-start | bytes 1179656 | tf_op jit(solution)/shard_map/ppermute | solution.py:41
  35.4 18.3 %collective-permute-start.5 = (bf16[128,1536]{0,1:T(8,128)(2,1)S(1)}, bf16[128,1536]{0,1:T(8,128)(2,1)}, u32[]{:S(2)}, u32[]{:S(2)}) collective-permute-start(bf16[128,1536]{0,1:T(8,128)(2,1)S(1)} %bitcast.131), channel_id=1, source_target_pairs={{0,28},{1,29},{2,30},{3,31},{4,0},{5,1},{6,2},{7,3},{8,4},{9,5},{1... | collective-permute-start | bytes 1179656 | tf_op jit(solution)/shard_map/ppermute | solution.py:41
  39.8 89.6 %collective-permute-start.4 = (bf16[128,384]{1,0:T(8,128)(2,1)}, bf16[128,384]{1,0:T(8,128)(2,1)}, u32[]{:S(2)}, u32[]{:S(2)}) collective-permute-start(bf16[128,384]{1,0:T(8,128)(2,1)} %convolution_convert_fusion.11), channel_id=1, source_target_pairs={{0,0},{1,1},{2,2},{3,3},{4,68},{5,69},{6,70},{7,71},{8,136},{9,137... | collective-permute-start | bytes 294920 | tf_op jit(solution)/shard_map/ppermute | solution.py:41
  46.9 38.3 %collective-permute-start.25 = (bf16[512,384]{1,0:T(8,128)(2,1)S(1)}, bf16[512,384]{1,0:T(8,128)(2,1)S(1)}, u32[]{:S(2)}, u32[]{:S(2)}) collective-permute-start(bf16[512,384]{1,0:T(8,128)(2,1)S(1)} %convolution_convert_fusion.2), channel_id=1, source_target_pairs={{0,3},{1,0},{2,1},{3,2},{4,7},{5,4},{6,5},{7,6},{8,11},{9,8},{10,9... | collective-permute-start | bytes 1179656 | tf_op jit(solution)/shard_map/ppermute | solution.py:41
  48.4 12.1 %collective-permute-start.23 = (bf16[512,384]{1,0:T(8,128)(2,1)S(1)}, bf16[512,384]{1,0:T(8,128)(2,1)S(1)}, u32[]{:S(2)}, u32[]{:S(2)}) collective-permute-start(bf16[512,384]{1,0:T(8,128)(2,1)S(1)} %convolution_convert_fusion.3), channel_id=1, source_target_pairs={{0,1},{1,2},{2,3},{3,0},{4,5},{5,6},{6,7},{7,4},{8,9},{9,10},{10,1... | collective-permute-start | bytes 1179656 | tf_op jit(solution)/shard_map/ppermute | solution.py:41
  50.5 15.4 %collective-permute-start.27 = (bf16[512,384]{1,0:T(8,128)(2,1)S(1)}, bf16[512,384]{1,0:T(8,128)(2,1)S(1)}, u32[]{:S(2)}, u32[]{:S(2)}) collective-permute-start(bf16[512,384]{1,0:T(8,128)(2,1)S(1)} %convolution_convert_fusion), channel_id=1, source_target_pairs={{0,3},{1,0},{2,1},{3,2},{4,7},{5,4},{6,5},{7,6},{8,11},{9,8},{10,9... | collective-permute-start | bytes 1179656 | tf_op jit(solution)/shard_map/ppermute | solution.py:41
  52.0 3.8 %copy-start.3 = (bf16[1024,1536]{0,1:T(8,128)(2,1)S(1)}, bf16[1024,1536]{0,1:T(8,128)(2,1)}, u32[]{:S(2)}) copy-start(bf16[1024,1536]{0,1:T(8,128)(2,1)} %constant_dynamic-update-slice_fusion.12) | copy-start | bytes 9437188
  53.7 30.2 %collective-permute-start.26 = (bf16[512,384]{1,0:T(8,128)(2,1)S(1)}, bf16[512,384]{1,0:T(8,128)(2,1)S(1)}, u32[]{:S(2)}, u32[]{:S(2)}) collective-permute-start(bf16[512,384]{1,0:T(8,128)(2,1)S(1)} %convolution_convert_fusion.1), channel_id=1, source_target_pairs={{0,1},{1,2},{2,3},{3,0},{4,5},{5,6},{6,7},{7,4},{8,9},{9,10},{10,1... | collective-permute-start | bytes 1179656 | tf_op jit(solution)/shard_map/ppermute | solution.py:41
  60.5 8.0 %collective-permute-start.7 = (bf16[128,1536]{0,1:T(8,128)(2,1)}, bf16[128,1536]{0,1:T(8,128)(2,1)S(1)}, u32[]{:S(2)}, u32[]{:S(2)}) collective-permute-start(bf16[128,1536]{0,1:T(8,128)(2,1)} %collective-permute-done.5), channel_id=1, source_target_pairs={{0,28},{1,29},{2,30},{3,31},{4,0},{5,1},{6,2},{7,3},{8,4},{9,5},{1... | collective-permute-start | bytes 1179656 | tf_op jit(solution)/shard_map/ppermute | solution.py:41
  66.0 11.0 %collective-permute-start.14 = (bf16[128,1536]{0,1:T(8,128)(2,1)}, bf16[128,1536]{0,1:T(8,128)(2,1)S(1)}, u32[]{:S(2)}, u32[]{:S(2)}) collective-permute-start(bf16[128,1536]{0,1:T(8,128)(2,1)} %collective-permute-done.13), channel_id=1, source_target_pairs={{0,4},{1,5},{2,6},{3,7},{4,8},{5,9},{6,10},{7,11},{8,12},{9,13},{1... | collective-permute-start | bytes 1179656 | tf_op jit(solution)/shard_map/ppermute | solution.py:41
  68.5 16.6 %collective-permute-start.28 = (bf16[512,384]{1,0:T(8,128)(2,1)S(1)}, bf16[512,384]{1,0:T(8,128)(2,1)S(1)}, u32[]{:S(2)}, u32[]{:S(2)}) collective-permute-start(bf16[512,384]{1,0:T(8,128)(2,1)S(1)} %add_convert_fusion), channel_id=1, source_target_pairs={{0,3},{1,0},{2,1},{3,2},{4,7},{5,4},{6,5},{7,6},{8,11},{9,8},{10,9... | collective-permute-start | bytes 1179656 | tf_op jit(solution)/shard_map/ppermute | solution.py:41
  77.0 58.5 %collective-permute-start.18 = (bf16[128,384]{1,0:T(8,128)(2,1)S(1)}, bf16[128,384]{1,0:T(8,128)(2,1)S(1)}, u32[]{:S(2)}, u32[]{:S(2)}) collective-permute-start(bf16[128,384]{1,0:T(8,128)(2,1)S(1)} %convolution_convert_fusion.4), channel_id=1, source_target_pairs={{0,224},{1,225},{2,226},{3,227},{4,4},{5,5},{6,6},{7,7},{8,72},{9,... | collective-permute-start | bytes 294920 | tf_op jit(solution)/shard_map/ppermute | solution.py:41
  83.9 10.0 %collective-permute-start.24 = (bf16[512,384]{1,0:T(8,128)(2,1)S(1)}, bf16[512,384]{1,0:T(8,128)(2,1)S(1)}, u32[]{:S(2)}, u32[]{:S(2)}) collective-permute-start(bf16[512,384]{1,0:T(8,128)(2,1)S(1)} %add_convert_fusion.1), channel_id=1, source_target_pairs={{0,1},{1,2},{2,3},{3,0},{4,5},{5,6},{6,7},{7,4},{8,9},{9,10},{10,1... | collective-permute-start | bytes 1179656 | tf_op jit(solution)/shard_map/ppermute | solution.py:41
  85.1 22.4 %collective-permute-start.15 = (bf16[128,1536]{0,1:T(8,128)(2,1)S(1)}, bf16[128,1536]{0,1:T(8,128)(2,1)S(1)}, u32[]{:S(2)}, u32[]{:S(2)}) collective-permute-start(bf16[128,1536]{0,1:T(8,128)(2,1)S(1)} %collective-permute-done.14), channel_id=1, source_target_pairs={{0,4},{1,5},{2,6},{3,7},{4,8},{5,9},{6,10},{7,11},{8,12},{9,13},{1... | collective-permute-start | bytes 1179656 | tf_op jit(solution)/shard_map/ppermute | solution.py:41
  85.2 21.6 %collective-permute-start.9 = (bf16[128,1536]{0,1:T(8,128)(2,1)S(1)}, bf16[128,1536]{0,1:T(8,128)(2,1)S(1)}, u32[]{:S(2)}, u32[]{:S(2)}) collective-permute-start(bf16[128,1536]{0,1:T(8,128)(2,1)S(1)} %collective-permute-done.7), channel_id=1, source_target_pairs={{0,28},{1,29},{2,30},{3,31},{4,0},{5,1},{6,2},{7,3},{8,4},{9,5},{1... | collective-permute-start | bytes 1179656 | tf_op jit(solution)/shard_map/ppermute | solution.py:41
  93.9 4.6 %collective-permute-start.33 = (bf16[128,384]{1,0:T(8,128)(2,1)S(1)}, bf16[128,384]{1,0:T(8,128)(2,1)S(1)}, u32[]{:S(2)}, u32[]{:S(2)}) collective-permute-start(bf16[128,384]{1,0:T(8,128)(2,1)S(1)} %get-tuple-element.8), channel_id=1, source_target_pairs={{0,28},{1,29},{2,30},{3,31},{4,0},{5,1},{6,2},{7,3},{8,4},{9,5},{1... | collective-permute-start | bytes 294920 | tf_op jit(solution)/shard_map/ppermute | solution.py:41
  98.5 5.8 %collective-permute-start.29 = (bf16[128,384]{1,0:T(8,128)(2,1)S(1)}, bf16[128,384]{1,0:T(8,128)(2,1)S(1)}, u32[]{:S(2)}, u32[]{:S(2)}) collective-permute-start(bf16[128,384]{1,0:T(8,128)(2,1)S(1)} %get-tuple-element.7), channel_id=1, source_target_pairs={{0,4},{1,5},{2,6},{3,7},{4,8},{5,9},{6,10},{7,11},{8,12},{9,13},{1... | collective-permute-start | bytes 294920 | tf_op jit(solution)/shard_map/ppermute | solution.py:41
  104.3 8.6 %collective-permute-start.34 = (bf16[128,384]{1,0:T(8,128)(2,1)S(1)}, bf16[128,384]{1,0:T(8,128)(2,1)S(1)}, u32[]{:S(2)}, u32[]{:S(2)}) collective-permute-start(bf16[128,384]{1,0:T(8,128)(2,1)S(1)} %fusion.25), channel_id=1, source_target_pairs={{0,28},{1,29},{2,30},{3,31},{4,0},{5,1},{6,2},{7,3},{8,4},{9,5},{1... | collective-permute-start | bytes 294920 | tf_op jit(solution)/shard_map/ppermute | solution.py:41
  106.9 5.9 %collective-permute-start.30 = (bf16[128,384]{1,0:T(8,128)(2,1)S(1)}, bf16[128,384]{1,0:T(8,128)(2,1)S(1)}, u32[]{:S(2)}, u32[]{:S(2)}) collective-permute-start(bf16[128,384]{1,0:T(8,128)(2,1)S(1)} %fusion.27), channel_id=1, source_target_pairs={{0,4},{1,5},{2,6},{3,7},{4,8},{5,9},{6,10},{7,11},{8,12},{9,13},{1... | collective-permute-start | bytes 294920 | tf_op jit(solution)/shard_map/ppermute | solution.py:41
  107.5 19.1 %collective-permute-start.11 = (bf16[128,1536]{0,1:T(8,128)(2,1)S(1)}, bf16[128,1536]{0,1:T(8,128)(2,1)S(1)}, u32[]{:S(2)}, u32[]{:S(2)}) collective-permute-start(bf16[128,1536]{0,1:T(8,128)(2,1)S(1)} %collective-permute-done.9), channel_id=1, source_target_pairs={{0,28},{1,29},{2,30},{3,31},{4,0},{5,1},{6,2},{7,3},{8,4},{9,5},{1... | collective-permute-start | bytes 1179656 | tf_op jit(solution)/shard_map/ppermute | solution.py:41
  112.8 5.9 %collective-permute-start.31 = (bf16[128,384]{1,0:T(8,128)(2,1)S(1)}, bf16[128,384]{1,0:T(8,128)(2,1)S(1)}, u32[]{:S(2)}, u32[]{:S(2)}) collective-permute-start(bf16[128,384]{1,0:T(8,128)(2,1)S(1)} %fusion.28), channel_id=1, source_target_pairs={{0,4},{1,5},{2,6},{3,7},{4,8},{5,9},{6,10},{7,11},{8,12},{9,13},{1... | collective-permute-start | bytes 294920 | tf_op jit(solution)/shard_map/ppermute | solution.py:41
  113.0 6.0 %collective-permute-start.35 = (bf16[128,384]{1,0:T(8,128)(2,1)S(1)}, bf16[128,384]{1,0:T(8,128)(2,1)S(1)}, u32[]{:S(2)}, u32[]{:S(2)}) collective-permute-start(bf16[128,384]{1,0:T(8,128)(2,1)S(1)} %fusion.26), channel_id=1, source_target_pairs={{0,28},{1,29},{2,30},{3,31},{4,0},{5,1},{6,2},{7,3},{8,4},{9,5},{1... | collective-permute-start | bytes 294920 | tf_op jit(solution)/shard_map/ppermute | solution.py:41
  118.8 5.9 %collective-permute-start.32 = (bf16[128,384]{1,0:T(8,128)(2,1)S(1)}, bf16[128,384]{1,0:T(8,128)(2,1)S(1)}, u32[]{:S(2)}, u32[]{:S(2)}) collective-permute-start(bf16[128,384]{1,0:T(8,128)(2,1)S(1)} %fusion.29), channel_id=1, source_target_pairs={{0,4},{1,5},{2,6},{3,7},{4,8},{5,9},{6,10},{7,11},{8,12},{9,13},{1... | collective-permute-start | bytes 294920 | tf_op jit(solution)/shard_map/ppermute | solution.py:41
  119.0 20.4 %collective-permute-start.6 = (bf16[128,384]{1,0:T(8,128)(2,1)S(1)}, bf16[128,384]{1,0:T(8,128)(2,1)S(1)}, u32[]{:S(2)}, u32[]{:S(2)}) collective-permute-start(bf16[128,384]{1,0:T(8,128)(2,1)S(1)} %convolution_convert_fusion.10), channel_id=1, source_target_pairs={{0,64},{1,65},{2,66},{3,67},{4,132},{5,133},{6,134},{7,135},{8,200... | collective-permute-start | bytes 294920 | tf_op jit(solution)/shard_map/ppermute | solution.py:41
  124.7 21.8 %collective-permute-start.17 = (bf16[128,384]{1,0:T(8,128)(2,1)S(1)}, bf16[128,384]{1,0:T(8,128)(2,1)S(1)}, u32[]{:S(2)}, u32[]{:S(2)}) collective-permute-start(bf16[128,384]{1,0:T(8,128)(2,1)S(1)} %convolution_convert_fusion.5), channel_id=1, source_target_pairs={{0,160},{1,161},{2,162},{3,163},{4,228},{5,229},{6,230},{7,231},{8... | collective-permute-start | bytes 294920 | tf_op jit(solution)/shard_map/ppermute | solution.py:41
  126.6 14.7 %collective-permute-start.36 = (bf16[128,384]{1,0:T(8,128)(2,1)S(1)}, bf16[128,384]{1,0:T(8,128)(2,1)S(1)}, u32[]{:S(2)}, u32[]{:S(2)}) collective-permute-start(bf16[128,384]{1,0:T(8,128)(2,1)S(1)} %fusion.31), channel_id=1, source_target_pairs={{0,0},{1,1},{2,2},{3,3},{4,64},{5,65},{6,66},{7,67},{8,128},{9,129... | collective-permute-start | bytes 294920 | tf_op jit(solution)/shard_map/ppermute | solution.py:41
  129.4 17.1 %collective-permute-start.8 = (bf16[128,384]{1,0:T(8,128)(2,1)S(1)}, bf16[128,384]{1,0:T(8,128)(2,1)S(1)}, u32[]{:S(2)}, u32[]{:S(2)}) collective-permute-start(bf16[128,384]{1,0:T(8,128)(2,1)S(1)} %convolution_convert_fusion.9), channel_id=1, source_target_pairs={{0,128},{1,129},{2,130},{3,131},{4,196},{5,197},{6,198},{7,199},{8... | collective-permute-start | bytes 294920 | tf_op jit(solution)/shard_map/ppermute | solution.py:41
  135.5 11.0 %collective-permute-start.16 = (bf16[128,384]{1,0:T(8,128)(2,1)S(1)}, bf16[128,384]{1,0:T(8,128)(2,1)S(1)}, u32[]{:S(2)}, u32[]{:S(2)}) collective-permute-start(bf16[128,384]{1,0:T(8,128)(2,1)S(1)} %convolution_convert_fusion.6), channel_id=1, source_target_pairs={{0,96},{1,97},{2,98},{3,99},{4,164},{5,165},{6,166},{7,167},{8,232... | collective-permute-start | bytes 294920 | tf_op jit(solution)/shard_map/ppermute | solution.py:41
  139.4 7.1 %collective-permute-start.10 = (bf16[128,384]{1,0:T(8,128)(2,1)S(1)}, bf16[128,384]{1,0:T(8,128)(2,1)S(1)}, u32[]{:S(2)}, u32[]{:S(2)}) collective-permute-start(bf16[128,384]{1,0:T(8,128)(2,1)S(1)} %convolution_convert_fusion.8), channel_id=1, source_target_pairs={{0,192},{1,193},{2,194},{3,195},{4,36},{5,37},{6,38},{7,39},{8,104... | collective-permute-start | bytes 294920 | tf_op jit(solution)/shard_map/ppermute | solution.py:41
  141.3 8.0 %collective-permute-start.12 = (bf16[128,384]{1,0:T(8,128)(2,1)S(1)}, bf16[128,384]{1,0:T(8,128)(2,1)S(1)}, u32[]{:S(2)}, u32[]{:S(2)}) collective-permute-start(bf16[128,384]{1,0:T(8,128)(2,1)S(1)} %convolution_convert_fusion.7), channel_id=1, source_target_pairs={{0,32},{1,33},{2,34},{3,35},{4,100},{5,101},{6,102},{7,103},{8,168... | collective-permute-start | bytes 294920 | tf_op jit(solution)/shard_map/ppermute | solution.py:41

commit v2 on v0

v2 whole, which is shorter than its diff:
```python
import jax
import jax.numpy as jnp
from jax import lax
from jax.experimental import pallas as pl
from jax.experimental.pallas import tpu as pltpu
from jax.sharding import Mesh
from jax.sharding import PartitionSpec as P

NR, NC, NZ, NX = 8, 2, 8, 4
BF, F32 = jnp.bfloat16, jnp.float32
VMEM = 48 * 1024 * 1024


def dequantize_rows(values, scales):
    blocks = (
        values.astype(F32).reshape(values.shape[0], scales.shape[1], -1)
        * scales[:, :, None]
    )
    return blocks.reshape(values.shape).astype(BF)


def skew(r):
    return r // NC + r % NC * (NR // NC)


def unskew(d):
    d = d % NZ
    return d % (NR // NC) * NC + d // (NR // NC)


def move(value, where):
    pairs = []
    for r in range(NR):
        for z in range(NZ):
            for x in range(NX):
                r2, z2, x2 = where(r, z, x)
                to = ((r2 % NR) * NZ + z2 % NZ) * NX + x2 % NX
                pairs.append(((r * NZ + z) * NX + x, to))
    return lax.ppermute(value, ("r", "z", "x"), pairs)


def along_x(value, k):
    return move(value, lambda r, z, x: (r, z, x + k))


def along_z(value, k):
    return move(value, lambda r, z, x: (r, z + k, x))


def mm(a, b):
    return jnp.dot(a, b, preferred_element_type=F32)


def grad_kernel(scales, cot, values, parts, weight):
    at = pl.program_id(0)
    size = 128
    for i in range(values.shape[0] // size):
        for j in range(values.shape[1] // size):
            rows, cols = pl.ds(i * size, size), pl.ds(j * size, size)
            scale = scales[at * (values.shape[0] // size) + i, j]
            weight[rows, cols] = (values[rows, cols].astype(F32) * scale).astype(BF)
    part = lax.dot_general(
        cot[...], weight[...], (((1,), (1,)), ((), ())), preferred_element_type=F32
    )
    parts[...] = part.astype(BF).reshape(parts.shape)


def grad_parts(cot, values, scales):
    t, n = cot.shape
    k = values.shape[0]
    rows = t // NR
    return pl.pallas_call(
        grad_kernel,
        grid=(NX,),
        out_shape=(
            jax.ShapeDtypeStruct((NR, NX, rows, k // NX), BF),
            jax.ShapeDtypeStruct((k, n), BF),
        ),
        in_specs=[
            pl.BlockSpec(memory_space=pltpu.SMEM),
            pl.BlockSpec((t, n), lambda i: (0, 0)),
            pl.BlockSpec((k // NX, n), lambda i: (i, 0)),
        ],
        out_specs=(
            pl.BlockSpec((NR, 1, rows, k // NX), lambda i: (0, i, 0, 0)),
            pl.BlockSpec((k // NX, n), lambda i: (i, 0)),
        ),
        compiler_params=pltpu.CompilerParams(vmem_limit_bytes=VMEM),
        cost_estimate=pl.CostEstimate(
            flops=2 * t * n * k, bytes_accessed=2 * t * k, transcendentals=0
        ),
    )(scales, cot, values)


def sum_kernel(z, parts, out):
    for s in range(NZ):
        at = lax.rem(z[0] + s, NZ)
        total = parts[at, 0].astype(F32)
        for i in range(1, NX):
            total = total + parts[at, i].astype(F32)
        out[s] = total


def sum_over_x(z, parts):
    _, _, rows, k = parts.shape
    return pl.pallas_call(
        sum_kernel,
        out_shape=jax.ShapeDtypeStruct((NZ, rows, k), F32),
        in_specs=[
            pl.BlockSpec(memory_space=pltpu.SMEM),
            pl.BlockSpec(memory_space=pltpu.VMEM),
        ],
        out_specs=pl.BlockSpec(memory_space=pltpu.VMEM),
        compiler_params=pltpu.CompilerParams(vmem_limit_bytes=VMEM),
        cost_estimate=pl.CostEstimate(
            flops=NZ * NX * rows * k, bytes_accessed=12 * NZ * rows * k, transcendentals=0
        ),
    )(z.reshape(1), parts)


def assemble_kernel(x, *refs):
    parts, out = refs[:NX], refs[NX]
    n = parts[0].shape[1]
    for off in range(NX):
        at = pl.multiple_of(lax.rem(x[0] + off, NX) * n, 128)
        out[:, pl.ds(at, n)] = parts[off][...]


def assemble(x, parts):
    t, n = parts[0].shape
    return pl.pallas_call(
        assemble_kernel,
        out_shape=jax.ShapeDtypeStruct((t, NX * n), BF),
        in_specs=[pl.BlockSpec(memory_space=pltpu.SMEM)]
        + [pl.BlockSpec(memory_space=pltpu.VMEM)] * NX,
        out_specs=pl.BlockSpec(memory_space=pltpu.VMEM),
        cost_estimate=pl.CostEstimate(
            flops=0, bytes_accessed=4 * t * NX * n, transcendentals=0
        ),
    )(x.reshape(1), *parts)


def together(*values):
    return lax.optimization_barrier(values)


def per_device(act_values, act_scales, weight_values, weight_scales, cotangent):
    r, z, x = (lax.axis_index(a) for a in ("r", "z", "x"))
    t, n = cotangent.shape

    act = dequantize_rows(act_values, act_scales)
    act, cotangent = together(act, cotangent)
    here = move(act, lambda r, z, x: (z, z + skew(r), x))
    cot = lax.all_gather(cotangent, "r", axis=0, tiled=True)
    here, cot = together(here, cot)

    sides = [along_x(here, -1), along_x(here, 2), along_x(here, 1)]
    parts, weight = grad_parts(cot, weight_values, weight_scales)
    parts, *sides = together(parts, *sides)
    parts = lax.all_to_all(
        parts.reshape(NR * NX, t, n), ("r", "x"), split_axis=0, concat_axis=0, tiled=True
    )

    blocks = {0: assemble(x, [here, *sides])}
    for s in range(1, NZ // 2 + 1):
        blocks[s] = along_z(blocks[s - 1], -1)
        if s < NZ // 2:
            blocks[NZ - s] = along_z(blocks[(NZ - s + 1) % NZ], 1)
    shares = jnp.zeros((NR, t, n), BF)
    for s in (0, 1, 7, 2, 6, 3, 5, 4):
        part = mm(blocks[s], weight).astype(BF)
        shares = lax.dynamic_update_slice(
            shares, part[None], (unskew(z + s - r), 0, 0)
        )
    shares = lax.all_to_all(shares, "r", split_axis=0, concat_axis=0, tiled=True)
    output = jnp.sum(shares.astype(F32), axis=0).astype(BF)

    sums = sum_over_x(z, parts.reshape(NZ, NX, t, n))
    low = sums.astype(BF)
    across = along_z(low[4], 4)
    up = along_z(jnp.stack([low[1], low[3]]), 1)
    down = along_z(jnp.stack([low[7], low[5]]), -1)
    up, down = up.astype(F32), down.astype(F32)
    up2 = along_z((sums[2] + up[1]).astype(BF), 2)
    down2 = along_z((sums[6] + down[1]).astype(BF), -2)
    total = sums[0] + up[0] + down[0] + across.astype(F32)
    activation_grad = (total + up2.astype(F32) + down2.astype(F32)).astype(BF)

    cot, _ = together(cot, blocks[1])
    cot = cot.reshape(NR, t, n)
    cot = jnp.concatenate(
        [
            lax.dynamic_index_in_dim(cot, unskew(z + s - r), keepdims=False)
            for s in range(NZ)
        ]
    )
    weight_grad = lax.dot_general(
        jnp.concatenate([blocks[s] for s in range(NZ)]),
        cot,
        (((0,), (0,)), ((), ())),
        preferred_element_type=F32,
    )
    weight_grad = weight_grad * float(NR * t) ** (-0.5)
    return output, activation_grad, weight_grad


def solution(mesh):
    grid = Mesh(mesh.devices.reshape(NR, NZ, NX), ("r", "z", "x"))
    spec = P("r", ("z", "x"))
    return jax.shard_map(
        per_device,
        mesh=grid,
        in_specs=(spec,) * 5,
        out_specs=(spec,) * 3,
        check_vma=False,
    )
```

time: 389 us -> 117 us (0.30)
  waiting for transfers between devices: 289 us -> 23.5 us
  starting transfers between devices: 4.41 us -> 41.3 us
  blocking collectives: 47.7 us -> 20.7 us
  between operations: 13.8 us -> 0.92 us
  matrix products: 21 us -> 11.4 us
  Pallas kernels: 0 us -> 8.6 us
    reduce_scatter x1 -> x0, waiting for transfers between devices: 157 us -> none  [per_device(): lax.psum_scatter(partials, 'col', scatter_dimension=1, tiled=True)]
    all_gather x2 -> x0, waiting for transfers between devices: 132 us -> none  [the longest x1 73.1 us: per_device(): act_wide = lax.all_gather(activations, 'col', axis=1, tiled=True)]
    ppermute x0 -> x16, starting transfers between devices: none -> 29.6 us  [move(): return lax.ppermute(value, ('r', 'z', 'x'), pairs)]
    all_gather x1, blocking collectives: 47.7 us -> 20.7 us  [per_device(): cot = lax.all_gather(cotangent, 'r', axis=0, tiled=True)]
    ppermute x0 -> x16, waiting for transfers between devices: none -> 22.9 us  [move(): return lax.ppermute(value, ('r', 'z', 'x'), pairs)]
    dot_general x3 -> x9, matrix products: 21 us -> 11.4 us  [the longest x8 8.12 us: mm(): return jnp.dot(a, b, preferred_element_type=F32)]
    pallas_call x0 -> x3, Pallas kernels: none -> 8.6 us  [the longest x1 4.53 us: grad_parts(): pl.pallas_call(grad_kernel, grid=(NX,), out_shape=(jax.ShapeDtypeStruct((...]
    all_to_all x1 -> x2, starting transfers between devices: 4.29 us -> 11.7 us  [the longest x1 6.03 us: per_device(): lax.all_to_all(parts.reshape(NR * NX, t, n), ('r', 'x'), split_axis=0, co...]
  transfers between devices with their start and end apart: 4 -> 18, of which waited for: 3 -> 8; matrix products, arithmetic and copies ran while one was open for 7% -> 13% of each run, Pallas kernels for 0% -> 6%
where the time goes in v2:
time: 117 us; the launch traced here: 115 us
  starting transfers between devices  41.3 us (35%)
  waiting for transfers between devices  23.5 us (20%)
  blocking collectives  20.7 us (18%)
  matrix products  11.4 us (10%)
  Pallas kernels  8.6 us (7%)
  local copies, waits for them, and re-layouts  5.47 us (5%)
  other arithmetic  3.25 us (3%)
    ppermute x16, starting transfers between devices, move(): return lax.ppermute(value, ('r', 'z', 'x'), pairs)  29.6 us
    ppermute x16, waiting for transfers between devices, move(): return lax.ppermute(value, ('r', 'z', 'x'), pairs)  22.9 us
    all_gather x1, blocking collectives, per_device(): cot = lax.all_gather(cotangent, 'r', axis=0, tiled=True)  20.7 us
    dot_general x8, matrix products, mm(): return jnp.dot(a, b, preferred_element_type=F32)  8.12 us
    all_to_all x1, starting transfers between devices, per_device(): lax.all_to_all(parts.reshape(NR * NX, t, n), ('r', 'x'), split_axis=0, co...  6.03 us
    all_to_all x1, starting transfers between devices, per_device(): lax.all_to_all(shares, 'r', split_axis=0, concat_axis=0, tiled=True)  5.64 us
    pallas_call x1, Pallas kernels, grad_parts(): pl.pallas_call(grad_kernel, grid=(NX,), out_shape=(jax.ShapeDtypeStruct((...  4.53 us
    dot_general x1, matrix products, per_device(): lax.dot_general(jnp.concatenate([blocks[s] for s in range(NZ)]), cot, (((...  3.26 us
  transfers between devices with their start and end apart: 18, of which 8 were waited for; matrix products, arithmetic and copies ran while one was open for 13% of the time, Pallas kernels for 6%

profile of v2, /device:TPU:2, one launch (start us, length us, event | category | flops | bytes accessed | tf_op | source)
XLA Modules:
  0.0 115.1 jit_solution(8130342219158232036)
XLA Ops:
  0.7 0.8 mul.49
  1.4 0.1 copy.10
  1.6 0.9 multiply_convert_fusion
  2.5 0.7 collective-permute-start
  3.2 20.7 %all_gather.3.cot = bf16[1024,384]{1,0:T(8,128)(2,1)S(1)} all-gather(bf16[128,384]{1,0:T(8,128)(2,1)} %param.9), channel_id=1, replica_groups=mesh['r'=8,'z'=8,'x'=4] {'r'}, dimensions={0}, use_global_device_ids=true | all-gather | bytes 884736 | tf_op jit(solution)/shard_map/all_gather | solution.py:154
  23.9 0.1 copy.11.scales
  24.0 1.6 %collective-permute-start.3 = (bf16[128,384]{1,0:T(8,128)(2,1)S(1)}, bf16[128,384]{1,0:T(8,128)(2,1)S(1)}, u32[]{:S(2)}, u32[]{:S(2)}) collective-permute-start(bf16[128,384]{1,0:T(8,128)(2,1)S(1)} %collective-permute-done.refs_0_), channel_id=1, source_target_pairs={{0,1},{1,2},{2,3},{3,0},{4,5},{5,6},{6,7},{7,4},{8,9},{9,10},{10,1... | collective-permute-start | bytes 294920 | tf_op jit(solution)/shard_map/ppermute | solution.py:39
  25.6 1.1 collective-permute-start.2
  26.7 2.2 %collective-permute-start.1 = (bf16[128,384]{1,0:T(8,128)(2,1)S(1)}, bf16[128,384]{1,0:T(8,128)(2,1)S(1)}, u32[]{:S(2)}, u32[]{:S(2)}) collective-permute-start(bf16[128,384]{1,0:T(8,128)(2,1)S(1)} %collective-permute-done.refs_0_), channel_id=1, source_target_pairs={{0,3},{1,0},{2,1},{3,2},{4,7},{5,4},{6,5},{7,6},{8,11},{9,8},{10,9... | collective-permute-start | bytes 294920 | tf_op jit(solution)/shard_map/ppermute | solution.py:39
  28.8 4.5 %shard_map.76 = (bf16[8,4,128,384]{3,2,1,0:T(8,128)(2,1)}, bf16[1536,384]{1,0:T(8,128)(2,1)S(1)}) custom-call(f32[12,3]{1,0:T(8,128)S(1)} %copy.11.scales, bf16[1024,384]{1,0:T(8,128)(2,1)S(1)} %all_gather.3.cot, bf16[1536,384]{1,0:T(8,128)(2,1)S(1)} %copy-done), custom_call_target="tpu_custom_call" | custom-call | flops 1207959552 | bytes 3145728 | tf_op jit(solution)/shard_map/pallas_call | solution.py:72
  33.4 0.6 copy-done.3
  34.1 1.8 %shard_map.77 = bf16[128,1536]{1,0:T(8,128)(2,1)} custom-call(s32[1]{0:T(128)} %bitcast.x, bf16[128,384]{1,0:T(8,128)(2,1)} %copy-done.2, bf16[128,384]{1,0:T(8,128)(2,1)} %copy-done.5, bf16[128,384]{1,0:T(8,128)(2,1)} %copy-done.4, bf16[128,384]{1,0:T(8,128)(2,1)} %copy-done.3), custom_call_target="tpu_custom_call" | custom-call | bytes 786432 | tf_op jit(solution)/shard_map/pallas_call | solution.py:131
  35.9 1.3 %collective-permute-start.5 = (bf16[128,1536]{1,0:T(8,128)(2,1)}, bf16[128,1536]{1,0:T(8,128)(2,1)S(1)}, u32[]{:S(2)}, u32[]{:S(2)}) collective-permute-start(bf16[128,1536]{1,0:T(8,128)(2,1)} %shard_map.77), channel_id=1, source_target_pairs={{0,4},{1,5},{2,6},{3,7},{4,8},{5,9},{6,10},{7,11},{8,12},{9,13},{1... | collective-permute-start | bytes 1179656 | tf_op jit(solution)/shard_map/ppermute | solution.py:39
  37.2 2.0 %collective-permute-start.4 = (bf16[128,1536]{1,0:T(8,128)(2,1)}, bf16[128,1536]{1,0:T(8,128)(2,1)S(1)}, u32[]{:S(2)}, u32[]{:S(2)}) collective-permute-start(bf16[128,1536]{1,0:T(8,128)(2,1)} %shard_map.77), channel_id=1, source_target_pairs={{0,28},{1,29},{2,30},{3,31},{4,0},{5,1},{6,2},{7,3},{8,4},{9,5},{1... | collective-permute-start | bytes 1179656 | tf_op jit(solution)/shard_map/ppermute | solution.py:39
  39.1 6.0 %all-to-all-start.1 = ((bf16[32,128,384]{2,1,0:T(8,128)(2,1)}), bf16[32,128,384]{2,1,0:T(8,128)(2,1)}, u32[]{:S(2)}, u32[]{:S(2)}) async-start(bf16[32,128,384]{2,1,0:T(8,128)(2,1)} %bitcast.96), calls=%async_computation.1 | async-start | bytes 6291456 | tf_op jit(solution)/shard_map/all_to_all | solution.py:160
  45.2 1.0 broadcast_in_dim.28
  46.2 1.0 fusion.1
  47.2 1.4 %collective-permute-done.4 = bf16[128,1536]{1,0:T(8,128)(2,1)S(1)} collective-permute-done((bf16[128,1536]{1,0:T(8,128)(2,1)}, bf16[128,1536]{1,0:T(8,128)(2,1)S(1)}, u32[]{:S(2)}, u32[]{:S(2)}) %collective-permute-start.4) | collective-permute-done | bytes 393248 | tf_op jit(solution)/shard_map/ppermute | solution.py:39
  48.7 2.5 %collective-permute-start.6 = (bf16[128,1536]{1,0:T(8,128)(2,1)S(1)}, bf16[128,1536]{1,0:T(8,128)(2,1)S(1)}, u32[]{:S(2)}, u32[]{:S(2)}) collective-permute-start(bf16[128,1536]{1,0:T(8,128)(2,1)S(1)} %collective-permute-done.4), channel_id=1, source_target_pairs={{0,28},{1,29},{2,30},{3,31},{4,0},{5,1},{6,2},{7,3},{8,4},{9,5},{1... | collective-permute-start | bytes 1179656 | tf_op jit(solution)/shard_map/ppermute | solution.py:39
  51.4 1.0 fusion.3
  52.6 1.0 fusion.5
  53.6 8.3 %collective-permute-done.7 = bf16[128,1536]{1,0:T(8,128)(2,1)S(1)} collective-permute-done((bf16[128,1536]{1,0:T(8,128)(2,1)S(1)}, bf16[128,1536]{1,0:T(8,128)(2,1)S(1)}, u32[]{:S(2)}, u32[]{:S(2)}) %collective-permute-start.7) | collective-permute-done | bytes 393248 | tf_op jit(solution)/shard_map/ppermute | solution.py:39
  61.9 3.2 %collective-permute-start.8 = (bf16[128,1536]{1,0:T(8,128)(2,1)S(1)}, bf16[128,1536]{1,0:T(8,128)(2,1)S(1)}, u32[]{:S(2)}, u32[]{:S(2)}) collective-permute-start(bf16[128,1536]{1,0:T(8,128)(2,1)S(1)} %collective-permute-done.6), channel_id=1, source_target_pairs={{0,28},{1,29},{2,30},{3,31},{4,0},{5,1},{6,2},{7,3},{8,4},{9,5},{1... | collective-permute-start | bytes 1179656 | tf_op jit(solution)/shard_map/ppermute | solution.py:39
  65.2 1.0 fusion.7
  66.2 1.0 fusion.9
  67.2 3.8 %collective-permute-done.8 = bf16[128,1536]{1,0:T(8,128)(2,1)S(1)} collective-permute-done((bf16[128,1536]{1,0:T(8,128)(2,1)S(1)}, bf16[128,1536]{1,0:T(8,128)(2,1)S(1)}, u32[]{:S(2)}, u32[]{:S(2)}) %collective-permute-start.8) | collective-permute-done | bytes 393248 | tf_op jit(solution)/shard_map/ppermute | solution.py:39
  71.0 3.6 %collective-permute-start.10 = (bf16[128,1536]{1,0:T(8,128)(2,1)S(1)}, bf16[128,1536]{1,0:T(8,128)(2,1)S(1)}, u32[]{:S(2)}, u32[]{:S(2)}) collective-permute-start(bf16[128,1536]{1,0:T(8,128)(2,1)S(1)} %collective-permute-done.8), channel_id=1, source_target_pairs={{0,28},{1,29},{2,30},{3,31},{4,0},{5,1},{6,2},{7,3},{8,4},{9,5},{1... | collective-permute-start | bytes 1179656 | tf_op jit(solution)/shard_map/ppermute | solution.py:39
  74.6 1.0 fusion.11
  75.7 1.0 fusion.13
  76.7 3.2 %collective-permute-done.10 = bf16[128,1536]{1,0:T(8,128)(2,1)S(1)} collective-permute-done((bf16[128,1536]{1,0:T(8,128)(2,1)S(1)}, bf16[128,1536]{1,0:T(8,128)(2,1)S(1)}, u32[]{:S(2)}, u32[]{:S(2)}) %collective-permute-start.10) | collective-permute-done | bytes 393248 | tf_op jit(solution)/shard_map/ppermute | solution.py:39
  80.0 1.7 %copy-done.6 = bf16[1024,1536]{1,0:T(8,128)(2,1)} copy-done((bf16[1024,1536]{1,0:T(8,128)(2,1)}, bf16[1024,1536]{1,0:T(8,128)(2,1)S(1)}, u32[]{:S(2)}) %copy-start.6) | copy-done | bytes 3145752
  81.7 1.0 fusion.15
  82.7 0.5 all-to-all-done.1
  83.2 5.6 %all-to-all-start = ((bf16[8,128,384]{2,1,0:T(8,128)(2,1)}), bf16[8,128,384]{2,1,0:T(8,128)(2,1)S(1)}, u32[]{:S(2)}, u32[]{:S(2)}) async-start(bf16[8,128,384]{2,1,0:T(8,128)(2,1)} %fusion.15), calls=%async_computation | async-start | bytes 1572864 | tf_op jit(solution)/shard_map/all_to_all | solution.py:175
  88.9 2.2 %shard_map.78 = f32[8,128,384]{2,1,0:T(8,128)S(1)} custom-call(s32[1]{0:T(128)} %bitcast.10.z, bf16[8,4,128,384]{3,2,1,0:T(8,128)(2,1)} %bitcast.12.parts), custom_call_target="tpu_custom_call" | custom-call | flops 1572864 | bytes 4718592 | tf_op jit(solution)/shard_map/pallas_call | solution.py:106
  91.2 0.1 convert_element_type.75
  91.3 0.7 slice_bitcast_fusion
  92.1 3.8 %collective-permute-start.12 = (bf16[2,128,384]{2,1,0:T(8,128)(2,1)S(1)}, bf16[2,128,384]{2,1,0:T(8,128)(2,1)S(1)}, u32[]{:S(2)}, u32[]{:S(2)}) collective-permute-start(bf16[2,128,384]{2,1,0:T(8,128)(2,1)S(1)} %pad_maximum_fusion.1), channel_id=1, source_target_pairs={{0,28},{1,29},{2,30},{3,31},{4,0},{5,1},{6,2},{7,3},{8,4},{9,5},{1... | collective-permute-start | bytes 589832 | tf_op jit(solution)/shard_map/ppermute | solution.py:39
  95.9 3.5 %collective-permute-start.13 = (bf16[128,384]{1,0:T(8,128)(2,1)}, bf16[128,384]{1,0:T(8,128)(2,1)S(1)}, u32[]{:S(2)}, u32[]{:S(2)}) collective-permute-start(bf16[128,384]{1,0:T(8,128)(2,1)} %get-tuple-element.27), channel_id=1, source_target_pairs={{0,16},{1,17},{2,18},{3,19},{4,20},{5,21},{6,22},{7,23},{8,24},{9,... | collective-permute-start | bytes 294920 | tf_op jit(solution)/shard_map/ppermute | solution.py:39
  99.4 1.9 %collective-permute-done.11 = bf16[2,128,384]{2,1,0:T(8,128)(2,1)S(1)} collective-permute-done((bf16[2,128,384]{2,1,0:T(8,128)(2,1)S(1)}, bf16[2,128,384]{2,1,0:T(8,128)(2,1)S(1)}, u32[]{:S(2)}, u32[]{:S(2)}) %collective-permute-start.11) | collective-permute-done | bytes 196640 | tf_op jit(solution)/shard_map/ppermute | solution.py:39
  101.4 1.9 %collective-permute-done.12 = bf16[2,128,384]{2,1,0:T(8,128)(2,1)S(1)} collective-permute-done((bf16[2,128,384]{2,1,0:T(8,128)(2,1)S(1)}, bf16[2,128,384]{2,1,0:T(8,128)(2,1)S(1)}, u32[]{:S(2)}, u32[]{:S(2)}) %collective-permute-start.12) | collective-permute-done | bytes 196640 | tf_op jit(solution)/shard_map/ppermute | solution.py:39
  103.3 0.7 fusion.23
  104.0 3.1 %collective-permute-start.14 = (bf16[128,384]{1,0:T(8,128)(2,1)}, bf16[128,384]{1,0:T(8,128)(2,1)S(1)}, u32[]{:S(2)}, u32[]{:S(2)}) collective-permute-start(bf16[128,384]{1,0:T(8,128)(2,1)} %get-tuple-element.25), channel_id=1, source_target_pairs={{0,8},{1,9},{2,10},{3,11},{4,12},{5,13},{6,14},{7,15},{8,16},{9,17... | collective-permute-start | bytes 294920 | tf_op jit(solution)/shard_map/ppermute | solution.py:39
  107.1 1.0 collective-permute-start.15
  108.1 3.3 %convolution_multiply_fusion = f32[1536,384]{1,0:T(8,128)} fusion(bf16[1024,1536]{1,0:T(8,128)(2,1)S(1)} %constant_dynamic-update-slice_fusion, bf16[1024,384]{1,0:T(8,128)(2,1)S(1)} %copy-done.9), kind=kOutput, calls=%fused_computation | convolution fusion | flops 1208549376 | bytes 6291456 | tf_op jit(solution)/shard_map/dot_general | solution.py:197
  111.4 0.8 reduce_sum.12
  112.2 2.3 %collective-permute-done.15 = bf16[128,384]{1,0:T(8,128)(2,1)S(1)} collective-permute-done((bf16[128,384]{1,0:T(8,128)(2,1)S(1)}, bf16[128,384]{1,0:T(8,128)(2,1)S(1)}, u32[]{:S(2)}, u32[]{:S(2)}) %collective-permute-start.15) | collective-permute-done | bytes 98336 | tf_op jit(solution)/shard_map/ppermute | solution.py:39
  114.4 0.7 fusion.22
  (53 shorter events, 0.8 us)
Async XLA Ops:
  0.6 23.3 %copy-start.10 = (f32[12,3]{0,1:T(4,128)S(1)}, f32[12,3]{0,1:T(4,128)}, u32[]{:S(2)}) copy-start(f32[12,3]{0,1:T(4,128)} %param.8) | copy-start | bytes 436
  0.6 28.2 %copy-start = (bf16[1536,384]{1,0:T(8,128)(2,1)S(1)}, bf16[1536,384]{1,0:T(8,128)(2,1)}, u32[]{:S(2)}) copy-start(bf16[1536,384]{1,0:T(8,128)(2,1)} %values.1) | copy-start | bytes 3538948
  2.5 21.5 %collective-permute-start = (bf16[128,384]{1,0:T(8,128)(2,1)S(1)}, bf16[128,384]{1,0:T(8,128)(2,1)S(1)}, u32[]{:S(2)}, u32[]{:S(2)}) collective-permute-start(bf16[128,384]{1,0:T(8,128)(2,1)S(1)} %multiply_convert_fusion), channel_id=1, source_target_pairs={{0,0},{1,1},{2,2},{3,3},{4,36},{5,37},{6,38},{7,39},{8,72},{9,73},... | collective-permute-start | bytes 294920 | tf_op jit(solution)/shard_map/ppermute | solution.py:39
  24.0 9.4 %copy-start.2 = (bf16[128,384]{1,0:T(8,128)(2,1)}, bf16[128,384]{1,0:T(8,128)(2,1)S(1)}, u32[]{:S(2)}) copy-start(bf16[128,384]{1,0:T(8,128)(2,1)S(1)} %collective-permute-done.refs_0_) | copy-start | bytes 294916
  24.0 9.4 %collective-permute-start.3 = (bf16[128,384]{1,0:T(8,128)(2,1)S(1)}, bf16[128,384]{1,0:T(8,128)(2,1)S(1)}, u32[]{:S(2)}, u32[]{:S(2)}) collective-permute-start(bf16[128,384]{1,0:T(8,128)(2,1)S(1)} %collective-permute-done.refs_0_), channel_id=1, source_target_pairs={{0,1},{1,2},{2,3},{3,0},{4,5},{5,6},{6,7},{7,4},{8,9},{9,10},{10,1... | collective-permute-start | bytes 294920 | tf_op jit(solution)/shard_map/ppermute | solution.py:39
  25.6 7.8 %collective-permute-start.2 = (bf16[128,384]{1,0:T(8,128)(2,1)S(1)}, bf16[128,384]{1,0:T(8,128)(2,1)S(1)}, u32[]{:S(2)}, u32[]{:S(2)}) collective-permute-start(bf16[128,384]{1,0:T(8,128)(2,1)S(1)} %collective-permute-done.refs_0_), channel_id=1, source_target_pairs={{0,2},{1,3},{2,0},{3,1},{4,6},{5,7},{6,4},{7,5},{8,10},{9,11},{10,... | collective-permute-start | bytes 294920 | tf_op jit(solution)/shard_map/ppermute | solution.py:39
  26.7 6.7 %collective-permute-start.1 = (bf16[128,384]{1,0:T(8,128)(2,1)S(1)}, bf16[128,384]{1,0:T(8,128)(2,1)S(1)}, u32[]{:S(2)}, u32[]{:S(2)}) collective-permute-start(bf16[128,384]{1,0:T(8,128)(2,1)S(1)} %collective-permute-done.refs_0_), channel_id=1, source_target_pairs={{0,3},{1,0},{2,1},{3,2},{4,7},{5,4},{6,5},{7,6},{8,11},{9,8},{10,9... | collective-permute-start | bytes 294920 | tf_op jit(solution)/shard_map/ppermute | solution.py:39
  33.4 0.7 copy-start.3
  33.4 0.7 copy-start.4
  33.4 0.7 copy-start.5
  35.9 15.4 %collective-permute-start.5 = (bf16[128,1536]{1,0:T(8,128)(2,1)}, bf16[128,1536]{1,0:T(8,128)(2,1)S(1)}, u32[]{:S(2)}, u32[]{:S(2)}) collective-permute-start(bf16[128,1536]{1,0:T(8,128)(2,1)} %shard_map.77), channel_id=1, source_target_pairs={{0,4},{1,5},{2,6},{3,7},{4,8},{5,9},{6,10},{7,11},{8,12},{9,13},{1... | collective-permute-start | bytes 1179656 | tf_op jit(solution)/shard_map/ppermute | solution.py:39
  37.2 11.5 %collective-permute-start.4 = (bf16[128,1536]{1,0:T(8,128)(2,1)}, bf16[128,1536]{1,0:T(8,128)(2,1)S(1)}, u32[]{:S(2)}, u32[]{:S(2)}) collective-permute-start(bf16[128,1536]{1,0:T(8,128)(2,1)} %shard_map.77), channel_id=1, source_target_pairs={{0,28},{1,29},{2,30},{3,31},{4,0},{5,1},{6,2},{7,3},{8,4},{9,5},{1... | collective-permute-start | bytes 1179656 | tf_op jit(solution)/shard_map/ppermute | solution.py:39
  39.1 6.0 %copy-start.1 = (bf16[128,1536]{1,0:T(8,128)(2,1)S(1)}, bf16[128,1536]{1,0:T(8,128)(2,1)}, u32[]{:S(2)}) copy-start(bf16[128,1536]{1,0:T(8,128)(2,1)} %shard_map.77) | copy-start | bytes 1179652
  39.1 44.1 %all-to-all-start.1 = ((bf16[32,128,384]{2,1,0:T(8,128)(2,1)}), bf16[32,128,384]{2,1,0:T(8,128)(2,1)}, u32[]{:S(2)}, u32[]{:S(2)}) async-start(bf16[32,128,384]{2,1,0:T(8,128)(2,1)} %bitcast.96), calls=%async_computation.1 | async-start | bytes 6291456 | tf_op jit(solution)/shard_map/all_to_all | solution.py:160
  48.7 13.2 %collective-permute-start.6 = (bf16[128,1536]{1,0:T(8,128)(2,1)S(1)}, bf16[128,1536]{1,0:T(8,128)(2,1)S(1)}, u32[]{:S(2)}, u32[]{:S(2)}) collective-permute-start(bf16[128,1536]{1,0:T(8,128)(2,1)S(1)} %collective-permute-done.4), channel_id=1, source_target_pairs={{0,28},{1,29},{2,30},{3,31},{4,0},{5,1},{6,2},{7,3},{8,4},{9,5},{1... | collective-permute-start | bytes 1179656 | tf_op jit(solution)/shard_map/ppermute | solution.py:39
  51.3 10.6 %collective-permute-start.7 = (bf16[128,1536]{1,0:T(8,128)(2,1)S(1)}, bf16[128,1536]{1,0:T(8,128)(2,1)S(1)}, u32[]{:S(2)}, u32[]{:S(2)}) collective-permute-start(bf16[128,1536]{1,0:T(8,128)(2,1)S(1)} %collective-permute-done.5), channel_id=1, source_target_pairs={{0,4},{1,5},{2,6},{3,7},{4,8},{5,9},{6,10},{7,11},{8,12},{9,13},{1... | collective-permute-start | bytes 1179656 | tf_op jit(solution)/shard_map/ppermute | solution.py:39
  52.5 14.7 %copy-start.8 = (bf16[1024,384]{1,0:T(8,128)(2,1)}, bf16[1024,384]{1,0:T(8,128)(2,1)S(1)}, u32[]{:S(2)}) copy-start(bf16[1024,384]{1,0:T(8,128)(2,1)S(1)} %bitcast_dynamic-update-slice_fusion) | copy-start | bytes 2359300
  61.9 13.7 %collective-permute-start.9 = (bf16[128,1536]{1,0:T(8,128)(2,1)S(1)}, bf16[128,1536]{1,0:T(8,128)(2,1)S(1)}, u32[]{:S(2)}, u32[]{:S(2)}) collective-permute-start(bf16[128,1536]{1,0:T(8,128)(2,1)S(1)} %collective-permute-done.7), channel_id=1, source_target_pairs={{0,4},{1,5},{2,6},{3,7},{4,8},{5,9},{6,10},{7,11},{8,12},{9,13},{1... | collective-permute-start | bytes 1179656 | tf_op jit(solution)/shard_map/ppermute | solution.py:39
  61.9 9.1 %collective-permute-start.8 = (bf16[128,1536]{1,0:T(8,128)(2,1)S(1)}, bf16[128,1536]{1,0:T(8,128)(2,1)S(1)}, u32[]{:S(2)}, u32[]{:S(2)}) collective-permute-start(bf16[128,1536]{1,0:T(8,128)(2,1)S(1)} %collective-permute-done.6), channel_id=1, source_target_pairs={{0,28},{1,29},{2,30},{3,31},{4,0},{5,1},{6,2},{7,3},{8,4},{9,5},{1... | collective-permute-start | bytes 1179656 | tf_op jit(solution)/shard_map/ppermute | solution.py:39
  71.0 8.9 %collective-permute-start.10 = (bf16[128,1536]{1,0:T(8,128)(2,1)S(1)}, bf16[128,1536]{1,0:T(8,128)(2,1)S(1)}, u32[]{:S(2)}, u32[]{:S(2)}) collective-permute-start(bf16[128,1536]{1,0:T(8,128)(2,1)S(1)} %collective-permute-done.8), channel_id=1, source_target_pairs={{0,28},{1,29},{2,30},{3,31},{4,0},{5,1},{6,2},{7,3},{8,4},{9,5},{1... | collective-permute-start | bytes 1179656 | tf_op jit(solution)/shard_map/ppermute | solution.py:39
  80.0 1.7 %copy-start.6 = (bf16[1024,1536]{1,0:T(8,128)(2,1)}, bf16[1024,1536]{1,0:T(8,128)(2,1)S(1)}, u32[]{:S(2)}) copy-start(bf16[1024,1536]{1,0:T(8,128)(2,1)S(1)} %constant_dynamic-update-slice_fusion.1) | copy-start | bytes 9437188
  83.2 28.2 %all-to-all-start = ((bf16[8,128,384]{2,1,0:T(8,128)(2,1)}), bf16[8,128,384]{2,1,0:T(8,128)(2,1)S(1)}, u32[]{:S(2)}, u32[]{:S(2)}) async-start(bf16[8,128,384]{2,1,0:T(8,128)(2,1)} %fusion.15), calls=%async_computation | async-start | bytes 1572864 | tf_op jit(solution)/shard_map/all_to_all | solution.py:175
  91.1 4.8 %copy-start.7 = (bf16[1024,1536]{1,0:T(8,128)(2,1)S(1)}, bf16[1024,1536]{1,0:T(8,128)(2,1)}, u32[]{:S(2)}) copy-start(bf16[1024,1536]{1,0:T(8,128)(2,1)} %copy-done.6) | copy-start | bytes 9437188
  91.3 16.9 %copy-start.9 = (bf16[1024,384]{1,0:T(8,128)(2,1)S(1)}, bf16[1024,384]{1,0:T(8,128)(2,1)}, u32[]{:S(2)}) copy-start(bf16[1024,384]{1,0:T(8,128)(2,1)} %copy-done.8) | copy-start | bytes 2359300
  92.0 9.3 %collective-permute-start.11 = (bf16[2,128,384]{2,1,0:T(8,128)(2,1)S(1)}, bf16[2,128,384]{2,1,0:T(8,128)(2,1)S(1)}, u32[]{:S(2)}, u32[]{:S(2)}) collective-permute-start(bf16[2,128,384]{2,1,0:T(8,128)(2,1)S(1)} %pad_maximum_fusion), channel_id=1, source_target_pairs={{0,4},{1,5},{2,6},{3,7},{4,8},{5,9},{6,10},{7,11},{8,12},{9,13},{1... | collective-permute-start | bytes 589832 | tf_op jit(solution)/shard_map/ppermute | solution.py:39
  92.1 11.2 %collective-permute-start.12 = (bf16[2,128,384]{2,1,0:T(8,128)(2,1)S(1)}, bf16[2,128,384]{2,1,0:T(8,128)(2,1)S(1)}, u32[]{:S(2)}, u32[]{:S(2)}) collective-permute-start(bf16[2,128,384]{2,1,0:T(8,128)(2,1)S(1)} %pad_maximum_fusion.1), channel_id=1, source_target_pairs={{0,28},{1,29},{2,30},{3,31},{4,0},{5,1},{6,2},{7,3},{8,4},{9,5},{1... | collective-permute-start | bytes 589832 | tf_op jit(solution)/shard_map/ppermute | solution.py:39
  95.9 16.2 %collective-permute-start.13 = (bf16[128,384]{1,0:T(8,128)(2,1)}, bf16[128,384]{1,0:T(8,128)(2,1)S(1)}, u32[]{:S(2)}, u32[]{:S(2)}) collective-permute-start(bf16[128,384]{1,0:T(8,128)(2,1)} %get-tuple-element.27), channel_id=1, source_target_pairs={{0,16},{1,17},{2,18},{3,19},{4,20},{5,21},{6,22},{7,23},{8,24},{9,... | collective-permute-start | bytes 294920 | tf_op jit(solution)/shard_map/ppermute | solution.py:39
  104.0 8.2 %collective-permute-start.14 = (bf16[128,384]{1,0:T(8,128)(2,1)}, bf16[128,384]{1,0:T(8,128)(2,1)S(1)}, u32[]{:S(2)}, u32[]{:S(2)}) collective-permute-start(bf16[128,384]{1,0:T(8,128)(2,1)} %get-tuple-element.25), channel_id=1, source_target_pairs={{0,8},{1,9},{2,10},{3,11},{4,12},{5,13},{6,14},{7,15},{8,16},{9,17... | collective-permute-start | bytes 294920 | tf_op jit(solution)/shard_map/ppermute | solution.py:39
  107.1 7.3 %collective-permute-start.15 = (bf16[128,384]{1,0:T(8,128)(2,1)S(1)}, bf16[128,384]{1,0:T(8,128)(2,1)S(1)}, u32[]{:S(2)}, u32[]{:S(2)}) collective-permute-start(bf16[128,384]{1,0:T(8,128)(2,1)S(1)} %get-tuple-element.26), channel_id=1, source_target_pairs={{0,24},{1,25},{2,26},{3,27},{4,28},{5,29},{6,30},{7,31},{8,0},{9,1... | collective-permute-start | bytes 294920 | tf_op jit(solution)/shard_map/ppermute | solution.py:39

commit v3 on v2

v3 whole, which is shorter than its diff:
```python
import jax
import jax.numpy as jnp
from jax import lax
from jax.experimental import pallas as pl
from jax.experimental.pallas import tpu as pltpu
from jax.sharding import Mesh
from jax.sharding import PartitionSpec as P

NR, NC, NY, NZ, NX = 8, 2, 4, 8, 4
BF, F32 = jnp.bfloat16, jnp.float32
BLOCK = 128
VMEM = 16 * 1024 * 1024


def dequantize_rows(values, scales):
    blocks = (
        values.astype(F32).reshape(values.shape[0], scales.shape[1], -1)
        * scales[:, :, None]
    )
    return blocks.reshape(values.shape).astype(BF)


def skew(r):
    return r // NC + r % NC * (NR // NC)


def unskew(d):
    d = d % NZ
    return d % (NR // NC) * NC + d // (NR // NC)


def move(value, where):
    pairs = []
    for r in range(NR):
        for z in range(NZ):
            for x in range(NX):
                r2, z2, x2 = where(r, z, x)
                to = ((r2 % NR) * NZ + z2 % NZ) * NX + x2 % NX
                pairs.append(((r * NZ + z) * NX + x, to))
    return lax.ppermute(value, ("r", "z", "x"), pairs)


def along_x(value, k):
    return move(value, lambda r, z, x: (r, z, x + k))


def along_y(value, k):
    return move(value, lambda r, z, x: (r + NC * k, z, x))


def along_z(value, k):
    return move(value, lambda r, z, x: (r, z + k, x))


def mm(a, b):
    return jnp.dot(a, b, preferred_element_type=F32)


def grad_kernel(place, scales, near, far, values, parts, weight, cot):
    at = pl.program_id(0)
    for i in range(values.shape[0] // BLOCK):
        for j in range(values.shape[1] // BLOCK):
            rows, cols = pl.ds(i * BLOCK, BLOCK), pl.ds(j * BLOCK, BLOCK)
            scale = scales[at * (values.shape[0] // BLOCK) + i, j]
            weight[rows, cols] = (values[rows, cols].astype(F32) * scale).astype(BF)
    half, rows, n = near.shape
    for h, some in enumerate((near, far)):
        part = lax.dot_general(
            some[...].reshape(half * rows, n),
            weight[...],
            (((1,), (1,)), ((), ())),
            preferred_element_type=F32,
        ).astype(BF)
        for i in range(half):
            parts[place[h * half + i], 0] = part[i * rows : (i + 1) * rows]

    @pl.when(at == 0)
    def _():
        for h, some in enumerate((near, far)):
            for i in range(half):
                cot[place[NR + h * half + i]] = some[i]


def grad_parts(place, near, far, values, scales):
    half, rows, n = near.shape
    k = values.shape[0]
    whole = pl.BlockSpec((half, rows, n), lambda i: (0, 0, 0))
    scalars = pl.BlockSpec(memory_space=pltpu.SMEM)
    return pl.pallas_call(
        grad_kernel,
        grid=(NX,),
        out_shape=(
            jax.ShapeDtypeStruct((NR, NX, rows, k // NX), BF),
            jax.ShapeDtypeStruct((k, n), BF),
            jax.ShapeDtypeStruct((NR, rows, n), BF),
        ),
        in_specs=[
            scalars,
            scalars,
            whole,
            whole,
            pl.BlockSpec((k // NX, n), lambda i: (i, 0)),
        ],
        out_specs=(
            pl.BlockSpec((NR, 1, rows, k // NX), lambda i: (0, i, 0, 0)),
            pl.BlockSpec((k // NX, n), lambda i: (i, 0)),
            pl.BlockSpec((NR, rows, n), lambda i: (0, 0, 0)),
        ),
        compiler_params=pltpu.CompilerParams(vmem_limit_bytes=VMEM),
        cost_estimate=pl.CostEstimate(
            flops=4 * half * rows * n * k,
            bytes_accessed=4 * half * rows * k,
            transcendentals=0,
        ),
    )(place, scales, near, far, values)


def sum_kernel(z, parts, ahead, behind, across, kept):
    def of(s):
        at = lax.rem(z[0] + s, NZ)
        total = parts[at, 0].astype(F32)
        for i in range(1, NX):
            total = total + parts[at, i].astype(F32)
        return total

    for i, (near, far) in enumerate(((1, 7), (3, 5))):
        ahead[i] = of(near).astype(BF)
        behind[i] = of(far).astype(BF)
    across[...] = of(4).astype(BF)
    for i, s in enumerate((0, 2, 6)):
        kept[i] = of(s)


def sum_over_x(z, parts):
    _, _, rows, k = parts.shape
    vmem = pl.BlockSpec(memory_space=pltpu.VMEM)
    return pl.pallas_call(
        sum_kernel,
        out_shape=(
            jax.ShapeDtypeStruct((2, rows, k), BF),
            jax.ShapeDtypeStruct((2, rows, k), BF),
            jax.ShapeDtypeStruct((rows, k), BF),
            jax.ShapeDtypeStruct((3, rows, k), F32),
        ),
        in_specs=[pl.BlockSpec(memory_space=pltpu.SMEM), vmem],
        out_specs=(vmem,) * 4,
        compiler_params=pltpu.CompilerParams(vmem_limit_bytes=VMEM),
        cost_estimate=pl.CostEstimate(
            flops=NZ * NX * rows * k, bytes_accessed=12 * NZ * rows * k, transcendentals=0
        ),
    )(z.reshape(1), parts)


def assemble_kernel(x, *refs):
    parts, out = refs[:NX], refs[NX]
    n = parts[0].shape[1]
    for off in range(NX):
        at = pl.multiple_of(lax.rem(x[0] + off, NX) * n, 128)
        out[:, pl.ds(at, n)] = parts[off][...]


def assemble(x, parts):
    t, n = parts[0].shape
    return pl.pallas_call(
        assemble_kernel,
        out_shape=jax.ShapeDtypeStruct((t, NX * n), BF),
        in_specs=[pl.BlockSpec(memory_space=pltpu.SMEM)]
        + [pl.BlockSpec(memory_space=pltpu.VMEM)] * NX,
        out_specs=pl.BlockSpec(memory_space=pltpu.VMEM),
        cost_estimate=pl.CostEstimate(
            flops=0, bytes_accessed=4 * t * NX * n, transcendentals=0
        ),
    )(x.reshape(1), *parts)


def together(*values):
    return lax.optimization_barrier(values)


def per_device(act_values, act_scales, weight_values, weight_scales, cotangent):
    r, z, x = (lax.axis_index(a) for a in ("r", "z", "x"))
    t, n = cotangent.shape

    act = dequantize_rows(act_values, act_scales)
    act, cotangent = together(act, cotangent)
    here = move(act, lambda r, z, x: (z, z + skew(r), x))

    turns = (0, 1, -1, 2)
    near = jnp.stack([along_y(cotangent, -k) if k else cotangent for k in turns])
    near, here = together(near, here)
    far = move(near, lambda r, z, x: (r ^ 1, z, x))
    rows = [(r + NC * k) % NR ^ other for other in (0, 1) for k in turns]
    place = jnp.stack(rows + [(r + skew(row) - z) % NZ for row in rows])

    sides = [along_x(here, -1), along_x(here, 2), along_x(here, 1)]
    parts, weight, cot = grad_parts(place, near, far, weight_values, weight_scales)
    parts, *sides = together(parts, *sides)
    parts = lax.all_to_all(
        parts.reshape(NR * NX, t, n), ("r", "x"), split_axis=0, concat_axis=0, tiled=True
    )

    blocks = {0: assemble(x, [here, *sides])}
    for s in range(1, NZ // 2 + 1):
        blocks[s] = along_z(blocks[s - 1], -1)
        if s < NZ // 2:
            blocks[NZ - s] = along_z(blocks[(NZ - s + 1) % NZ], 1)
    shares = jnp.zeros((NR, t, n), BF)
    for s in (0, 1, 7, 2, 6, 3, 5, 4):
        part = mm(blocks[s], weight).astype(BF)
        row = unskew(z + s - r)
        at = (row // NC - r // NC) % NY + (row % NC ^ r % NC) * NY
        shares = lax.dynamic_update_slice(shares, part[None], (at, 0, 0))
    both = move(shares[NY:], lambda r, z, x: (r ^ 1, z, x)).astype(F32)
    both = shares[:NY].astype(F32) + both

    ahead, behind, across, kept = sum_over_x(z, parts.reshape(NZ, NX, t, n))
    up, down, across = along_z(ahead, 1), along_z(behind, -1), along_z(across, 4)
    up2 = along_z((kept[1] + up[1].astype(F32)).astype(BF), 2)
    down2 = along_z((kept[2] + down[1].astype(F32)).astype(BF), -2)
    total = kept[0] + up[0].astype(F32) + down[0].astype(F32) + across.astype(F32)
    activation_grad = (total + up2.astype(F32) + down2.astype(F32)).astype(BF)

    parts = [along_y(both[k].astype(BF), k) for k in range(1, NY)]
    output = (both[0] + sum(part.astype(F32) for part in parts)).astype(BF)

    cot = cot.reshape(NZ, t, n)

    def grad_of(some):
        return lax.dot_general(
            jnp.concatenate([blocks[s] for s in some]),
            jnp.concatenate([cot[s] for s in some]),
            (((0,), (0,)), ((), ())),
            preferred_element_type=F32,
        )

    first = (0, 1, 7, 2, 6, 3, 5)
    for s, block in zip(first, together(*(blocks[s] for s in first))):
        blocks[s] = block
    weight_grad = grad_of(first)
    weight_grad, blocks[4] = together(weight_grad, blocks[4])
    weight_grad = (weight_grad + grad_of((4,))) * float(NR * t) ** (-0.5)
    return output, activation_grad, weight_grad


def solution(mesh):
    grid = Mesh(mesh.devices.reshape(NR, NZ, NX), ("r", "z", "x"))
    spec = P("r", ("z", "x"))
    return jax.shard_map(
        per_device,
        mesh=grid,
        in_specs=(spec,) * 5,
        out_specs=(spec,) * 3,
        check_vma=False,
    )
```

time: 117 us -> 111 us (0.949)
  blocking collectives: 20.7 us -> 0 us
  starting transfers between devices: 41.3 us -> 58.8 us
  matrix products: 11.4 us -> 5.35 us
  waiting for transfers between devices: 23.5 us -> 26.9 us
  other arithmetic: 3.25 us -> 5.09 us
    ppermute x16 -> x24, starting transfers between devices: 29.6 us -> 52.9 us  [move(): return lax.ppermute(value, ('r', 'z', 'x'), pairs)]
    all_gather x1 -> x0, blocking collectives: 20.7 us -> none  [per_device(): cot = lax.all_gather(cotangent, 'r', axis=0, tiled=True)]
    all_to_all x1 -> x0, starting transfers between devices: 5.64 us -> none  [per_device(): lax.all_to_all(shares, 'r', split_axis=0, concat_axis=0, tiled=True)]
    dot_general x8, matrix products: 8.12 us -> 3.1 us  [mm(): return jnp.dot(a, b, preferred_element_type=F32)]
    ppermute x16 -> x24, waiting for transfers between devices: 22.9 us -> 25.4 us  [move(): return lax.ppermute(value, ('r', 'z', 'x'), pairs)]
    mul x0 -> x1, other arithmetic: none -> 1.65 us  [per_device(): weight_grad = (weight_grad + grad_of((4,))) * float(NR * t) ** (-0.5)]
    dot_general x1 -> x2, matrix products: 3.26 us -> 2.25 us  [grad_of(): lax.dot_general(jnp.concatenate([blocks[s] for s in some]), jnp.concatena...]
    unnamed x37 -> x25, local copies, waits for them, and re-layouts: 2.84 us -> 3.74 us
  transfers between devices with their start and end apart: 18 -> 25, of which waited for: 8 -> 9; matrix products, arithmetic and copies ran while one was open for 13% -> 9% of each run, Pallas kernels for 6% -> 4%
where the time goes in v3:
time: 111 us; the launch traced here: 110 us
  starting transfers between devices  58.8 us (53%)
  waiting for transfers between devices  26.9 us (24%)
  Pallas kernels  7.95 us (7%)
  matrix products  5.35 us (5%)
  other arithmetic  5.09 us (5%)
  local copies, waits for them, and re-layouts  4.95 us (4%)
    ppermute x24, starting transfers between devices, move(): return lax.ppermute(value, ('r', 'z', 'x'), pairs)  52.9 us
    ppermute x24, waiting for transfers between devices, move(): return lax.ppermute(value, ('r', 'z', 'x'), pairs)  25.4 us
    all_to_all x1, starting transfers between devices, per_device(): lax.all_to_all(parts.reshape(NR * NX, t, n), ('r', 'x'), split_axis=0, co...  5.97 us
    pallas_call x1, Pallas kernels, grad_parts(): pl.pallas_call(grad_kernel, grid=(NX,), out_shape=(jax.ShapeDtypeStruct((...  3.85 us
    unnamed x25, local copies, waits for them, and re-layouts  3.74 us
    dot_general x8, matrix products, mm(): return jnp.dot(a, b, preferred_element_type=F32)  3.1 us
    pallas_call x1, Pallas kernels, sum_over_x(): pl.pallas_call(sum_kernel, out_shape=(jax.ShapeDtypeStruct((2, rows, k),...  2.27 us
    dot_general x2, matrix products, grad_of(): lax.dot_general(jnp.concatenate([blocks[s] for s in some]), jnp.concatena...  2.25 us
  transfers between devices with their start and end apart: 25, of which 9 were waited for; matrix products, arithmetic and copies ran while one was open for 9% of the time, Pallas kernels for 4%

profile of v3, /device:TPU:2, one launch (start us, length us, event | category | flops | bytes accessed | tf_op | source)
XLA Modules:
  0.0 110.0 jit_solution(18333412771588098941)
XLA Ops:
  0.7 0.8 mul.89
  1.6 0.9 multiply_convert_fusion
  2.5 3.3 %collective-permute-start.2 = (bf16[128,384]{1,0:T(8,128)(2,1)}, bf16[128,384]{1,0:T(8,128)(2,1)S(1)}, u32[]{:S(2)}, u32[]{:S(2)}) collective-permute-start(bf16[128,384]{1,0:T(8,128)(2,1)} %param.9), channel_id=1, source_target_pairs={{0,128},{1,129},{2,130},{3,131},{4,132},{5,133},{6,134},{7,135},{8... | collective-permute-start | bytes 294920 | tf_op jit(solution)/shard_map/ppermute | solution.py:40
  5.8 0.7 collective-permute-start.1
  6.5 2.6 %collective-permute-start = (bf16[128,384]{1,0:T(8,128)(2,1)}, bf16[128,384]{1,0:T(8,128)(2,1)S(1)}, u32[]{:S(2)}, u32[]{:S(2)}) collective-permute-start(bf16[128,384]{1,0:T(8,128)(2,1)} %param.9), channel_id=1, source_target_pairs={{0,192},{1,193},{2,194},{3,195},{4,196},{5,197},{6,198},{7,199},{8... | collective-permute-start | bytes 294920 | tf_op jit(solution)/shard_map/ppermute | solution.py:40
  9.0 1.3 %collective-permute-start.3 = (bf16[128,384]{1,0:T(8,128)(2,1)S(1)}, bf16[128,384]{1,0:T(8,128)(2,1)}, u32[]{:S(2)}, u32[]{:S(2)}) collective-permute-start(bf16[128,384]{1,0:T(8,128)(2,1)S(1)} %multiply_convert_fusion), channel_id=1, source_target_pairs={{0,0},{1,1},{2,2},{3,3},{4,36},{5,37},{6,38},{7,39},{8,72},{9,73},... | collective-permute-start | bytes 294920 | tf_op jit(solution)/shard_map/ppermute | solution.py:40
  10.3 1.5 %collective-permute-done.1 = bf16[128,384]{1,0:T(8,128)(2,1)S(1)} collective-permute-done((bf16[128,384]{1,0:T(8,128)(2,1)}, bf16[128,384]{1,0:T(8,128)(2,1)S(1)}, u32[]{:S(2)}, u32[]{:S(2)}) %collective-permute-start.1) | collective-permute-done | bytes 98336 | tf_op jit(solution)/shard_map/ppermute | solution.py:40
  11.8 1.0 pad_maximum_fusion.near
  12.8 7.4 %collective-permute-start.4 = (bf16[4,128,384]{2,1,0:T(8,128)(2,1)S(1)}, bf16[4,128,384]{2,1,0:T(8,128)(2,1)S(1)}, u32[]{:S(2)}, u32[]{:S(2)}) collective-permute-start(bf16[4,128,384]{2,1,0:T(8,128)(2,1)S(1)} %pad_maximum_fusion.near), channel_id=1, source_target_pairs={{0,32},{1,33},{2,34},{3,35},{4,36},{5,37},{6,38},{7,39},{8,40},{9,... | collective-permute-start | bytes 1179656 | tf_op jit(solution)/shard_map/ppermute | solution.py:40
  20.4 1.6 %collective-permute-start.7 = (bf16[128,384]{1,0:T(8,128)(2,1)}, bf16[128,384]{1,0:T(8,128)(2,1)}, u32[]{:S(2)}, u32[]{:S(2)}) collective-permute-start(bf16[128,384]{1,0:T(8,128)(2,1)} %collective-permute-done.3.refs_0_), channel_id=1, source_target_pairs={{0,1},{1,2},{2,3},{3,0},{4,5},{5,6},{6,7},{7,4},{8,9},{9,10},{10,1... | collective-permute-start | bytes 294920 | tf_op jit(solution)/shard_map/ppermute | solution.py:40
  22.0 1.2 %collective-permute-start.6 = (bf16[128,384]{1,0:T(8,128)(2,1)}, bf16[128,384]{1,0:T(8,128)(2,1)}, u32[]{:S(2)}, u32[]{:S(2)}) collective-permute-start(bf16[128,384]{1,0:T(8,128)(2,1)} %collective-permute-done.3.refs_0_), channel_id=1, source_target_pairs={{0,2},{1,3},{2,0},{3,1},{4,6},{5,7},{6,4},{7,5},{8,10},{9,11},{10,... | collective-permute-start | bytes 294920 | tf_op jit(solution)/shard_map/ppermute | solution.py:40
  23.3 2.0 %collective-permute-start.5 = (bf16[128,384]{1,0:T(8,128)(2,1)}, bf16[128,384]{1,0:T(8,128)(2,1)}, u32[]{:S(2)}, u32[]{:S(2)}) collective-permute-start(bf16[128,384]{1,0:T(8,128)(2,1)} %collective-permute-done.3.refs_0_), channel_id=1, source_target_pairs={{0,3},{1,0},{2,1},{3,2},{4,7},{5,4},{6,5},{7,6},{8,11},{9,8},{10,9... | collective-permute-start | bytes 294920 | tf_op jit(solution)/shard_map/ppermute | solution.py:40
  25.3 0.7 copy-done.2
  26.1 1.0 copy-done.3
  27.0 3.9 %shard_map.76 = (bf16[8,4,128,384]{3,2,1,0:T(8,128)(2,1)S(1)}, bf16[1536,384]{1,0:T(8,128)(2,1)S(1)}, bf16[8,128,384]{2,1,0:T(8,128)(2,1)S(1)}) custom-call(s32[16]{0:T(128)S(1)} %stack.87.place, f32[12,3]{1,0:T(8,128)S(1)} %copy.11.scales, bf16[4,128,384]{2,1,0:T(8,128)(2,1)S(1)} %pad_maximum_fusion.near, bf16[4,128,384]{2,1,0:T(8,128)(2,1)S(1)} %copy-done.3, ...), custom_call_target="tpu_custom_call" | custom-call | flops 1207959552 | bytes 3145728 | tf_op jit(solution)/shard_map/pallas_call | solution.py:89
  30.9 1.6 %copy-done = bf16[8,4,128,384]{3,2,1,0:T(8,128)(2,1)} copy-done((bf16[8,4,128,384]{3,2,1,0:T(8,128)(2,1)}, bf16[8,4,128,384]{3,2,1,0:T(8,128)(2,1)S(1)}, u32[]{:S(2)}) %copy-start) | copy-done | bytes 3145752
  32.6 1.8 %shard_map.77 = bf16[128,1536]{1,0:T(8,128)(2,1)} custom-call(s32[1]{0:T(128)} %bitcast.x, bf16[128,384]{1,0:T(8,128)(2,1)} %collective-permute-done.3.refs_0_, bf16[128,384]{1,0:T(8,128)(2,1)} %collective-permute-done.5.refs_1_, bf16[128,384]{1,0:T(8,128)(2,1)} %collective-permute-done.6.refs_2_, bf16[128,384]{1,0:T(8,128)(2,1)} %collective-permute-done.7.refs_3_), custom_call_target="tpu_custom_call" | custom-call | bytes 786432 | tf_op jit(solution)/shard_map/pallas_call | solution.py:164
  34.4 4.8 %collective-permute-start.8 = (bf16[128,1536]{1,0:T(8,128)(2,1)}, bf16[128,1536]{1,0:T(8,128)(2,1)S(1)}, u32[]{:S(2)}, u32[]{:S(2)}) collective-permute-start(bf16[128,1536]{1,0:T(8,128)(2,1)} %shard_map.77), channel_id=1, source_target_pairs={{0,28},{1,29},{2,30},{3,31},{4,0},{5,1},{6,2},{7,3},{8,4},{9,5},{1... | collective-permute-start | bytes 1179656 | tf_op jit(solution)/shard_map/ppermute | solution.py:40
  39.2 6.0 %all-to-all-start = ((bf16[32,128,384]{2,1,0:T(8,128)(2,1)}), bf16[32,128,384]{2,1,0:T(8,128)(2,1)}, u32[]{:S(2)}, u32[]{:S(2)}) async-start(bf16[32,128,384]{2,1,0:T(8,128)(2,1)} %bitcast.117), calls=%async_computation | async-start | bytes 6291456 | tf_op jit(solution)/shard_map/all_to_all | solution.py:198
  45.5 0.4 fusion.1
  45.9 2.5 %collective-permute-done.9 = bf16[128,1536]{1,0:T(8,128)(2,1)S(1)} collective-permute-done((bf16[128,1536]{1,0:T(8,128)(2,1)}, bf16[128,1536]{1,0:T(8,128)(2,1)S(1)}, u32[]{:S(2)}, u32[]{:S(2)}) %collective-permute-start.9) | collective-permute-done | bytes 393248 | tf_op jit(solution)/shard_map/ppermute | solution.py:40
  48.4 3.2 %collective-permute-start.10 = (bf16[128,1536]{1,0:T(8,128)(2,1)S(1)}, bf16[128,1536]{1,0:T(8,128)(2,1)S(1)}, u32[]{:S(2)}, u32[]{:S(2)}) collective-permute-start(bf16[128,1536]{1,0:T(8,128)(2,1)S(1)} %collective-permute-done.8), channel_id=1, source_target_pairs={{0,28},{1,29},{2,30},{3,31},{4,0},{5,1},{6,2},{7,3},{8,4},{9,5},{1... | collective-permute-start | bytes 1179656 | tf_op jit(solution)/shard_map/ppermute | solution.py:40
  52.0 0.4 fusion.5
  52.4 7.3 %collective-permute-done.11 = bf16[128,1536]{1,0:T(8,128)(2,1)S(1)} collective-permute-done((bf16[128,1536]{1,0:T(8,128)(2,1)S(1)}, bf16[128,1536]{1,0:T(8,128)(2,1)S(1)}, u32[]{:S(2)}, u32[]{:S(2)}) %collective-permute-start.11) | collective-permute-done | bytes 393248 | tf_op jit(solution)/shard_map/ppermute | solution.py:40
  59.7 3.2 %collective-permute-start.12 = (bf16[128,1536]{1,0:T(8,128)(2,1)S(1)}, bf16[128,1536]{1,0:T(8,128)(2,1)S(1)}, u32[]{:S(2)}, u32[]{:S(2)}) collective-permute-start(bf16[128,1536]{1,0:T(8,128)(2,1)S(1)} %collective-permute-done.10), channel_id=1, source_target_pairs={{0,28},{1,29},{2,30},{3,31},{4,0},{5,1},{6,2},{7,3},{8,4},{9,5},{1... | collective-permute-start | bytes 1179656 | tf_op jit(solution)/shard_map/ppermute | solution.py:40
  62.9 0.4 fusion.7
  63.3 0.4 fusion.9
  63.7 6.5 %collective-permute-done.13 = bf16[128,1536]{1,0:T(8,128)(2,1)S(1)} collective-permute-done((bf16[128,1536]{1,0:T(8,128)(2,1)S(1)}, bf16[128,1536]{1,0:T(8,128)(2,1)S(1)}, u32[]{:S(2)}, u32[]{:S(2)}) %collective-permute-start.13) | collective-permute-done | bytes 393248 | tf_op jit(solution)/shard_map/ppermute | solution.py:40
  70.3 3.0 %collective-permute-start.14 = (bf16[128,1536]{1,0:T(8,128)(2,1)S(1)}, bf16[128,1536]{1,0:T(8,128)(2,1)S(1)}, u32[]{:S(2)}, u32[]{:S(2)}) collective-permute-start(bf16[128,1536]{1,0:T(8,128)(2,1)S(1)} %collective-permute-done.12), channel_id=1, source_target_pairs={{0,28},{1,29},{2,30},{3,31},{4,0},{5,1},{6,2},{7,3},{8,4},{9,5},{1... | collective-permute-start | bytes 1179656 | tf_op jit(solution)/shard_map/ppermute | solution.py:40
  73.4 0.4 fusion.11
  73.8 0.4 fusion.13
  74.3 1.8 %fusion.27 = f32[1536,384]{1,0:T(8,128)S(1)} fusion(bf16[896,1536]{1,0:T(8,128)(2,1)S(1)} %constant_dynamic-update-slice_fusion, bf16[896,384]{1,0:T(8,128)(2,1)S(1)} %bitcast_dynamic-update-slice_fusion), kind=kOutput, calls=%fused_computation.60 | convolution fusion | flops 1056964608 | bytes 5799936 | tf_op jit(solution)/shard_map/dot_general | solution.py:229
  76.0 3.0 %collective-permute-done.14 = bf16[128,1536]{1,0:T(8,128)(2,1)S(1)} collective-permute-done((bf16[128,1536]{1,0:T(8,128)(2,1)S(1)}, bf16[128,1536]{1,0:T(8,128)(2,1)S(1)}, u32[]{:S(2)}, u32[]{:S(2)}) %collective-permute-start.14) | collective-permute-done | bytes 393248 | tf_op jit(solution)/shard_map/ppermute | solution.py:40
  79.1 0.4 fusion.15
  79.6 0.5 fusion.23
  80.1 1.6 %add_multiply_fusion = f32[1536,384]{1,0:T(8,128)} fusion(f32[1536,384]{1,0:T(8,128)S(1)} %fusion.27, f32[1536,384]{1,0:T(8,128)S(1)} %fusion.23), kind=kLoop, calls=%fused_computation | loop fusion | flops 1179648 | bytes 7077888 | tf_op jit(solution)/shard_map/mul | solution.py:241
  81.9 1.4 %all-to-all-done = bf16[32,128,384]{2,1,0:T(8,128)(2,1)} async-done(((bf16[32,128,384]{2,1,0:T(8,128)(2,1)}), bf16[32,128,384]{2,1,0:T(8,128)(2,1)}, u32[]{:S(2)}, u32[]{:S(2)}) %all-to-all-start) | async-done | bytes 3145760 | tf_op jit(solution)/shard_map/all_to_all | solution.py:198
  83.3 2.3 %shard_map.78 = (bf16[2,128,384]{2,1,0:T(8,128)(2,1)S(1)}, bf16[2,128,384]{2,1,0:T(8,128)(2,1)S(1)}, bf16[128,384]{1,0:T(8,128)(2,1)S(1)}, f32[3,128,384]{2,1,0:T(8,128)S(1)}) custom-call(s32[1]{0:T(128)} %bitcast.34.z, bf16[8,4,128,384]{3,2,1,0:T(8,128)(2,1)} %bitcast.36.parts), custom_call_target="tpu_custom_call" | custom-call | flops 1572864 | bytes 4718592 | tf_op jit(solution)/shard_map/pallas_call | solution.py:137
  85.7 3.2 %collective-permute-start.20 = (bf16[2,128,384]{2,1,0:T(8,128)(2,1)S(1)}, bf16[2,128,384]{2,1,0:T(8,128)(2,1)S(1)}, u32[]{:S(2)}, u32[]{:S(2)}) collective-permute-start(bf16[2,128,384]{2,1,0:T(8,128)(2,1)S(1)} %get-tuple-element.39), channel_id=1, source_target_pairs={{0,28},{1,29},{2,30},{3,31},{4,0},{5,1},{6,2},{7,3},{8,4},{9,5},{1... | collective-permute-start | bytes 589832 | tf_op jit(solution)/shard_map/ppermute | solution.py:40
  89.0 1.5 %collective-permute-start.16 = (bf16[128,384]{1,0:T(8,128)(2,1)S(1)}, bf16[128,384]{1,0:T(8,128)(2,1)S(1)}, u32[]{:S(2)}, u32[]{:S(2)}) collective-permute-start(bf16[128,384]{1,0:T(8,128)(2,1)S(1)} %get-tuple-element.55), channel_id=1, source_target_pairs={{0,64},{1,65},{2,66},{3,67},{4,68},{5,69},{6,70},{7,71},{8,72},{9,... | collective-permute-start | bytes 294920 | tf_op jit(solution)/shard_map/ppermute | solution.py:40
  90.4 1.9 %collective-permute-start.18 = (bf16[128,384]{1,0:T(8,128)(2,1)S(1)}, bf16[128,384]{1,0:T(8,128)(2,1)S(1)}, u32[]{:S(2)}, u32[]{:S(2)}) collective-permute-start(bf16[128,384]{1,0:T(8,128)(2,1)S(1)} %get-tuple-element.56), channel_id=1, source_target_pairs={{0,192},{1,193},{2,194},{3,195},{4,196},{5,197},{6,198},{7,199},{8... | collective-permute-start | bytes 294920 | tf_op jit(solution)/shard_map/ppermute | solution.py:40
  92.3 1.7 %collective-permute-start.17 = (bf16[128,384]{1,0:T(8,128)(2,1)S(1)}, bf16[128,384]{1,0:T(8,128)(2,1)S(1)}, u32[]{:S(2)}, u32[]{:S(2)}) collective-permute-start(bf16[128,384]{1,0:T(8,128)(2,1)S(1)} %get-tuple-element.57), channel_id=1, source_target_pairs={{0,128},{1,129},{2,130},{3,131},{4,132},{5,133},{6,134},{7,135},{8... | collective-permute-start | bytes 294920 | tf_op jit(solution)/shard_map/ppermute | solution.py:40
  94.3 5.8 %collective-permute-start.21 = (bf16[128,384]{1,0:T(8,128)(2,1)S(1)}, bf16[128,384]{1,0:T(8,128)(2,1)S(1)}, u32[]{:S(2)}, u32[]{:S(2)}) collective-permute-start(bf16[128,384]{1,0:T(8,128)(2,1)S(1)} %get-tuple-element.40), channel_id=1, source_target_pairs={{0,16},{1,17},{2,18},{3,19},{4,20},{5,21},{6,22},{7,23},{8,24},{9,... | collective-permute-start | bytes 294920 | tf_op jit(solution)/shard_map/ppermute | solution.py:40
  100.2 4.1 %collective-permute-start.23 = (bf16[128,384]{1,0:T(8,128)(2,1)S(1)}, bf16[128,384]{1,0:T(8,128)(2,1)S(1)}, u32[]{:S(2)}, u32[]{:S(2)}) collective-permute-start(bf16[128,384]{1,0:T(8,128)(2,1)S(1)} %get-tuple-element.54), channel_id=1, source_target_pairs={{0,24},{1,25},{2,26},{3,27},{4,28},{5,29},{6,30},{7,31},{8,0},{9,1... | collective-permute-start | bytes 294920 | tf_op jit(solution)/shard_map/ppermute | solution.py:40
  104.4 0.7 fusion.17
  105.1 1.9 %collective-permute-done.21 = bf16[128,384]{1,0:T(8,128)(2,1)S(1)} collective-permute-done((bf16[128,384]{1,0:T(8,128)(2,1)S(1)}, bf16[128,384]{1,0:T(8,128)(2,1)S(1)}, u32[]{:S(2)}, u32[]{:S(2)}) %collective-permute-start.21) | collective-permute-done | bytes 98336 | tf_op jit(solution)/shard_map/ppermute | solution.py:40
  107.0 2.3 %collective-permute-done.22 = bf16[128,384]{1,0:T(8,128)(2,1)S(1)} collective-permute-done((bf16[128,384]{1,0:T(8,128)(2,1)S(1)}, bf16[128,384]{1,0:T(8,128)(2,1)S(1)}, u32[]{:S(2)}, u32[]{:S(2)}) %collective-permute-start.22) | collective-permute-done | bytes 98336 | tf_op jit(solution)/shard_map/ppermute | solution.py:40
  109.3 0.7 fusion.20
  (55 shorter events, 1.9 us)
Async XLA Ops:
  0.6 19.6 %copy-start.5 = (f32[12,3]{0,1:T(4,128)S(1)}, f32[12,3]{0,1:T(4,128)}, u32[]{:S(2)}) copy-start(f32[12,3]{0,1:T(4,128)} %param.8) | copy-start | bytes 436
  0.6 25.4 %copy-start.1 = (bf16[1536,384]{1,0:T(8,128)(2,1)S(1)}, bf16[1536,384]{1,0:T(8,128)(2,1)}, u32[]{:S(2)}) copy-start(bf16[1536,384]{1,0:T(8,128)(2,1)} %values.1) | copy-start | bytes 3538948
  2.5 7.8 %collective-permute-start.2 = (bf16[128,384]{1,0:T(8,128)(2,1)}, bf16[128,384]{1,0:T(8,128)(2,1)S(1)}, u32[]{:S(2)}, u32[]{:S(2)}) collective-permute-start(bf16[128,384]{1,0:T(8,128)(2,1)} %param.9), channel_id=1, source_target_pairs={{0,128},{1,129},{2,130},{3,131},{4,132},{5,133},{6,134},{7,135},{8... | collective-permute-start | bytes 294920 | tf_op jit(solution)/shard_map/ppermute | solution.py:40
  5.8 6.0 %collective-permute-start.1 = (bf16[128,384]{1,0:T(8,128)(2,1)}, bf16[128,384]{1,0:T(8,128)(2,1)S(1)}, u32[]{:S(2)}, u32[]{:S(2)}) collective-permute-start(bf16[128,384]{1,0:T(8,128)(2,1)} %param.9), channel_id=1, source_target_pairs={{0,64},{1,65},{2,66},{3,67},{4,68},{5,69},{6,70},{7,71},{8,72},{9,... | collective-permute-start | bytes 294920 | tf_op jit(solution)/shard_map/ppermute | solution.py:40
  6.5 5.4 %collective-permute-start = (bf16[128,384]{1,0:T(8,128)(2,1)}, bf16[128,384]{1,0:T(8,128)(2,1)S(1)}, u32[]{:S(2)}, u32[]{:S(2)}) collective-permute-start(bf16[128,384]{1,0:T(8,128)(2,1)} %param.9), channel_id=1, source_target_pairs={{0,192},{1,193},{2,194},{3,195},{4,196},{5,197},{6,198},{7,199},{8... | collective-permute-start | bytes 294920 | tf_op jit(solution)/shard_map/ppermute | solution.py:40
  9.0 3.8 %collective-permute-start.3 = (bf16[128,384]{1,0:T(8,128)(2,1)S(1)}, bf16[128,384]{1,0:T(8,128)(2,1)}, u32[]{:S(2)}, u32[]{:S(2)}) collective-permute-start(bf16[128,384]{1,0:T(8,128)(2,1)S(1)} %multiply_convert_fusion), channel_id=1, source_target_pairs={{0,0},{1,1},{2,2},{3,3},{4,36},{5,37},{6,38},{7,39},{8,72},{9,73},... | collective-permute-start | bytes 294920 | tf_op jit(solution)/shard_map/ppermute | solution.py:40
  12.8 12.5 %collective-permute-start.4 = (bf16[4,128,384]{2,1,0:T(8,128)(2,1)S(1)}, bf16[4,128,384]{2,1,0:T(8,128)(2,1)S(1)}, u32[]{:S(2)}, u32[]{:S(2)}) collective-permute-start(bf16[4,128,384]{2,1,0:T(8,128)(2,1)S(1)} %pad_maximum_fusion.near), channel_id=1, source_target_pairs={{0,32},{1,33},{2,34},{3,35},{4,36},{5,37},{6,38},{7,39},{8,40},{9,... | collective-permute-start | bytes 1179656 | tf_op jit(solution)/shard_map/ppermute | solution.py:40
  20.4 12.1 %collective-permute-start.7 = (bf16[128,384]{1,0:T(8,128)(2,1)}, bf16[128,384]{1,0:T(8,128)(2,1)}, u32[]{:S(2)}, u32[]{:S(2)}) collective-permute-start(bf16[128,384]{1,0:T(8,128)(2,1)} %collective-permute-done.3.refs_0_), channel_id=1, source_target_pairs={{0,1},{1,2},{2,3},{3,0},{4,5},{5,6},{6,7},{7,4},{8,9},{9,10},{10,1... | collective-permute-start | bytes 294920 | tf_op jit(solution)/shard_map/ppermute | solution.py:40
  22.0 10.5 %collective-permute-start.6 = (bf16[128,384]{1,0:T(8,128)(2,1)}, bf16[128,384]{1,0:T(8,128)(2,1)}, u32[]{:S(2)}, u32[]{:S(2)}) collective-permute-start(bf16[128,384]{1,0:T(8,128)(2,1)} %collective-permute-done.3.refs_0_), channel_id=1, source_target_pairs={{0,2},{1,3},{2,0},{3,1},{4,6},{5,7},{6,4},{7,5},{8,10},{9,11},{10,... | collective-permute-start | bytes 294920 | tf_op jit(solution)/shard_map/ppermute | solution.py:40
  23.3 9.3 %collective-permute-start.5 = (bf16[128,384]{1,0:T(8,128)(2,1)}, bf16[128,384]{1,0:T(8,128)(2,1)}, u32[]{:S(2)}, u32[]{:S(2)}) collective-permute-start(bf16[128,384]{1,0:T(8,128)(2,1)} %collective-permute-done.3.refs_0_), channel_id=1, source_target_pairs={{0,3},{1,0},{2,1},{3,2},{4,7},{5,4},{6,5},{7,6},{8,11},{9,8},{10,9... | collective-permute-start | bytes 294920 | tf_op jit(solution)/shard_map/ppermute | solution.py:40
  25.3 0.7 copy-start.2
  26.1 1.0 copy-start.3
  30.9 1.6 %copy-start = (bf16[8,4,128,384]{3,2,1,0:T(8,128)(2,1)}, bf16[8,4,128,384]{3,2,1,0:T(8,128)(2,1)S(1)}, u32[]{:S(2)}) copy-start(bf16[8,4,128,384]{3,2,1,0:T(8,128)(2,1)S(1)} %get-tuple-element.36) | copy-start | bytes 9437188
  34.4 14.0 %collective-permute-start.9 = (bf16[128,1536]{1,0:T(8,128)(2,1)}, bf16[128,1536]{1,0:T(8,128)(2,1)S(1)}, u32[]{:S(2)}, u32[]{:S(2)}) collective-permute-start(bf16[128,1536]{1,0:T(8,128)(2,1)} %shard_map.77), channel_id=1, source_target_pairs={{0,4},{1,5},{2,6},{3,7},{4,8},{5,9},{6,10},{7,11},{8,12},{9,13},{1... | collective-permute-start | bytes 1179656 | tf_op jit(solution)/shard_map/ppermute | solution.py:40
  34.4 14.0 %collective-permute-start.8 = (bf16[128,1536]{1,0:T(8,128)(2,1)}, bf16[128,1536]{1,0:T(8,128)(2,1)S(1)}, u32[]{:S(2)}, u32[]{:S(2)}) collective-permute-start(bf16[128,1536]{1,0:T(8,128)(2,1)} %shard_map.77), channel_id=1, source_target_pairs={{0,28},{1,29},{2,30},{3,31},{4,0},{5,1},{6,2},{7,3},{8,4},{9,5},{1... | collective-permute-start | bytes 1179656 | tf_op jit(solution)/shard_map/ppermute | solution.py:40
  39.2 6.2 %copy-start.4 = (bf16[128,1536]{1,0:T(8,128)(2,1)S(1)}, bf16[128,1536]{1,0:T(8,128)(2,1)}, u32[]{:S(2)}) copy-start(bf16[128,1536]{1,0:T(8,128)(2,1)} %shard_map.77) | copy-start | bytes 1179652
  39.2 44.1 %all-to-all-start = ((bf16[32,128,384]{2,1,0:T(8,128)(2,1)}), bf16[32,128,384]{2,1,0:T(8,128)(2,1)}, u32[]{:S(2)}, u32[]{:S(2)}) async-start(bf16[32,128,384]{2,1,0:T(8,128)(2,1)} %bitcast.117), calls=%async_computation | async-start | bytes 6291456 | tf_op jit(solution)/shard_map/all_to_all | solution.py:198
  48.4 11.3 %collective-permute-start.11 = (bf16[128,1536]{1,0:T(8,128)(2,1)S(1)}, bf16[128,1536]{1,0:T(8,128)(2,1)S(1)}, u32[]{:S(2)}, u32[]{:S(2)}) collective-permute-start(bf16[128,1536]{1,0:T(8,128)(2,1)S(1)} %collective-permute-done.9), channel_id=1, source_target_pairs={{0,4},{1,5},{2,6},{3,7},{4,8},{5,9},{6,10},{7,11},{8,12},{9,13},{1... | collective-permute-start | bytes 1179656 | tf_op jit(solution)/shard_map/ppermute | solution.py:40
  48.4 11.3 %collective-permute-start.10 = (bf16[128,1536]{1,0:T(8,128)(2,1)S(1)}, bf16[128,1536]{1,0:T(8,128)(2,1)S(1)}, u32[]{:S(2)}, u32[]{:S(2)}) collective-permute-start(bf16[128,1536]{1,0:T(8,128)(2,1)S(1)} %collective-permute-done.8), channel_id=1, source_target_pairs={{0,28},{1,29},{2,30},{3,31},{4,0},{5,1},{6,2},{7,3},{8,4},{9,5},{1... | collective-permute-start | bytes 1179656 | tf_op jit(solution)/shard_map/ppermute | solution.py:40
  59.7 10.5 %collective-permute-start.13 = (bf16[128,1536]{1,0:T(8,128)(2,1)S(1)}, bf16[128,1536]{1,0:T(8,128)(2,1)S(1)}, u32[]{:S(2)}, u32[]{:S(2)}) collective-permute-start(bf16[128,1536]{1,0:T(8,128)(2,1)S(1)} %collective-permute-done.11), channel_id=1, source_target_pairs={{0,4},{1,5},{2,6},{3,7},{4,8},{5,9},{6,10},{7,11},{8,12},{9,13},{1... | collective-permute-start | bytes 1179656 | tf_op jit(solution)/shard_map/ppermute | solution.py:40
  59.7 10.5 %collective-permute-start.12 = (bf16[128,1536]{1,0:T(8,128)(2,1)S(1)}, bf16[128,1536]{1,0:T(8,128)(2,1)S(1)}, u32[]{:S(2)}, u32[]{:S(2)}) collective-permute-start(bf16[128,1536]{1,0:T(8,128)(2,1)S(1)} %collective-permute-done.10), channel_id=1, source_target_pairs={{0,28},{1,29},{2,30},{3,31},{4,0},{5,1},{6,2},{7,3},{8,4},{9,5},{1... | collective-permute-start | bytes 1179656 | tf_op jit(solution)/shard_map/ppermute | solution.py:40
  70.3 8.7 %collective-permute-start.14 = (bf16[128,1536]{1,0:T(8,128)(2,1)S(1)}, bf16[128,1536]{1,0:T(8,128)(2,1)S(1)}, u32[]{:S(2)}, u32[]{:S(2)}) collective-permute-start(bf16[128,1536]{1,0:T(8,128)(2,1)S(1)} %collective-permute-done.12), channel_id=1, source_target_pairs={{0,28},{1,29},{2,30},{3,31},{4,0},{5,1},{6,2},{7,3},{8,4},{9,5},{1... | collective-permute-start | bytes 1179656 | tf_op jit(solution)/shard_map/ppermute | solution.py:40
  79.5 2.2 %collective-permute-start.15 = (bf16[4,128,384]{2,1,0:T(8,128)(2,1)S(1)}, bf16[4,128,384]{2,1,0:T(8,128)(2,1)S(1)}, u32[]{:S(2)}, u32[]{:S(2)}) collective-permute-start(bf16[4,128,384]{2,1,0:T(8,128)(2,1)S(1)} %slice.88), channel_id=1, source_target_pairs={{0,32},{1,33},{2,34},{3,35},{4,36},{5,37},{6,38},{7,39},{8,40},{9,... | collective-permute-start | bytes 1179656 | tf_op jit(solution)/shard_map/ppermute | solution.py:40
  85.6 8.6 %collective-permute-start.19 = (bf16[2,128,384]{2,1,0:T(8,128)(2,1)S(1)}, bf16[2,128,384]{2,1,0:T(8,128)(2,1)S(1)}, u32[]{:S(2)}, u32[]{:S(2)}) collective-permute-start(bf16[2,128,384]{2,1,0:T(8,128)(2,1)S(1)} %get-tuple-element.38), channel_id=1, source_target_pairs={{0,4},{1,5},{2,6},{3,7},{4,8},{5,9},{6,10},{7,11},{8,12},{9,13},{1... | collective-permute-start | bytes 589832 | tf_op jit(solution)/shard_map/ppermute | solution.py:40
  85.7 14.4 %collective-permute-start.20 = (bf16[2,128,384]{2,1,0:T(8,128)(2,1)S(1)}, bf16[2,128,384]{2,1,0:T(8,128)(2,1)S(1)}, u32[]{:S(2)}, u32[]{:S(2)}) collective-permute-start(bf16[2,128,384]{2,1,0:T(8,128)(2,1)S(1)} %get-tuple-element.39), channel_id=1, source_target_pairs={{0,28},{1,29},{2,30},{3,31},{4,0},{5,1},{6,2},{7,3},{8,4},{9,5},{1... | collective-permute-start | bytes 589832 | tf_op jit(solution)/shard_map/ppermute | solution.py:40
  89.0 11.3 %collective-permute-start.16 = (bf16[128,384]{1,0:T(8,128)(2,1)S(1)}, bf16[128,384]{1,0:T(8,128)(2,1)S(1)}, u32[]{:S(2)}, u32[]{:S(2)}) collective-permute-start(bf16[128,384]{1,0:T(8,128)(2,1)S(1)} %get-tuple-element.55), channel_id=1, source_target_pairs={{0,64},{1,65},{2,66},{3,67},{4,68},{5,69},{6,70},{7,71},{8,72},{9,... | collective-permute-start | bytes 294920 | tf_op jit(solution)/shard_map/ppermute | solution.py:40
  90.4 13.9 %collective-permute-start.18 = (bf16[128,384]{1,0:T(8,128)(2,1)S(1)}, bf16[128,384]{1,0:T(8,128)(2,1)S(1)}, u32[]{:S(2)}, u32[]{:S(2)}) collective-permute-start(bf16[128,384]{1,0:T(8,128)(2,1)S(1)} %get-tuple-element.56), channel_id=1, source_target_pairs={{0,192},{1,193},{2,194},{3,195},{4,196},{5,197},{6,198},{7,199},{8... | collective-permute-start | bytes 294920 | tf_op jit(solution)/shard_map/ppermute | solution.py:40
  92.3 12.1 %collective-permute-start.17 = (bf16[128,384]{1,0:T(8,128)(2,1)S(1)}, bf16[128,384]{1,0:T(8,128)(2,1)S(1)}, u32[]{:S(2)}, u32[]{:S(2)}) collective-permute-start(bf16[128,384]{1,0:T(8,128)(2,1)S(1)} %get-tuple-element.57), channel_id=1, source_target_pairs={{0,128},{1,129},{2,130},{3,131},{4,132},{5,133},{6,134},{7,135},{8... | collective-permute-start | bytes 294920 | tf_op jit(solution)/shard_map/ppermute | solution.py:40
  94.3 12.7 %collective-permute-start.21 = (bf16[128,384]{1,0:T(8,128)(2,1)S(1)}, bf16[128,384]{1,0:T(8,128)(2,1)S(1)}, u32[]{:S(2)}, u32[]{:S(2)}) collective-permute-start(bf16[128,384]{1,0:T(8,128)(2,1)S(1)} %get-tuple-element.40), channel_id=1, source_target_pairs={{0,16},{1,17},{2,18},{3,19},{4,20},{5,21},{6,22},{7,23},{8,24},{9,... | collective-permute-start | bytes 294920 | tf_op jit(solution)/shard_map/ppermute | solution.py:40
  100.1 9.2 %collective-permute-start.22 = (bf16[128,384]{1,0:T(8,128)(2,1)S(1)}, bf16[128,384]{1,0:T(8,128)(2,1)S(1)}, u32[]{:S(2)}, u32[]{:S(2)}) collective-permute-start(bf16[128,384]{1,0:T(8,128)(2,1)S(1)} %get-tuple-element.53), channel_id=1, source_target_pairs={{0,8},{1,9},{2,10},{3,11},{4,12},{5,13},{6,14},{7,15},{8,16},{9,17... | collective-permute-start | bytes 294920 | tf_op jit(solution)/shard_map/ppermute | solution.py:40
  100.2 9.1 %collective-permute-start.23 = (bf16[128,384]{1,0:T(8,128)(2,1)S(1)}, bf16[128,384]{1,0:T(8,128)(2,1)S(1)}, u32[]{:S(2)}, u32[]{:S(2)}) collective-permute-start(bf16[128,384]{1,0:T(8,128)(2,1)S(1)} %get-tuple-element.54), channel_id=1, source_target_pairs={{0,24},{1,25},{2,26},{3,27},{4,28},{5,29},{6,30},{7,31},{8,0},{9,1... | collective-permute-start | bytes 294920 | tf_op jit(solution)/shard_map/ppermute | solution.py:40

commit v4 on v3

--- a/solution.py
+++ b/solution.py
@@ -90,7 +90,7 @@
         grad_kernel,
         grid=(NX,),
         out_shape=(
-            jax.ShapeDtypeStruct((NR, NX, rows, k // NX), BF),
+            pltpu.HBM((NR, NX, rows, k // NX), BF),
             jax.ShapeDtypeStruct((k, n), BF),
             jax.ShapeDtypeStruct((NR, rows, n), BF),
         ),
@@ -189,6 +189,7 @@
     near = jnp.stack([along_y(cotangent, -k) if k else cotangent for k in turns])
     near, here = together(near, here)
     far = move(near, lambda r, z, x: (r ^ 1, z, x))
+    far = pltpu.with_memory_space_constraint(far, pltpu.HBM)
     rows = [(r + NC * k) % NR ^ other for other in (0, 1) for k in turns]
     place = jnp.stack(rows + [(r + skew(row) - z) % NZ for row in rows])
 
@@ -200,10 +201,13 @@
     )
 
     blocks = {0: assemble(x, [here, *sides])}
-    for s in range(1, NZ // 2 + 1):
+    for s in range(1, NZ // 2):
         blocks[s] = along_z(blocks[s - 1], -1)
-        if s < NZ // 2:
-            blocks[NZ - s] = along_z(blocks[(NZ - s + 1) % NZ], 1)
+        blocks[NZ - s] = along_z(blocks[(NZ - s + 1) % NZ], 1)
+    half = t // 2
+    blocks[4] = jnp.concatenate(
+        [along_z(blocks[3][:half], -1), along_z(blocks[5][half:], 1)]
+    )
     shares = jnp.zeros((NR, t, n), BF)
     for s in (0, 1, 7, 2, 6, 3, 5, 4):
         part = mm(blocks[s], weight).astype(BF)

time: 111 us -> 108 us (0.973)
  local copies, waits for them, and re-layouts: 4.95 us -> 2.64 us
  waiting for transfers between devices: 26.9 us -> 25 us
  Pallas kernels: 7.95 us -> 9.08 us
    ppermute x24 -> x25, waiting for transfers between devices: 25.4 us -> 22 us  [move(): return lax.ppermute(value, ('r', 'z', 'x'), pairs)]
    unnamed x25 -> x24, local copies, waits for them, and re-layouts: 3.74 us -> 1.4 us
    all_to_all x1, waiting for transfers between devices: 1.45 us -> 3.06 us  [per_device(): lax.all_to_all(parts.reshape(NR * NX, t, n), ('r', 'x'), split_axis=0, co...]
    pallas_call x1, Pallas kernels: 3.85 us -> 4.98 us  [grad_parts(): pl.pallas_call(grad_kernel, grid=(NX,), out_shape=(pltpu.HBM((NR, NX, row...]
    ppermute x24 -> x25, starting transfers between devices: 52.9 us -> 52.6 us  [move(): return lax.ppermute(value, ('r', 'z', 'x'), pairs)]
  transfers between devices with their start and end apart: 25 -> 26, of which waited for: 9 -> 8; matrix products, arithmetic and copies ran while one was open for 9% -> 11% of each run, Pallas kernels for 4% -> 5%
where the time goes in v4:
time: 108 us
  starting transfers between devices  58.5 us (54%)
  waiting for transfers between devices  25 us (23%)
  Pallas kernels  9.08 us (8%)
  matrix products  6.36 us (6%)
  other arithmetic  5.09 us (5%)
  local copies, waits for them, and re-layouts  2.64 us (2%)
    ppermute x25, starting transfers between devices, move(): return lax.ppermute(value, ('r', 'z', 'x'), pairs)  52.6 us
    ppermute x25, waiting for transfers between devices, move(): return lax.ppermute(value, ('r', 'z', 'x'), pairs)  22 us
    all_to_all x1, starting transfers between devices, per_device(): lax.all_to_all(parts.reshape(NR * NX, t, n), ('r', 'x'), split_axis=0, co...  5.97 us
    pallas_call x1, Pallas kernels, grad_parts(): pl.pallas_call(grad_kernel, grid=(NX,), out_shape=(pltpu.HBM((NR, NX, row...  4.98 us
    dot_general x8, matrix products, mm(): return jnp.dot(a, b, preferred_element_type=F32)  4.11 us
    all_to_all x1, waiting for transfers between devices, per_device(): lax.all_to_all(parts.reshape(NR * NX, t, n), ('r', 'x'), split_axis=0, co...  3.06 us
    pallas_call x1, Pallas kernels, sum_over_x(): pl.pallas_call(sum_kernel, out_shape=(jax.ShapeDtypeStruct((2, rows, k),...  2.27 us
    dot_general x2, matrix products, grad_of(): lax.dot_general(jnp.concatenate([blocks[s] for s in some]), jnp.concatena...  2.25 us
  transfers between devices with their start and end apart: 26, of which 8 were waited for; matrix products, arithmetic and copies ran while one was open for 11% of the time, Pallas kernels for 5%

profile of v4, /device:TPU:2, one launch (start us, length us, event | category | flops | bytes accessed | tf_op | source)
XLA Modules:
  0.0 107.8 jit_solution(2997161595132775444)
XLA Ops:
  0.7 0.8 mul.89
  1.4 0.1 copy.10
  1.6 0.9 multiply_convert_fusion
  2.5 3.3 %collective-permute-start.2 = (bf16[128,384]{1,0:T(8,128)(2,1)}, bf16[128,384]{1,0:T(8,128)(2,1)S(1)}, u32[]{:S(2)}, u32[]{:S(2)}) collective-permute-start(bf16[128,384]{1,0:T(8,128)(2,1)} %param.9), channel_id=1, source_target_pairs={{0,128},{1,129},{2,130},{3,131},{4,132},{5,133},{6,134},{7,135},{8... | collective-permute-start | bytes 294920 | tf_op jit(solution)/shard_map/ppermute | solution.py:40
  5.8 0.7 collective-permute-start.1
  6.5 2.6 %collective-permute-start = (bf16[128,384]{1,0:T(8,128)(2,1)}, bf16[128,384]{1,0:T(8,128)(2,1)S(1)}, u32[]{:S(2)}, u32[]{:S(2)}) collective-permute-start(bf16[128,384]{1,0:T(8,128)(2,1)} %param.9), channel_id=1, source_target_pairs={{0,192},{1,193},{2,194},{3,195},{4,196},{5,197},{6,198},{7,199},{8... | collective-permute-start | bytes 294920 | tf_op jit(solution)/shard_map/ppermute | solution.py:40
  9.0 1.3 %collective-permute-start.3 = (bf16[128,384]{1,0:T(8,128)(2,1)S(1)}, bf16[128,384]{1,0:T(8,128)(2,1)}, u32[]{:S(2)}, u32[]{:S(2)}) collective-permute-start(bf16[128,384]{1,0:T(8,128)(2,1)S(1)} %multiply_convert_fusion), channel_id=1, source_target_pairs={{0,0},{1,1},{2,2},{3,3},{4,36},{5,37},{6,38},{7,39},{8,72},{9,73},... | collective-permute-start | bytes 294920 | tf_op jit(solution)/shard_map/ppermute | solution.py:40
  10.3 1.5 %collective-permute-done.1 = bf16[128,384]{1,0:T(8,128)(2,1)S(1)} collective-permute-done((bf16[128,384]{1,0:T(8,128)(2,1)}, bf16[128,384]{1,0:T(8,128)(2,1)S(1)}, u32[]{:S(2)}, u32[]{:S(2)}) %collective-permute-start.1) | collective-permute-done | bytes 98336 | tf_op jit(solution)/shard_map/ppermute | solution.py:40
  11.8 1.0 pad_maximum_fusion.near
  12.8 7.4 %collective-permute-start.4 = (bf16[4,128,384]{2,1,0:T(8,128)(2,1)S(1)}, bf16[4,128,384]{2,1,0:T(8,128)(2,1)}, u32[]{:S(2)}, u32[]{:S(2)}) collective-permute-start(bf16[4,128,384]{2,1,0:T(8,128)(2,1)S(1)} %pad_maximum_fusion.near), channel_id=1, source_target_pairs={{0,32},{1,33},{2,34},{3,35},{4,36},{5,37},{6,38},{7,39},{8,40},{9,... | collective-permute-start | bytes 1179656 | tf_op jit(solution)/shard_map/ppermute | solution.py:40
  20.4 1.6 %collective-permute-start.7 = (bf16[128,384]{1,0:T(8,128)(2,1)}, bf16[128,384]{1,0:T(8,128)(2,1)}, u32[]{:S(2)}, u32[]{:S(2)}) collective-permute-start(bf16[128,384]{1,0:T(8,128)(2,1)} %collective-permute-done.3.refs_0_), channel_id=1, source_target_pairs={{0,1},{1,2},{2,3},{3,0},{4,5},{5,6},{6,7},{7,4},{8,9},{9,10},{10,1... | collective-permute-start | bytes 294920 | tf_op jit(solution)/shard_map/ppermute | solution.py:40
  22.0 1.2 %collective-permute-start.6 = (bf16[128,384]{1,0:T(8,128)(2,1)}, bf16[128,384]{1,0:T(8,128)(2,1)}, u32[]{:S(2)}, u32[]{:S(2)}) collective-permute-start(bf16[128,384]{1,0:T(8,128)(2,1)} %collective-permute-done.3.refs_0_), channel_id=1, source_target_pairs={{0,2},{1,3},{2,0},{3,1},{4,6},{5,7},{6,4},{7,5},{8,10},{9,11},{10,... | collective-permute-start | bytes 294920 | tf_op jit(solution)/shard_map/ppermute | solution.py:40
  23.3 2.0 %collective-permute-start.5 = (bf16[128,384]{1,0:T(8,128)(2,1)}, bf16[128,384]{1,0:T(8,128)(2,1)}, u32[]{:S(2)}, u32[]{:S(2)}) collective-permute-start(bf16[128,384]{1,0:T(8,128)(2,1)} %collective-permute-done.3.refs_0_), channel_id=1, source_target_pairs={{0,3},{1,0},{2,1},{3,2},{4,7},{5,4},{6,5},{7,6},{8,11},{9,8},{10,9... | collective-permute-start | bytes 294920 | tf_op jit(solution)/shard_map/ppermute | solution.py:40
  25.3 5.0 %shard_map.76 = (bf16[8,4,128,384]{3,2,1,0:T(8,128)(2,1)}, bf16[1536,384]{1,0:T(8,128)(2,1)S(1)}, bf16[8,128,384]{2,1,0:T(8,128)(2,1)S(1)}) custom-call(s32[16]{0:T(128)S(1)} %stack.87.place, f32[12,3]{1,0:T(8,128)S(1)} %copy.11.scales, bf16[4,128,384]{2,1,0:T(8,128)(2,1)S(1)} %pad_maximum_fusion.near, bf16[4,128,384]{2,1,0:T(8,128)(2,1)} %collective-permute-done.4.far, ...), custom_call_target="tpu_custom_call" | custom-call | flops 1207959552 | bytes 3145728 | tf_op jit(solution)/shard_map/pallas_call | solution.py:89
  30.3 1.8 %shard_map.77 = bf16[128,1536]{1,0:T(8,128)(2,1)} custom-call(s32[1]{0:T(128)} %bitcast.x, bf16[128,384]{1,0:T(8,128)(2,1)} %collective-permute-done.3.refs_0_, bf16[128,384]{1,0:T(8,128)(2,1)} %collective-permute-done.5.refs_1_, bf16[128,384]{1,0:T(8,128)(2,1)} %collective-permute-done.6.refs_2_, bf16[128,384]{1,0:T(8,128)(2,1)} %collective-permute-done.7.refs_3_), custom_call_target="tpu_custom_call" | custom-call | bytes 786432 | tf_op jit(solution)/shard_map/pallas_call | solution.py:164
  32.1 4.8 %collective-permute-start.8 = (bf16[128,1536]{1,0:T(8,128)(2,1)}, bf16[128,1536]{1,0:T(8,128)(2,1)}, u32[]{:S(2)}, u32[]{:S(2)}) collective-permute-start(bf16[128,1536]{1,0:T(8,128)(2,1)} %shard_map.77), channel_id=1, source_target_pairs={{0,28},{1,29},{2,30},{3,31},{4,0},{5,1},{6,2},{7,3},{8,4},{9,5},{1... | collective-permute-start | bytes 1179656 | tf_op jit(solution)/shard_map/ppermute | solution.py:40
  37.0 6.0 %all-to-all-start = ((bf16[32,128,384]{2,1,0:T(8,128)(2,1)}), bf16[32,128,384]{2,1,0:T(8,128)(2,1)}, u32[]{:S(2)}, u32[]{:S(2)}) async-start(bf16[32,128,384]{2,1,0:T(8,128)(2,1)} %bitcast.117), calls=%async_computation | async-start | bytes 6291456 | tf_op jit(solution)/shard_map/all_to_all | solution.py:199
  43.2 0.4 fusion.1
  43.6 2.5 %collective-permute-done.9 = bf16[128,1536]{1,0:T(8,128)(2,1)S(1)} collective-permute-done((bf16[128,1536]{1,0:T(8,128)(2,1)}, bf16[128,1536]{1,0:T(8,128)(2,1)S(1)}, u32[]{:S(2)}, u32[]{:S(2)}) %collective-permute-start.9) | collective-permute-done | bytes 393248 | tf_op jit(solution)/shard_map/ppermute | solution.py:40
  46.1 3.2 %collective-permute-start.10 = (bf16[128,1536]{1,0:T(8,128)(2,1)}, bf16[128,1536]{1,0:T(8,128)(2,1)S(1)}, u32[]{:S(2)}, u32[]{:S(2)}) collective-permute-start(bf16[128,1536]{1,0:T(8,128)(2,1)} %collective-permute-done.8), channel_id=1, source_target_pairs={{0,28},{1,29},{2,30},{3,31},{4,0},{5,1},{6,2},{7,3},{8,4},{9,5},{1... | collective-permute-start | bytes 1179656 | tf_op jit(solution)/shard_map/ppermute | solution.py:40
  49.4 1.4 %fusion.3 = bf16[8,128,384]{2,1,0:T(8,128)(2,1)S(1)} fusion(bf16[8,128,384]{2,1,0:T(8,128)(2,1)S(1)} %fusion.1, s32[]{:T(128)S(6)} %select_n.387, bf16[128,1536]{1,0:T(8,128)(2,1)} %collective-permute-done.8, bf16[1536,384]{1,0:T(8,128)(2,1)S(1)} %get-tuple-element.35), kind=kOutput, calls=%fused_computation.12 | convolution fusion | flops 151044096 | bytes 1671172 | tf_op jit(solution)/shard_map/dot_general | solution.py:56
  50.8 0.4 fusion.5
  51.2 6.3 %collective-permute-done.11 = bf16[128,1536]{1,0:T(8,128)(2,1)S(1)} collective-permute-done((bf16[128,1536]{1,0:T(8,128)(2,1)S(1)}, bf16[128,1536]{1,0:T(8,128)(2,1)S(1)}, u32[]{:S(2)}, u32[]{:S(2)}) %collective-permute-start.11) | collective-permute-done | bytes 393248 | tf_op jit(solution)/shard_map/ppermute | solution.py:40
  57.5 3.2 %collective-permute-start.12 = (bf16[128,1536]{1,0:T(8,128)(2,1)S(1)}, bf16[128,1536]{1,0:T(8,128)(2,1)S(1)}, u32[]{:S(2)}, u32[]{:S(2)}) collective-permute-start(bf16[128,1536]{1,0:T(8,128)(2,1)S(1)} %collective-permute-done.10), channel_id=1, source_target_pairs={{0,28},{1,29},{2,30},{3,31},{4,0},{5,1},{6,2},{7,3},{8,4},{9,5},{1... | collective-permute-start | bytes 1179656 | tf_op jit(solution)/shard_map/ppermute | solution.py:40
  60.7 0.4 fusion.7
  61.1 0.4 fusion.9
  61.5 6.5 %collective-permute-done.13 = bf16[128,1536]{1,0:T(8,128)(2,1)S(1)} collective-permute-done((bf16[128,1536]{1,0:T(8,128)(2,1)S(1)}, bf16[128,1536]{1,0:T(8,128)(2,1)S(1)}, u32[]{:S(2)}, u32[]{:S(2)}) %collective-permute-start.13) | collective-permute-done | bytes 393248 | tf_op jit(solution)/shard_map/ppermute | solution.py:40
  68.1 3.3 %collective-permute-start.14 = (bf16[64,1536]{1,0:T(8,128)(2,1)S(1)}, bf16[64,1536]{1,0:T(8,128)(2,1)S(1)}, u32[]{:S(2)}, u32[]{:S(2)}) collective-permute-start(bf16[64,1536]{1,0:T(8,128)(2,1)S(1)} %slice.95), channel_id=1, source_target_pairs={{0,28},{1,29},{2,30},{3,31},{4,0},{5,1},{6,2},{7,3},{8,4},{9,5},{1... | collective-permute-start | bytes 589832 | tf_op jit(solution)/shard_map/ppermute | solution.py:40
  71.4 1.0 constant_dynamic-update-slice_fusion.7
  72.6 0.4 fusion.11
  73.0 1.8 %fusion.27 = f32[1536,384]{1,0:T(8,128)S(1)} fusion(bf16[896,1536]{1,0:T(8,128)(2,1)S(1)} %constant_dynamic-update-slice_fusion.2, bf16[896,384]{1,0:T(8,128)(2,1)S(1)} %bitcast_dynamic-update-slice_fusion), kind=kOutput, calls=%fused_computation.62 | convolution fusion | flops 1056964608 | bytes 5799936 | tf_op jit(solution)/shard_map/dot_general | solution.py:233
  74.8 0.4 fusion.13
  75.2 0.4 fusion.15
  75.8 0.5 fusion.23
  76.3 1.6 %add_multiply_fusion = f32[1536,384]{1,0:T(8,128)} fusion(f32[1536,384]{1,0:T(8,128)S(1)} %fusion.27, f32[1536,384]{1,0:T(8,128)S(1)} %fusion.23), kind=kLoop, calls=%fused_computation | loop fusion | flops 1179648 | bytes 7077888 | tf_op jit(solution)/shard_map/mul | solution.py:245
  78.0 3.1 %all-to-all-done = bf16[32,128,384]{2,1,0:T(8,128)(2,1)} async-done(((bf16[32,128,384]{2,1,0:T(8,128)(2,1)}), bf16[32,128,384]{2,1,0:T(8,128)(2,1)}, u32[]{:S(2)}, u32[]{:S(2)}) %all-to-all-start) | async-done | bytes 3145760 | tf_op jit(solution)/shard_map/all_to_all | solution.py:199
  81.1 2.3 %shard_map.78 = (bf16[2,128,384]{2,1,0:T(8,128)(2,1)S(1)}, bf16[2,128,384]{2,1,0:T(8,128)(2,1)S(1)}, bf16[128,384]{1,0:T(8,128)(2,1)S(1)}, f32[3,128,384]{2,1,0:T(8,128)S(1)}) custom-call(s32[1]{0:T(128)} %bitcast.34.z, bf16[8,4,128,384]{3,2,1,0:T(8,128)(2,1)} %bitcast.36.parts), custom_call_target="tpu_custom_call" | custom-call | flops 1572864 | bytes 4718592 | tf_op jit(solution)/shard_map/pallas_call | solution.py:137
  83.5 3.2 %collective-permute-start.21 = (bf16[2,128,384]{2,1,0:T(8,128)(2,1)S(1)}, bf16[2,128,384]{2,1,0:T(8,128)(2,1)S(1)}, u32[]{:S(2)}, u32[]{:S(2)}) collective-permute-start(bf16[2,128,384]{2,1,0:T(8,128)(2,1)S(1)} %get-tuple-element.39), channel_id=1, source_target_pairs={{0,28},{1,29},{2,30},{3,31},{4,0},{5,1},{6,2},{7,3},{8,4},{9,5},{1... | collective-permute-start | bytes 589832 | tf_op jit(solution)/shard_map/ppermute | solution.py:40
  86.7 0.3 collective-permute-start.17
  87.1 3.0 %collective-permute-start.19 = (bf16[128,384]{1,0:T(8,128)(2,1)S(1)}, bf16[128,384]{1,0:T(8,128)(2,1)S(1)}, u32[]{:S(2)}, u32[]{:S(2)}) collective-permute-start(bf16[128,384]{1,0:T(8,128)(2,1)S(1)} %get-tuple-element.56), channel_id=1, source_target_pairs={{0,192},{1,193},{2,194},{3,195},{4,196},{5,197},{6,198},{7,199},{8... | collective-permute-start | bytes 294920 | tf_op jit(solution)/shard_map/ppermute | solution.py:40
  90.0 1.1 collective-permute-start.18
  91.1 0.9 collective-permute-done.20
  92.0 5.8 %collective-permute-start.22 = (bf16[128,384]{1,0:T(8,128)(2,1)S(1)}, bf16[128,384]{1,0:T(8,128)(2,1)S(1)}, u32[]{:S(2)}, u32[]{:S(2)}) collective-permute-start(bf16[128,384]{1,0:T(8,128)(2,1)S(1)} %get-tuple-element.40), channel_id=1, source_target_pairs={{0,16},{1,17},{2,18},{3,19},{4,20},{5,21},{6,22},{7,23},{8,24},{9,... | collective-permute-start | bytes 294920 | tf_op jit(solution)/shard_map/ppermute | solution.py:40
  98.0 4.1 %collective-permute-start.24 = (bf16[128,384]{1,0:T(8,128)(2,1)S(1)}, bf16[128,384]{1,0:T(8,128)(2,1)S(1)}, u32[]{:S(2)}, u32[]{:S(2)}) collective-permute-start(bf16[128,384]{1,0:T(8,128)(2,1)S(1)} %get-tuple-element.54), channel_id=1, source_target_pairs={{0,24},{1,25},{2,26},{3,27},{4,28},{5,29},{6,30},{7,31},{8,0},{9,1... | collective-permute-start | bytes 294920 | tf_op jit(solution)/shard_map/ppermute | solution.py:40
  102.1 0.7 fusion.17
  102.8 1.6 %collective-permute-done.22 = bf16[128,384]{1,0:T(8,128)(2,1)S(1)} collective-permute-done((bf16[128,384]{1,0:T(8,128)(2,1)S(1)}, bf16[128,384]{1,0:T(8,128)(2,1)S(1)}, u32[]{:S(2)}, u32[]{:S(2)}) %collective-permute-start.22) | collective-permute-done | bytes 98336 | tf_op jit(solution)/shard_map/ppermute | solution.py:40
  104.4 2.7 %collective-permute-done.23 = bf16[128,384]{1,0:T(8,128)(2,1)S(1)} collective-permute-done((bf16[128,384]{1,0:T(8,128)(2,1)S(1)}, bf16[128,384]{1,0:T(8,128)(2,1)S(1)}, u32[]{:S(2)}, u32[]{:S(2)}) %collective-permute-start.23) | collective-permute-done | bytes 98336 | tf_op jit(solution)/shard_map/ppermute | solution.py:40
  107.1 0.7 fusion.20
  (59 shorter events, 1.3 us)
Async XLA Ops:
  0.6 19.6 %copy-start.4 = (f32[12,3]{0,1:T(4,128)S(1)}, f32[12,3]{0,1:T(4,128)}, u32[]{:S(2)}) copy-start(f32[12,3]{0,1:T(4,128)} %param.8) | copy-start | bytes 436
  0.6 24.7 %copy-start = (bf16[1536,384]{1,0:T(8,128)(2,1)S(1)}, bf16[1536,384]{1,0:T(8,128)(2,1)}, u32[]{:S(2)}) copy-start(bf16[1536,384]{1,0:T(8,128)(2,1)} %values.1) | copy-start | bytes 3538948
  2.5 7.8 %collective-permute-start.2 = (bf16[128,384]{1,0:T(8,128)(2,1)}, bf16[128,384]{1,0:T(8,128)(2,1)S(1)}, u32[]{:S(2)}, u32[]{:S(2)}) collective-permute-start(bf16[128,384]{1,0:T(8,128)(2,1)} %param.9), channel_id=1, source_target_pairs={{0,128},{1,129},{2,130},{3,131},{4,132},{5,133},{6,134},{7,135},{8... | collective-permute-start | bytes 294920 | tf_op jit(solution)/shard_map/ppermute | solution.py:40
  5.8 6.0 %collective-permute-start.1 = (bf16[128,384]{1,0:T(8,128)(2,1)}, bf16[128,384]{1,0:T(8,128)(2,1)S(1)}, u32[]{:S(2)}, u32[]{:S(2)}) collective-permute-start(bf16[128,384]{1,0:T(8,128)(2,1)} %param.9), channel_id=1, source_target_pairs={{0,64},{1,65},{2,66},{3,67},{4,68},{5,69},{6,70},{7,71},{8,72},{9,... | collective-permute-start | bytes 294920 | tf_op jit(solution)/shard_map/ppermute | solution.py:40
  6.5 5.4 %collective-permute-start = (bf16[128,384]{1,0:T(8,128)(2,1)}, bf16[128,384]{1,0:T(8,128)(2,1)S(1)}, u32[]{:S(2)}, u32[]{:S(2)}) collective-permute-start(bf16[128,384]{1,0:T(8,128)(2,1)} %param.9), channel_id=1, source_target_pairs={{0,192},{1,193},{2,194},{3,195},{4,196},{5,197},{6,198},{7,199},{8... | collective-permute-start | bytes 294920 | tf_op jit(solution)/shard_map/ppermute | solution.py:40
  9.0 3.8 %collective-permute-start.3 = (bf16[128,384]{1,0:T(8,128)(2,1)S(1)}, bf16[128,384]{1,0:T(8,128)(2,1)}, u32[]{:S(2)}, u32[]{:S(2)}) collective-permute-start(bf16[128,384]{1,0:T(8,128)(2,1)S(1)} %multiply_convert_fusion), channel_id=1, source_target_pairs={{0,0},{1,1},{2,2},{3,3},{4,36},{5,37},{6,38},{7,39},{8,72},{9,73},... | collective-permute-start | bytes 294920 | tf_op jit(solution)/shard_map/ppermute | solution.py:40
  12.8 12.5 %collective-permute-start.4 = (bf16[4,128,384]{2,1,0:T(8,128)(2,1)S(1)}, bf16[4,128,384]{2,1,0:T(8,128)(2,1)}, u32[]{:S(2)}, u32[]{:S(2)}) collective-permute-start(bf16[4,128,384]{2,1,0:T(8,128)(2,1)S(1)} %pad_maximum_fusion.near), channel_id=1, source_target_pairs={{0,32},{1,33},{2,34},{3,35},{4,36},{5,37},{6,38},{7,39},{8,40},{9,... | collective-permute-start | bytes 1179656 | tf_op jit(solution)/shard_map/ppermute | solution.py:40
  20.4 9.9 %collective-permute-start.7 = (bf16[128,384]{1,0:T(8,128)(2,1)}, bf16[128,384]{1,0:T(8,128)(2,1)}, u32[]{:S(2)}, u32[]{:S(2)}) collective-permute-start(bf16[128,384]{1,0:T(8,128)(2,1)} %collective-permute-done.3.refs_0_), channel_id=1, source_target_pairs={{0,1},{1,2},{2,3},{3,0},{4,5},{5,6},{6,7},{7,4},{8,9},{9,10},{10,1... | collective-permute-start | bytes 294920 | tf_op jit(solution)/shard_map/ppermute | solution.py:40
  22.0 8.3 %collective-permute-start.6 = (bf16[128,384]{1,0:T(8,128)(2,1)}, bf16[128,384]{1,0:T(8,128)(2,1)}, u32[]{:S(2)}, u32[]{:S(2)}) collective-permute-start(bf16[128,384]{1,0:T(8,128)(2,1)} %collective-permute-done.3.refs_0_), channel_id=1, source_target_pairs={{0,2},{1,3},{2,0},{3,1},{4,6},{5,7},{6,4},{7,5},{8,10},{9,11},{10,... | collective-permute-start | bytes 294920 | tf_op jit(solution)/shard_map/ppermute | solution.py:40
  23.3 7.0 %collective-permute-start.5 = (bf16[128,384]{1,0:T(8,128)(2,1)}, bf16[128,384]{1,0:T(8,128)(2,1)}, u32[]{:S(2)}, u32[]{:S(2)}) collective-permute-start(bf16[128,384]{1,0:T(8,128)(2,1)} %collective-permute-done.3.refs_0_), channel_id=1, source_target_pairs={{0,3},{1,0},{2,1},{3,2},{4,7},{5,4},{6,5},{7,6},{8,11},{9,8},{10,9... | collective-permute-start | bytes 294920 | tf_op jit(solution)/shard_map/ppermute | solution.py:40
  32.1 14.0 %collective-permute-start.9 = (bf16[128,1536]{1,0:T(8,128)(2,1)}, bf16[128,1536]{1,0:T(8,128)(2,1)S(1)}, u32[]{:S(2)}, u32[]{:S(2)}) collective-permute-start(bf16[128,1536]{1,0:T(8,128)(2,1)} %shard_map.77), channel_id=1, source_target_pairs={{0,4},{1,5},{2,6},{3,7},{4,8},{5,9},{6,10},{7,11},{8,12},{9,13},{1... | collective-permute-start | bytes 1179656 | tf_op jit(solution)/shard_map/ppermute | solution.py:40
  32.1 14.0 %collective-permute-start.8 = (bf16[128,1536]{1,0:T(8,128)(2,1)}, bf16[128,1536]{1,0:T(8,128)(2,1)}, u32[]{:S(2)}, u32[]{:S(2)}) collective-permute-start(bf16[128,1536]{1,0:T(8,128)(2,1)} %shard_map.77), channel_id=1, source_target_pairs={{0,28},{1,29},{2,30},{3,31},{4,0},{5,1},{6,2},{7,3},{8,4},{9,5},{1... | collective-permute-start | bytes 1179656 | tf_op jit(solution)/shard_map/ppermute | solution.py:40
  37.0 6.2 %copy-start.1 = (bf16[128,1536]{1,0:T(8,128)(2,1)S(1)}, bf16[128,1536]{1,0:T(8,128)(2,1)}, u32[]{:S(2)}) copy-start(bf16[128,1536]{1,0:T(8,128)(2,1)} %shard_map.77) | copy-start | bytes 1179652
  37.0 44.1 %all-to-all-start = ((bf16[32,128,384]{2,1,0:T(8,128)(2,1)}), bf16[32,128,384]{2,1,0:T(8,128)(2,1)}, u32[]{:S(2)}, u32[]{:S(2)}) async-start(bf16[32,128,384]{2,1,0:T(8,128)(2,1)} %bitcast.117), calls=%async_computation | async-start | bytes 6291456 | tf_op jit(solution)/shard_map/all_to_all | solution.py:199
  46.1 5.0 %copy-start.2 = (bf16[128,1536]{1,0:T(8,128)(2,1)}, bf16[128,1536]{1,0:T(8,128)(2,1)S(1)}, u32[]{:S(2)}) copy-start(bf16[128,1536]{1,0:T(8,128)(2,1)S(1)} %collective-permute-done.9) | copy-start | bytes 1179652
  46.1 11.3 %collective-permute-start.11 = (bf16[128,1536]{1,0:T(8,128)(2,1)S(1)}, bf16[128,1536]{1,0:T(8,128)(2,1)S(1)}, u32[]{:S(2)}, u32[]{:S(2)}) collective-permute-start(bf16[128,1536]{1,0:T(8,128)(2,1)S(1)} %collective-permute-done.9), channel_id=1, source_target_pairs={{0,4},{1,5},{2,6},{3,7},{4,8},{5,9},{6,10},{7,11},{8,12},{9,13},{1... | collective-permute-start | bytes 1179656 | tf_op jit(solution)/shard_map/ppermute | solution.py:40
  46.1 11.3 %collective-permute-start.10 = (bf16[128,1536]{1,0:T(8,128)(2,1)}, bf16[128,1536]{1,0:T(8,128)(2,1)S(1)}, u32[]{:S(2)}, u32[]{:S(2)}) collective-permute-start(bf16[128,1536]{1,0:T(8,128)(2,1)} %collective-permute-done.8), channel_id=1, source_target_pairs={{0,28},{1,29},{2,30},{3,31},{4,0},{5,1},{6,2},{7,3},{8,4},{9,5},{1... | collective-permute-start | bytes 1179656 | tf_op jit(solution)/shard_map/ppermute | solution.py:40
  57.4 10.5 %collective-permute-start.13 = (bf16[128,1536]{1,0:T(8,128)(2,1)S(1)}, bf16[128,1536]{1,0:T(8,128)(2,1)S(1)}, u32[]{:S(2)}, u32[]{:S(2)}) collective-permute-start(bf16[128,1536]{1,0:T(8,128)(2,1)S(1)} %collective-permute-done.11), channel_id=1, source_target_pairs={{0,4},{1,5},{2,6},{3,7},{4,8},{5,9},{6,10},{7,11},{8,12},{9,13},{1... | collective-permute-start | bytes 1179656 | tf_op jit(solution)/shard_map/ppermute | solution.py:40
  57.5 10.6 %collective-permute-start.12 = (bf16[128,1536]{1,0:T(8,128)(2,1)S(1)}, bf16[128,1536]{1,0:T(8,128)(2,1)S(1)}, u32[]{:S(2)}, u32[]{:S(2)}) collective-permute-start(bf16[128,1536]{1,0:T(8,128)(2,1)S(1)} %collective-permute-done.10), channel_id=1, source_target_pairs={{0,28},{1,29},{2,30},{3,31},{4,0},{5,1},{6,2},{7,3},{8,4},{9,5},{1... | collective-permute-start | bytes 1179656 | tf_op jit(solution)/shard_map/ppermute | solution.py:40
  61.1 11.4 %copy-start.3 = (bf16[128,1536]{1,0:T(8,128)(2,1)S(1)}, bf16[128,1536]{1,0:T(8,128)(2,1)}, u32[]{:S(2)}) copy-start(bf16[128,1536]{1,0:T(8,128)(2,1)} %copy-done.2) | copy-start | bytes 1179652
  68.0 7.2 %collective-permute-start.15 = (bf16[64,1536]{1,0:T(8,128)(2,1)S(1)}, bf16[64,1536]{1,0:T(8,128)(2,1)S(1)}, u32[]{:S(2)}, u32[]{:S(2)}) collective-permute-start(bf16[64,1536]{1,0:T(8,128)(2,1)S(1)} %slice.96), channel_id=1, source_target_pairs={{0,4},{1,5},{2,6},{3,7},{4,8},{5,9},{6,10},{7,11},{8,12},{9,13},{1... | collective-permute-start | bytes 589832 | tf_op jit(solution)/shard_map/ppermute | solution.py:40
  68.1 7.1 %collective-permute-start.14 = (bf16[64,1536]{1,0:T(8,128)(2,1)S(1)}, bf16[64,1536]{1,0:T(8,128)(2,1)S(1)}, u32[]{:S(2)}, u32[]{:S(2)}) collective-permute-start(bf16[64,1536]{1,0:T(8,128)(2,1)S(1)} %slice.95), channel_id=1, source_target_pairs={{0,28},{1,29},{2,30},{3,31},{4,0},{5,1},{6,2},{7,3},{8,4},{9,5},{1... | collective-permute-start | bytes 589832 | tf_op jit(solution)/shard_map/ppermute | solution.py:40
  75.7 2.2 %collective-permute-start.16 = (bf16[4,128,384]{2,1,0:T(8,128)(2,1)S(1)}, bf16[4,128,384]{2,1,0:T(8,128)(2,1)S(1)}, u32[]{:S(2)}, u32[]{:S(2)}) collective-permute-start(bf16[4,128,384]{2,1,0:T(8,128)(2,1)S(1)} %slice.98), channel_id=1, source_target_pairs={{0,32},{1,33},{2,34},{3,35},{4,36},{5,37},{6,38},{7,39},{8,40},{9,... | collective-permute-start | bytes 1179656 | tf_op jit(solution)/shard_map/ppermute | solution.py:40
  83.4 8.6 %collective-permute-start.20 = (bf16[2,128,384]{2,1,0:T(8,128)(2,1)S(1)}, bf16[2,128,384]{2,1,0:T(8,128)(2,1)S(1)}, u32[]{:S(2)}, u32[]{:S(2)}) collective-permute-start(bf16[2,128,384]{2,1,0:T(8,128)(2,1)S(1)} %get-tuple-element.38), channel_id=1, source_target_pairs={{0,4},{1,5},{2,6},{3,7},{4,8},{5,9},{6,10},{7,11},{8,12},{9,13},{1... | collective-permute-start | bytes 589832 | tf_op jit(solution)/shard_map/ppermute | solution.py:40
  83.5 14.4 %collective-permute-start.21 = (bf16[2,128,384]{2,1,0:T(8,128)(2,1)S(1)}, bf16[2,128,384]{2,1,0:T(8,128)(2,1)S(1)}, u32[]{:S(2)}, u32[]{:S(2)}) collective-permute-start(bf16[2,128,384]{2,1,0:T(8,128)(2,1)S(1)} %get-tuple-element.39), channel_id=1, source_target_pairs={{0,28},{1,29},{2,30},{3,31},{4,0},{5,1},{6,2},{7,3},{8,4},{9,5},{1... | collective-permute-start | bytes 589832 | tf_op jit(solution)/shard_map/ppermute | solution.py:40
  86.7 11.3 %collective-permute-start.17 = (bf16[128,384]{1,0:T(8,128)(2,1)S(1)}, bf16[128,384]{1,0:T(8,128)(2,1)S(1)}, u32[]{:S(2)}, u32[]{:S(2)}) collective-permute-start(bf16[128,384]{1,0:T(8,128)(2,1)S(1)} %get-tuple-element.55), channel_id=1, source_target_pairs={{0,64},{1,65},{2,66},{3,67},{4,68},{5,69},{6,70},{7,71},{8,72},{9,... | collective-permute-start | bytes 294920 | tf_op jit(solution)/shard_map/ppermute | solution.py:40
  87.1 15.1 %collective-permute-start.19 = (bf16[128,384]{1,0:T(8,128)(2,1)S(1)}, bf16[128,384]{1,0:T(8,128)(2,1)S(1)}, u32[]{:S(2)}, u32[]{:S(2)}) collective-permute-start(bf16[128,384]{1,0:T(8,128)(2,1)S(1)} %get-tuple-element.56), channel_id=1, source_target_pairs={{0,192},{1,193},{2,194},{3,195},{4,196},{5,197},{6,198},{7,199},{8... | collective-permute-start | bytes 294920 | tf_op jit(solution)/shard_map/ppermute | solution.py:40
  90.0 12.1 %collective-permute-start.18 = (bf16[128,384]{1,0:T(8,128)(2,1)S(1)}, bf16[128,384]{1,0:T(8,128)(2,1)S(1)}, u32[]{:S(2)}, u32[]{:S(2)}) collective-permute-start(bf16[128,384]{1,0:T(8,128)(2,1)S(1)} %get-tuple-element.57), channel_id=1, source_target_pairs={{0,128},{1,129},{2,130},{3,131},{4,132},{5,133},{6,134},{7,135},{8... | collective-permute-start | bytes 294920 | tf_op jit(solution)/shard_map/ppermute | solution.py:40
  92.0 12.4 %collective-permute-start.22 = (bf16[128,384]{1,0:T(8,128)(2,1)S(1)}, bf16[128,384]{1,0:T(8,128)(2,1)S(1)}, u32[]{:S(2)}, u32[]{:S(2)}) collective-permute-start(bf16[128,384]{1,0:T(8,128)(2,1)S(1)} %get-tuple-element.40), channel_id=1, source_target_pairs={{0,16},{1,17},{2,18},{3,19},{4,20},{5,21},{6,22},{7,23},{8,24},{9,... | collective-permute-start | bytes 294920 | tf_op jit(solution)/shard_map/ppermute | solution.py:40
  97.9 9.2 %collective-permute-start.23 = (bf16[128,384]{1,0:T(8,128)(2,1)S(1)}, bf16[128,384]{1,0:T(8,128)(2,1)S(1)}, u32[]{:S(2)}, u32[]{:S(2)}) collective-permute-start(bf16[128,384]{1,0:T(8,128)(2,1)S(1)} %get-tuple-element.53), channel_id=1, source_target_pairs={{0,8},{1,9},{2,10},{3,11},{4,12},{5,13},{6,14},{7,15},{8,16},{9,17... | collective-permute-start | bytes 294920 | tf_op jit(solution)/shard_map/ppermute | solution.py:40
  98.0 9.1 %collective-permute-start.24 = (bf16[128,384]{1,0:T(8,128)(2,1)S(1)}, bf16[128,384]{1,0:T(8,128)(2,1)S(1)}, u32[]{:S(2)}, u32[]{:S(2)}) collective-permute-start(bf16[128,384]{1,0:T(8,128)(2,1)S(1)} %get-tuple-element.54), channel_id=1, source_target_pairs={{0,24},{1,25},{2,26},{3,27},{4,28},{5,29},{6,30},{7,31},{8,0},{9,1... | collective-permute-start | bytes 294920 | tf_op jit(solution)/shard_map/ppermute | solution.py:40

commit v5 on v4

--- a/solution.py
+++ b/solution.py
@@ -152,11 +152,17 @@
 
 
 def assemble_kernel(x, *refs):
-    parts, out = refs[:NX], refs[NX]
+    parts, out, sems = refs[:NX], refs[NX], refs[NX + 1]
     n = parts[0].shape[1]
+    copies = []
     for off in range(NX):
         at = pl.multiple_of(lax.rem(x[0] + off, NX) * n, 128)
-        out[:, pl.ds(at, n)] = parts[off][...]
+        copies.append(
+            pltpu.make_async_copy(parts[off], out.at[:, pl.ds(at, n)], sems.at[off])
+        )
+        copies[-1].start()
+    for copy in copies:
+        copy.wait()
 
 
 def assemble(x, parts):
@@ -165,8 +171,9 @@
         assemble_kernel,
         out_shape=jax.ShapeDtypeStruct((t, NX * n), BF),
         in_specs=[pl.BlockSpec(memory_space=pltpu.SMEM)]
-        + [pl.BlockSpec(memory_space=pltpu.VMEM)] * NX,
-        out_specs=pl.BlockSpec(memory_space=pltpu.VMEM),
+        + [pl.BlockSpec(memory_space=pl.ANY)] * NX,
+        out_specs=pl.BlockSpec(memory_space=pl.ANY),
+        scratch_shapes=[pltpu.SemaphoreType.DMA((NX,))],
         cost_estimate=pl.CostEstimate(
             flops=0, bytes_accessed=4 * t * NX * n, transcendentals=0
         ),

time: 108 us -> 120 us (1.11)
  Pallas kernels: 9.08 us -> 20.3 us
    pallas_call x1, Pallas kernels: 1.82 us -> 13.1 us  [assemble(): pl.pallas_call(assemble_kernel, out_shape=jax.ShapeDtypeStruct((t, NX * n...]
  transfers between devices with their start and end apart: 26 -> 26, of which waited for: 8 -> 8; matrix products, arithmetic and copies ran while one was open for 11% -> 10% of each run, Pallas kernels for 5% -> 4%
where the time goes in v5:
time: 120 us; the launch traced here: 119 us
  starting transfers between devices  58.6 us (49%)
  waiting for transfers between devices  25.1 us (21%)
  Pallas kernels  20.3 us (17%)
  matrix products  6.36 us (5%)
  other arithmetic  5.09 us (4%)
  local copies, waits for them, and re-layouts  2.64 us (2%)
    ppermute x25, starting transfers between devices, move(): return lax.ppermute(value, ('r', 'z', 'x'), pairs)  52.6 us
    ppermute x25, waiting for transfers between devices, move(): return lax.ppermute(value, ('r', 'z', 'x'), pairs)  22 us
    pallas_call x1, Pallas kernels, assemble(): pl.pallas_call(assemble_kernel, out_shape=jax.ShapeDtypeStruct((t, NX * n...  13.1 us
    all_to_all x1, starting transfers between devices, per_device(): lax.all_to_all(parts.reshape(NR * NX, t, n), ('r', 'x'), split_axis=0, co...  5.97 us
    pallas_call x1, Pallas kernels, grad_parts(): pl.pallas_call(grad_kernel, grid=(NX,), out_shape=(pltpu.HBM((NR, NX, row...  4.98 us
    dot_general x8, matrix products, mm(): return jnp.dot(a, b, preferred_element_type=F32)  4.11 us
    all_to_all x1, waiting for transfers between devices, per_device(): lax.all_to_all(parts.reshape(NR * NX, t, n), ('r', 'x'), split_axis=0, co...  3.14 us
  transfers between devices with their start and end apart: 26, of which 8 were waited for; matrix products, arithmetic and copies ran while one was open for 10% of the time, Pallas kernels for 4%

profile of v5, /device:TPU:2, one launch (start us, length us, event | category | flops | bytes accessed | tf_op | source)
XLA Modules:
  0.0 119.2 jit_solution(13200791860874963249)
XLA Ops:
  0.7 0.8 mul.89
  1.4 0.1 copy.10
  1.6 0.9 multiply_convert_fusion
  2.5 3.3 %collective-permute-start.2 = (bf16[128,384]{1,0:T(8,128)(2,1)}, bf16[128,384]{1,0:T(8,128)(2,1)S(1)}, u32[]{:S(2)}, u32[]{:S(2)}) collective-permute-start(bf16[128,384]{1,0:T(8,128)(2,1)} %param.9), channel_id=1, source_target_pairs={{0,128},{1,129},{2,130},{3,131},{4,132},{5,133},{6,134},{7,135},{8... | collective-permute-start | bytes 294920 | tf_op jit(solution)/shard_map/ppermute | solution.py:40
  5.8 0.7 collective-permute-start.1
  6.5 2.6 %collective-permute-start = (bf16[128,384]{1,0:T(8,128)(2,1)}, bf16[128,384]{1,0:T(8,128)(2,1)S(1)}, u32[]{:S(2)}, u32[]{:S(2)}) collective-permute-start(bf16[128,384]{1,0:T(8,128)(2,1)} %param.9), channel_id=1, source_target_pairs={{0,192},{1,193},{2,194},{3,195},{4,196},{5,197},{6,198},{7,199},{8... | collective-permute-start | bytes 294920 | tf_op jit(solution)/shard_map/ppermute | solution.py:40
  9.0 1.3 %collective-permute-start.3 = (bf16[128,384]{1,0:T(8,128)(2,1)S(1)}, bf16[128,384]{1,0:T(8,128)(2,1)}, u32[]{:S(2)}, u32[]{:S(2)}) collective-permute-start(bf16[128,384]{1,0:T(8,128)(2,1)S(1)} %multiply_convert_fusion), channel_id=1, source_target_pairs={{0,0},{1,1},{2,2},{3,3},{4,36},{5,37},{6,38},{7,39},{8,72},{9,73},... | collective-permute-start | bytes 294920 | tf_op jit(solution)/shard_map/ppermute | solution.py:40
  10.3 1.5 %collective-permute-done.1 = bf16[128,384]{1,0:T(8,128)(2,1)S(1)} collective-permute-done((bf16[128,384]{1,0:T(8,128)(2,1)}, bf16[128,384]{1,0:T(8,128)(2,1)S(1)}, u32[]{:S(2)}, u32[]{:S(2)}) %collective-permute-start.1) | collective-permute-done | bytes 98336 | tf_op jit(solution)/shard_map/ppermute | solution.py:40
  11.8 1.0 pad_maximum_fusion.near
  12.8 7.4 %collective-permute-start.4 = (bf16[4,128,384]{2,1,0:T(8,128)(2,1)S(1)}, bf16[4,128,384]{2,1,0:T(8,128)(2,1)}, u32[]{:S(2)}, u32[]{:S(2)}) collective-permute-start(bf16[4,128,384]{2,1,0:T(8,128)(2,1)S(1)} %pad_maximum_fusion.near), channel_id=1, source_target_pairs={{0,32},{1,33},{2,34},{3,35},{4,36},{5,37},{6,38},{7,39},{8,40},{9,... | collective-permute-start | bytes 1179656 | tf_op jit(solution)/shard_map/ppermute | solution.py:40
  20.4 1.6 %collective-permute-start.7 = (bf16[128,384]{1,0:T(8,128)(2,1)}, bf16[128,384]{1,0:T(8,128)(2,1)}, u32[]{:S(2)}, u32[]{:S(2)}) collective-permute-start(bf16[128,384]{1,0:T(8,128)(2,1)} %collective-permute-done.3.refs_0_), channel_id=1, source_target_pairs={{0,1},{1,2},{2,3},{3,0},{4,5},{5,6},{6,7},{7,4},{8,9},{9,10},{10,1... | collective-permute-start | bytes 294920 | tf_op jit(solution)/shard_map/ppermute | solution.py:40
  22.0 1.2 %collective-permute-start.6 = (bf16[128,384]{1,0:T(8,128)(2,1)}, bf16[128,384]{1,0:T(8,128)(2,1)}, u32[]{:S(2)}, u32[]{:S(2)}) collective-permute-start(bf16[128,384]{1,0:T(8,128)(2,1)} %collective-permute-done.3.refs_0_), channel_id=1, source_target_pairs={{0,2},{1,3},{2,0},{3,1},{4,6},{5,7},{6,4},{7,5},{8,10},{9,11},{10,... | collective-permute-start | bytes 294920 | tf_op jit(solution)/shard_map/ppermute | solution.py:40
  23.3 2.0 %collective-permute-start.5 = (bf16[128,384]{1,0:T(8,128)(2,1)}, bf16[128,384]{1,0:T(8,128)(2,1)}, u32[]{:S(2)}, u32[]{:S(2)}) collective-permute-start(bf16[128,384]{1,0:T(8,128)(2,1)} %collective-permute-done.3.refs_0_), channel_id=1, source_target_pairs={{0,3},{1,0},{2,1},{3,2},{4,7},{5,4},{6,5},{7,6},{8,11},{9,8},{10,9... | collective-permute-start | bytes 294920 | tf_op jit(solution)/shard_map/ppermute | solution.py:40
  25.3 5.0 %shard_map.76 = (bf16[8,4,128,384]{3,2,1,0:T(8,128)(2,1)}, bf16[1536,384]{1,0:T(8,128)(2,1)S(1)}, bf16[8,128,384]{2,1,0:T(8,128)(2,1)S(1)}) custom-call(s32[16]{0:T(128)S(1)} %stack.87.place, f32[12,3]{1,0:T(8,128)S(1)} %copy.11.scales, bf16[4,128,384]{2,1,0:T(8,128)(2,1)S(1)} %pad_maximum_fusion.near, bf16[4,128,384]{2,1,0:T(8,128)(2,1)} %collective-permute-done.4.far, ...), custom_call_target="tpu_custom_call" | custom-call | flops 1207959552 | bytes 3145728 | tf_op jit(solution)/shard_map/pallas_call | solution.py:89
  30.3 13.1 %shard_map.77 = bf16[128,1536]{1,0:T(8,128)(2,1)} custom-call(s32[1]{0:T(128)} %bitcast.x, bf16[128,384]{1,0:T(8,128)(2,1)} %collective-permute-done.3.refs_0_, bf16[128,384]{1,0:T(8,128)(2,1)} %collective-permute-done.5.refs_1_, bf16[128,384]{1,0:T(8,128)(2,1)} %collective-permute-done.6.refs_2_, bf16[128,384]{1,0:T(8,128)(2,1)} %collective-permute-done.7.refs_3_), custom_call_target="tpu_custom_call" | custom-call | bytes 786432 | tf_op jit(solution)/shard_map/pallas_call | solution.py:170
  43.5 4.9 %collective-permute-start.8 = (bf16[128,1536]{1,0:T(8,128)(2,1)}, bf16[128,1536]{1,0:T(8,128)(2,1)}, u32[]{:S(2)}, u32[]{:S(2)}) collective-permute-start(bf16[128,1536]{1,0:T(8,128)(2,1)} %shard_map.77), channel_id=1, source_target_pairs={{0,28},{1,29},{2,30},{3,31},{4,0},{5,1},{6,2},{7,3},{8,4},{9,5},{1... | collective-permute-start | bytes 1179656 | tf_op jit(solution)/shard_map/ppermute | solution.py:40
  48.4 6.0 %all-to-all-start = ((bf16[32,128,384]{2,1,0:T(8,128)(2,1)}), bf16[32,128,384]{2,1,0:T(8,128)(2,1)}, u32[]{:S(2)}, u32[]{:S(2)}) async-start(bf16[32,128,384]{2,1,0:T(8,128)(2,1)} %bitcast.117), calls=%async_computation | async-start | bytes 6291456 | tf_op jit(solution)/shard_map/all_to_all | solution.py:206
  54.6 0.4 fusion.1
  55.0 2.4 %collective-permute-done.9 = bf16[128,1536]{1,0:T(8,128)(2,1)S(1)} collective-permute-done((bf16[128,1536]{1,0:T(8,128)(2,1)}, bf16[128,1536]{1,0:T(8,128)(2,1)S(1)}, u32[]{:S(2)}, u32[]{:S(2)}) %collective-permute-start.9) | collective-permute-done | bytes 393248 | tf_op jit(solution)/shard_map/ppermute | solution.py:40
  57.5 3.2 %collective-permute-start.10 = (bf16[128,1536]{1,0:T(8,128)(2,1)}, bf16[128,1536]{1,0:T(8,128)(2,1)S(1)}, u32[]{:S(2)}, u32[]{:S(2)}) collective-permute-start(bf16[128,1536]{1,0:T(8,128)(2,1)} %collective-permute-done.8), channel_id=1, source_target_pairs={{0,28},{1,29},{2,30},{3,31},{4,0},{5,1},{6,2},{7,3},{8,4},{9,5},{1... | collective-permute-start | bytes 1179656 | tf_op jit(solution)/shard_map/ppermute | solution.py:40
  60.7 1.4 %fusion.3 = bf16[8,128,384]{2,1,0:T(8,128)(2,1)S(1)} fusion(bf16[8,128,384]{2,1,0:T(8,128)(2,1)S(1)} %fusion.1, s32[]{:T(128)S(6)} %select_n.387, bf16[128,1536]{1,0:T(8,128)(2,1)} %collective-permute-done.8, bf16[1536,384]{1,0:T(8,128)(2,1)S(1)} %get-tuple-element.35), kind=kOutput, calls=%fused_computation.12 | convolution fusion | flops 151044096 | bytes 1671172 | tf_op jit(solution)/shard_map/dot_general | solution.py:56
  62.1 0.4 fusion.5
  62.5 6.3 %collective-permute-done.11 = bf16[128,1536]{1,0:T(8,128)(2,1)S(1)} collective-permute-done((bf16[128,1536]{1,0:T(8,128)(2,1)S(1)}, bf16[128,1536]{1,0:T(8,128)(2,1)S(1)}, u32[]{:S(2)}, u32[]{:S(2)}) %collective-permute-start.11) | collective-permute-done | bytes 393248 | tf_op jit(solution)/shard_map/ppermute | solution.py:40
  68.8 3.2 %collective-permute-start.12 = (bf16[128,1536]{1,0:T(8,128)(2,1)S(1)}, bf16[128,1536]{1,0:T(8,128)(2,1)S(1)}, u32[]{:S(2)}, u32[]{:S(2)}) collective-permute-start(bf16[128,1536]{1,0:T(8,128)(2,1)S(1)} %collective-permute-done.10), channel_id=1, source_target_pairs={{0,28},{1,29},{2,30},{3,31},{4,0},{5,1},{6,2},{7,3},{8,4},{9,5},{1... | collective-permute-start | bytes 1179656 | tf_op jit(solution)/shard_map/ppermute | solution.py:40
  72.0 0.4 fusion.7
  72.4 0.4 fusion.9
  72.8 6.5 %collective-permute-done.13 = bf16[128,1536]{1,0:T(8,128)(2,1)S(1)} collective-permute-done((bf16[128,1536]{1,0:T(8,128)(2,1)S(1)}, bf16[128,1536]{1,0:T(8,128)(2,1)S(1)}, u32[]{:S(2)}, u32[]{:S(2)}) %collective-permute-start.13) | collective-permute-done | bytes 393248 | tf_op jit(solution)/shard_map/ppermute | solution.py:40
  79.4 3.3 %collective-permute-start.14 = (bf16[64,1536]{1,0:T(8,128)(2,1)S(1)}, bf16[64,1536]{1,0:T(8,128)(2,1)S(1)}, u32[]{:S(2)}, u32[]{:S(2)}) collective-permute-start(bf16[64,1536]{1,0:T(8,128)(2,1)S(1)} %slice.95), channel_id=1, source_target_pairs={{0,28},{1,29},{2,30},{3,31},{4,0},{5,1},{6,2},{7,3},{8,4},{9,5},{1... | collective-permute-start | bytes 589832 | tf_op jit(solution)/shard_map/ppermute | solution.py:40
  82.7 1.0 constant_dynamic-update-slice_fusion.7
  83.9 0.4 fusion.11
  84.3 1.8 %fusion.27 = f32[1536,384]{1,0:T(8,128)S(1)} fusion(bf16[896,1536]{1,0:T(8,128)(2,1)S(1)} %constant_dynamic-update-slice_fusion.2, bf16[896,384]{1,0:T(8,128)(2,1)S(1)} %bitcast_dynamic-update-slice_fusion), kind=kOutput, calls=%fused_computation.62 | convolution fusion | flops 1056964608 | bytes 5799936 | tf_op jit(solution)/shard_map/dot_general | solution.py:240
  86.1 0.4 fusion.13
  86.6 0.4 fusion.15
  87.1 0.5 fusion.23
  87.6 1.6 %add_multiply_fusion = f32[1536,384]{1,0:T(8,128)} fusion(f32[1536,384]{1,0:T(8,128)S(1)} %fusion.27, f32[1536,384]{1,0:T(8,128)S(1)} %fusion.23), kind=kLoop, calls=%fused_computation | loop fusion | flops 1179648 | bytes 7077888 | tf_op jit(solution)/shard_map/mul | solution.py:252
  89.4 3.1 %all-to-all-done = bf16[32,128,384]{2,1,0:T(8,128)(2,1)} async-done(((bf16[32,128,384]{2,1,0:T(8,128)(2,1)}), bf16[32,128,384]{2,1,0:T(8,128)(2,1)}, u32[]{:S(2)}, u32[]{:S(2)}) %all-to-all-start) | async-done | bytes 3145760 | tf_op jit(solution)/shard_map/all_to_all | solution.py:206
  92.5 2.3 %shard_map.78 = (bf16[2,128,384]{2,1,0:T(8,128)(2,1)S(1)}, bf16[2,128,384]{2,1,0:T(8,128)(2,1)S(1)}, bf16[128,384]{1,0:T(8,128)(2,1)S(1)}, f32[3,128,384]{2,1,0:T(8,128)S(1)}) custom-call(s32[1]{0:T(128)} %bitcast.34.z, bf16[8,4,128,384]{3,2,1,0:T(8,128)(2,1)} %bitcast.36.parts), custom_call_target="tpu_custom_call" | custom-call | flops 1572864 | bytes 4718592 | tf_op jit(solution)/shard_map/pallas_call | solution.py:137
  94.9 3.2 %collective-permute-start.21 = (bf16[2,128,384]{2,1,0:T(8,128)(2,1)S(1)}, bf16[2,128,384]{2,1,0:T(8,128)(2,1)S(1)}, u32[]{:S(2)}, u32[]{:S(2)}) collective-permute-start(bf16[2,128,384]{2,1,0:T(8,128)(2,1)S(1)} %get-tuple-element.39), channel_id=1, source_target_pairs={{0,28},{1,29},{2,30},{3,31},{4,0},{5,1},{6,2},{7,3},{8,4},{9,5},{1... | collective-permute-start | bytes 589832 | tf_op jit(solution)/shard_map/ppermute | solution.py:40
  98.1 0.3 collective-permute-start.17
  98.5 3.0 %collective-permute-start.19 = (bf16[128,384]{1,0:T(8,128)(2,1)S(1)}, bf16[128,384]{1,0:T(8,128)(2,1)S(1)}, u32[]{:S(2)}, u32[]{:S(2)}) collective-permute-start(bf16[128,384]{1,0:T(8,128)(2,1)S(1)} %get-tuple-element.56), channel_id=1, source_target_pairs={{0,192},{1,193},{2,194},{3,195},{4,196},{5,197},{6,198},{7,199},{8... | collective-permute-start | bytes 294920 | tf_op jit(solution)/shard_map/ppermute | solution.py:40
  101.4 1.1 collective-permute-start.18
  102.5 0.9 collective-permute-done.20
  103.4 5.7 %collective-permute-start.22 = (bf16[128,384]{1,0:T(8,128)(2,1)S(1)}, bf16[128,384]{1,0:T(8,128)(2,1)S(1)}, u32[]{:S(2)}, u32[]{:S(2)}) collective-permute-start(bf16[128,384]{1,0:T(8,128)(2,1)S(1)} %get-tuple-element.40), channel_id=1, source_target_pairs={{0,16},{1,17},{2,18},{3,19},{4,20},{5,21},{6,22},{7,23},{8,24},{9,... | collective-permute-start | bytes 294920 | tf_op jit(solution)/shard_map/ppermute | solution.py:40
  109.3 4.1 %collective-permute-start.24 = (bf16[128,384]{1,0:T(8,128)(2,1)S(1)}, bf16[128,384]{1,0:T(8,128)(2,1)S(1)}, u32[]{:S(2)}, u32[]{:S(2)}) collective-permute-start(bf16[128,384]{1,0:T(8,128)(2,1)S(1)} %get-tuple-element.54), channel_id=1, source_target_pairs={{0,24},{1,25},{2,26},{3,27},{4,28},{5,29},{6,30},{7,31},{8,0},{9,1... | collective-permute-start | bytes 294920 | tf_op jit(solution)/shard_map/ppermute | solution.py:40
  113.4 0.7 fusion.17
  114.1 1.6 %collective-permute-done.22 = bf16[128,384]{1,0:T(8,128)(2,1)S(1)} collective-permute-done((bf16[128,384]{1,0:T(8,128)(2,1)S(1)}, bf16[128,384]{1,0:T(8,128)(2,1)S(1)}, u32[]{:S(2)}, u32[]{:S(2)}) %collective-permute-start.22) | collective-permute-done | bytes 98336 | tf_op jit(solution)/shard_map/ppermute | solution.py:40
  115.8 2.7 %collective-permute-done.23 = bf16[128,384]{1,0:T(8,128)(2,1)S(1)} collective-permute-done((bf16[128,384]{1,0:T(8,128)(2,1)S(1)}, bf16[128,384]{1,0:T(8,128)(2,1)S(1)}, u32[]{:S(2)}, u32[]{:S(2)}) %collective-permute-start.23) | collective-permute-done | bytes 98336 | tf_op jit(solution)/shard_map/ppermute | solution.py:40
  118.5 0.7 fusion.20
  (59 shorter events, 1.3 us)
Async XLA Ops:
  0.6 19.6 %copy-start.4 = (f32[12,3]{0,1:T(4,128)S(1)}, f32[12,3]{0,1:T(4,128)}, u32[]{:S(2)}) copy-start(f32[12,3]{0,1:T(4,128)} %param.8) | copy-start | bytes 436
  0.6 24.7 %copy-start = (bf16[1536,384]{1,0:T(8,128)(2,1)S(1)}, bf16[1536,384]{1,0:T(8,128)(2,1)}, u32[]{:S(2)}) copy-start(bf16[1536,384]{1,0:T(8,128)(2,1)} %values.1) | copy-start | bytes 3538948
  2.5 7.8 %collective-permute-start.2 = (bf16[128,384]{1,0:T(8,128)(2,1)}, bf16[128,384]{1,0:T(8,128)(2,1)S(1)}, u32[]{:S(2)}, u32[]{:S(2)}) collective-permute-start(bf16[128,384]{1,0:T(8,128)(2,1)} %param.9), channel_id=1, source_target_pairs={{0,128},{1,129},{2,130},{3,131},{4,132},{5,133},{6,134},{7,135},{8... | collective-permute-start | bytes 294920 | tf_op jit(solution)/shard_map/ppermute | solution.py:40
  5.8 6.0 %collective-permute-start.1 = (bf16[128,384]{1,0:T(8,128)(2,1)}, bf16[128,384]{1,0:T(8,128)(2,1)S(1)}, u32[]{:S(2)}, u32[]{:S(2)}) collective-permute-start(bf16[128,384]{1,0:T(8,128)(2,1)} %param.9), channel_id=1, source_target_pairs={{0,64},{1,65},{2,66},{3,67},{4,68},{5,69},{6,70},{7,71},{8,72},{9,... | collective-permute-start | bytes 294920 | tf_op jit(solution)/shard_map/ppermute | solution.py:40
  6.5 5.4 %collective-permute-start = (bf16[128,384]{1,0:T(8,128)(2,1)}, bf16[128,384]{1,0:T(8,128)(2,1)S(1)}, u32[]{:S(2)}, u32[]{:S(2)}) collective-permute-start(bf16[128,384]{1,0:T(8,128)(2,1)} %param.9), channel_id=1, source_target_pairs={{0,192},{1,193},{2,194},{3,195},{4,196},{5,197},{6,198},{7,199},{8... | collective-permute-start | bytes 294920 | tf_op jit(solution)/shard_map/ppermute | solution.py:40
  9.0 3.8 %collective-permute-start.3 = (bf16[128,384]{1,0:T(8,128)(2,1)S(1)}, bf16[128,384]{1,0:T(8,128)(2,1)}, u32[]{:S(2)}, u32[]{:S(2)}) collective-permute-start(bf16[128,384]{1,0:T(8,128)(2,1)S(1)} %multiply_convert_fusion), channel_id=1, source_target_pairs={{0,0},{1,1},{2,2},{3,3},{4,36},{5,37},{6,38},{7,39},{8,72},{9,73},... | collective-permute-start | bytes 294920 | tf_op jit(solution)/shard_map/ppermute | solution.py:40
  12.8 12.5 %collective-permute-start.4 = (bf16[4,128,384]{2,1,0:T(8,128)(2,1)S(1)}, bf16[4,128,384]{2,1,0:T(8,128)(2,1)}, u32[]{:S(2)}, u32[]{:S(2)}) collective-permute-start(bf16[4,128,384]{2,1,0:T(8,128)(2,1)S(1)} %pad_maximum_fusion.near), channel_id=1, source_target_pairs={{0,32},{1,33},{2,34},{3,35},{4,36},{5,37},{6,38},{7,39},{8,40},{9,... | collective-permute-start | bytes 1179656 | tf_op jit(solution)/shard_map/ppermute | solution.py:40
  20.4 9.9 %collective-permute-start.7 = (bf16[128,384]{1,0:T(8,128)(2,1)}, bf16[128,384]{1,0:T(8,128)(2,1)}, u32[]{:S(2)}, u32[]{:S(2)}) collective-permute-start(bf16[128,384]{1,0:T(8,128)(2,1)} %collective-permute-done.3.refs_0_), channel_id=1, source_target_pairs={{0,1},{1,2},{2,3},{3,0},{4,5},{5,6},{6,7},{7,4},{8,9},{9,10},{10,1... | collective-permute-start | bytes 294920 | tf_op jit(solution)/shard_map/ppermute | solution.py:40
  22.0 8.3 %collective-permute-start.6 = (bf16[128,384]{1,0:T(8,128)(2,1)}, bf16[128,384]{1,0:T(8,128)(2,1)}, u32[]{:S(2)}, u32[]{:S(2)}) collective-permute-start(bf16[128,384]{1,0:T(8,128)(2,1)} %collective-permute-done.3.refs_0_), channel_id=1, source_target_pairs={{0,2},{1,3},{2,0},{3,1},{4,6},{5,7},{6,4},{7,5},{8,10},{9,11},{10,... | collective-permute-start | bytes 294920 | tf_op jit(solution)/shard_map/ppermute | solution.py:40
  23.3 7.0 %collective-permute-start.5 = (bf16[128,384]{1,0:T(8,128)(2,1)}, bf16[128,384]{1,0:T(8,128)(2,1)}, u32[]{:S(2)}, u32[]{:S(2)}) collective-permute-start(bf16[128,384]{1,0:T(8,128)(2,1)} %collective-permute-done.3.refs_0_), channel_id=1, source_target_pairs={{0,3},{1,0},{2,1},{3,2},{4,7},{5,4},{6,5},{7,6},{8,11},{9,8},{10,9... | collective-permute-start | bytes 294920 | tf_op jit(solution)/shard_map/ppermute | solution.py:40
  43.4 14.1 %collective-permute-start.9 = (bf16[128,1536]{1,0:T(8,128)(2,1)}, bf16[128,1536]{1,0:T(8,128)(2,1)S(1)}, u32[]{:S(2)}, u32[]{:S(2)}) collective-permute-start(bf16[128,1536]{1,0:T(8,128)(2,1)} %shard_map.77), channel_id=1, source_target_pairs={{0,4},{1,5},{2,6},{3,7},{4,8},{5,9},{6,10},{7,11},{8,12},{9,13},{1... | collective-permute-start | bytes 1179656 | tf_op jit(solution)/shard_map/ppermute | solution.py:40
  43.5 14.0 %collective-permute-start.8 = (bf16[128,1536]{1,0:T(8,128)(2,1)}, bf16[128,1536]{1,0:T(8,128)(2,1)}, u32[]{:S(2)}, u32[]{:S(2)}) collective-permute-start(bf16[128,1536]{1,0:T(8,128)(2,1)} %shard_map.77), channel_id=1, source_target_pairs={{0,28},{1,29},{2,30},{3,31},{4,0},{5,1},{6,2},{7,3},{8,4},{9,5},{1... | collective-permute-start | bytes 1179656 | tf_op jit(solution)/shard_map/ppermute | solution.py:40
  48.4 6.2 %copy-start.1 = (bf16[128,1536]{1,0:T(8,128)(2,1)S(1)}, bf16[128,1536]{1,0:T(8,128)(2,1)}, u32[]{:S(2)}) copy-start(bf16[128,1536]{1,0:T(8,128)(2,1)} %shard_map.77) | copy-start | bytes 1179652
  48.4 44.1 %all-to-all-start = ((bf16[32,128,384]{2,1,0:T(8,128)(2,1)}), bf16[32,128,384]{2,1,0:T(8,128)(2,1)}, u32[]{:S(2)}, u32[]{:S(2)}) async-start(bf16[32,128,384]{2,1,0:T(8,128)(2,1)} %bitcast.117), calls=%async_computation | async-start | bytes 6291456 | tf_op jit(solution)/shard_map/all_to_all | solution.py:206
  57.4 5.0 %copy-start.2 = (bf16[128,1536]{1,0:T(8,128)(2,1)}, bf16[128,1536]{1,0:T(8,128)(2,1)S(1)}, u32[]{:S(2)}) copy-start(bf16[128,1536]{1,0:T(8,128)(2,1)S(1)} %collective-permute-done.9) | copy-start | bytes 1179652
  57.4 11.3 %collective-permute-start.11 = (bf16[128,1536]{1,0:T(8,128)(2,1)S(1)}, bf16[128,1536]{1,0:T(8,128)(2,1)S(1)}, u32[]{:S(2)}, u32[]{:S(2)}) collective-permute-start(bf16[128,1536]{1,0:T(8,128)(2,1)S(1)} %collective-permute-done.9), channel_id=1, source_target_pairs={{0,4},{1,5},{2,6},{3,7},{4,8},{5,9},{6,10},{7,11},{8,12},{9,13},{1... | collective-permute-start | bytes 1179656 | tf_op jit(solution)/shard_map/ppermute | solution.py:40
  57.5 11.3 %collective-permute-start.10 = (bf16[128,1536]{1,0:T(8,128)(2,1)}, bf16[128,1536]{1,0:T(8,128)(2,1)S(1)}, u32[]{:S(2)}, u32[]{:S(2)}) collective-permute-start(bf16[128,1536]{1,0:T(8,128)(2,1)} %collective-permute-done.8), channel_id=1, source_target_pairs={{0,28},{1,29},{2,30},{3,31},{4,0},{5,1},{6,2},{7,3},{8,4},{9,5},{1... | collective-permute-start | bytes 1179656 | tf_op jit(solution)/shard_map/ppermute | solution.py:40
  68.8 10.5 %collective-permute-start.13 = (bf16[128,1536]{1,0:T(8,128)(2,1)S(1)}, bf16[128,1536]{1,0:T(8,128)(2,1)S(1)}, u32[]{:S(2)}, u32[]{:S(2)}) collective-permute-start(bf16[128,1536]{1,0:T(8,128)(2,1)S(1)} %collective-permute-done.11), channel_id=1, source_target_pairs={{0,4},{1,5},{2,6},{3,7},{4,8},{5,9},{6,10},{7,11},{8,12},{9,13},{1... | collective-permute-start | bytes 1179656 | tf_op jit(solution)/shard_map/ppermute | solution.py:40
  68.8 10.6 %collective-permute-start.12 = (bf16[128,1536]{1,0:T(8,128)(2,1)S(1)}, bf16[128,1536]{1,0:T(8,128)(2,1)S(1)}, u32[]{:S(2)}, u32[]{:S(2)}) collective-permute-start(bf16[128,1536]{1,0:T(8,128)(2,1)S(1)} %collective-permute-done.10), channel_id=1, source_target_pairs={{0,28},{1,29},{2,30},{3,31},{4,0},{5,1},{6,2},{7,3},{8,4},{9,5},{1... | collective-permute-start | bytes 1179656 | tf_op jit(solution)/shard_map/ppermute | solution.py:40
  72.4 11.4 %copy-start.3 = (bf16[128,1536]{1,0:T(8,128)(2,1)S(1)}, bf16[128,1536]{1,0:T(8,128)(2,1)}, u32[]{:S(2)}) copy-start(bf16[128,1536]{1,0:T(8,128)(2,1)} %copy-done.2) | copy-start | bytes 1179652
  79.3 7.2 %collective-permute-start.15 = (bf16[64,1536]{1,0:T(8,128)(2,1)S(1)}, bf16[64,1536]{1,0:T(8,128)(2,1)S(1)}, u32[]{:S(2)}, u32[]{:S(2)}) collective-permute-start(bf16[64,1536]{1,0:T(8,128)(2,1)S(1)} %slice.96), channel_id=1, source_target_pairs={{0,4},{1,5},{2,6},{3,7},{4,8},{5,9},{6,10},{7,11},{8,12},{9,13},{1... | collective-permute-start | bytes 589832 | tf_op jit(solution)/shard_map/ppermute | solution.py:40
  79.4 7.1 %collective-permute-start.14 = (bf16[64,1536]{1,0:T(8,128)(2,1)S(1)}, bf16[64,1536]{1,0:T(8,128)(2,1)S(1)}, u32[]{:S(2)}, u32[]{:S(2)}) collective-permute-start(bf16[64,1536]{1,0:T(8,128)(2,1)S(1)} %slice.95), channel_id=1, source_target_pairs={{0,28},{1,29},{2,30},{3,31},{4,0},{5,1},{6,2},{7,3},{8,4},{9,5},{1... | collective-permute-start | bytes 589832 | tf_op jit(solution)/shard_map/ppermute | solution.py:40
  87.0 2.2 %collective-permute-start.16 = (bf16[4,128,384]{2,1,0:T(8,128)(2,1)S(1)}, bf16[4,128,384]{2,1,0:T(8,128)(2,1)S(1)}, u32[]{:S(2)}, u32[]{:S(2)}) collective-permute-start(bf16[4,128,384]{2,1,0:T(8,128)(2,1)S(1)} %slice.98), channel_id=1, source_target_pairs={{0,32},{1,33},{2,34},{3,35},{4,36},{5,37},{6,38},{7,39},{8,40},{9,... | collective-permute-start | bytes 1179656 | tf_op jit(solution)/shard_map/ppermute | solution.py:40
  94.8 8.6 %collective-permute-start.20 = (bf16[2,128,384]{2,1,0:T(8,128)(2,1)S(1)}, bf16[2,128,384]{2,1,0:T(8,128)(2,1)S(1)}, u32[]{:S(2)}, u32[]{:S(2)}) collective-permute-start(bf16[2,128,384]{2,1,0:T(8,128)(2,1)S(1)} %get-tuple-element.38), channel_id=1, source_target_pairs={{0,4},{1,5},{2,6},{3,7},{4,8},{5,9},{6,10},{7,11},{8,12},{9,13},{1... | collective-permute-start | bytes 589832 | tf_op jit(solution)/shard_map/ppermute | solution.py:40
  94.9 14.3 %collective-permute-start.21 = (bf16[2,128,384]{2,1,0:T(8,128)(2,1)S(1)}, bf16[2,128,384]{2,1,0:T(8,128)(2,1)S(1)}, u32[]{:S(2)}, u32[]{:S(2)}) collective-permute-start(bf16[2,128,384]{2,1,0:T(8,128)(2,1)S(1)} %get-tuple-element.39), channel_id=1, source_target_pairs={{0,28},{1,29},{2,30},{3,31},{4,0},{5,1},{6,2},{7,3},{8,4},{9,5},{1... | collective-permute-start | bytes 589832 | tf_op jit(solution)/shard_map/ppermute | solution.py:40
  98.1 11.2 %collective-permute-start.17 = (bf16[128,384]{1,0:T(8,128)(2,1)S(1)}, bf16[128,384]{1,0:T(8,128)(2,1)S(1)}, u32[]{:S(2)}, u32[]{:S(2)}) collective-permute-start(bf16[128,384]{1,0:T(8,128)(2,1)S(1)} %get-tuple-element.55), channel_id=1, source_target_pairs={{0,64},{1,65},{2,66},{3,67},{4,68},{5,69},{6,70},{7,71},{8,72},{9,... | collective-permute-start | bytes 294920 | tf_op jit(solution)/shard_map/ppermute | solution.py:40
  98.5 15.0 %collective-permute-start.19 = (bf16[128,384]{1,0:T(8,128)(2,1)S(1)}, bf16[128,384]{1,0:T(8,128)(2,1)S(1)}, u32[]{:S(2)}, u32[]{:S(2)}) collective-permute-start(bf16[128,384]{1,0:T(8,128)(2,1)S(1)} %get-tuple-element.56), channel_id=1, source_target_pairs={{0,192},{1,193},{2,194},{3,195},{4,196},{5,197},{6,198},{7,199},{8... | collective-permute-start | bytes 294920 | tf_op jit(solution)/shard_map/ppermute | solution.py:40
  101.4 12.0 %collective-permute-start.18 = (bf16[128,384]{1,0:T(8,128)(2,1)S(1)}, bf16[128,384]{1,0:T(8,128)(2,1)S(1)}, u32[]{:S(2)}, u32[]{:S(2)}) collective-permute-start(bf16[128,384]{1,0:T(8,128)(2,1)S(1)} %get-tuple-element.57), channel_id=1, source_target_pairs={{0,128},{1,129},{2,130},{3,131},{4,132},{5,133},{6,134},{7,135},{8... | collective-permute-start | bytes 294920 | tf_op jit(solution)/shard_map/ppermute | solution.py:40
  103.4 12.3 %collective-permute-start.22 = (bf16[128,384]{1,0:T(8,128)(2,1)S(1)}, bf16[128,384]{1,0:T(8,128)(2,1)S(1)}, u32[]{:S(2)}, u32[]{:S(2)}) collective-permute-start(bf16[128,384]{1,0:T(8,128)(2,1)S(1)} %get-tuple-element.40), channel_id=1, source_target_pairs={{0,16},{1,17},{2,18},{3,19},{4,20},{5,21},{6,22},{7,23},{8,24},{9,... | collective-permute-start | bytes 294920 | tf_op jit(solution)/shard_map/ppermute | solution.py:40
  109.2 9.3 %collective-permute-start.23 = (bf16[128,384]{1,0:T(8,128)(2,1)S(1)}, bf16[128,384]{1,0:T(8,128)(2,1)S(1)}, u32[]{:S(2)}, u32[]{:S(2)}) collective-permute-start(bf16[128,384]{1,0:T(8,128)(2,1)S(1)} %get-tuple-element.53), channel_id=1, source_target_pairs={{0,8},{1,9},{2,10},{3,11},{4,12},{5,13},{6,14},{7,15},{8,16},{9,17... | collective-permute-start | bytes 294920 | tf_op jit(solution)/shard_map/ppermute | solution.py:40
  109.3 9.2 %collective-permute-start.24 = (bf16[128,384]{1,0:T(8,128)(2,1)S(1)}, bf16[128,384]{1,0:T(8,128)(2,1)S(1)}, u32[]{:S(2)}, u32[]{:S(2)}) collective-permute-start(bf16[128,384]{1,0:T(8,128)(2,1)S(1)} %get-tuple-element.54), channel_id=1, source_target_pairs={{0,24},{1,25},{2,26},{3,27},{4,28},{5,29},{6,30},{7,31},{8,0},{9,1... | collective-permute-start | bytes 294920 | tf_op jit(solution)/shard_map/ppermute | solution.py:40
